TPU v7x, 256 devices: a whole 4x4x8 slice. The times are simulated.
256 devices in a mesh: dp: 16 (over z_hi, y), tensor: 16 (over z_lo, x, core).
Axes of the slice: x: 4, y: 4, z: 8 (z_hi: 4, z_lo: 2; z = z_hi * 2 + z_lo), core: 2. Of those that a mesh axis runs over, the one named last changes fastest.
Arguments:
- grad: bfloat16 [16, 16, 524288], P('dp', 'tensor'), may hold values from -18 to 18
- worker_err: bfloat16 [16, 16, 524288], P('dp', 'tensor'), may hold values from -3 to 3
- momentum: float32 [16, 524288], P('tensor'), may hold values from -6 to 6
- variance: float32 [16, 524288], P('tensor'), may hold values from 6e-06 to 80, as said below
- params: bfloat16 [16, 524288], P('tensor'), may hold values from -5 to 5
- server_err: float32 [16, 524288], P('tensor', 'dp'), may hold values from -3 to 3
- offsets: int32 [4], replicated, may hold values from 0 to 524160, as said below
- step_count: int32 [1], replicated, may hold values from 1 to 2000
Outputs:
- momentum_new: float32 [16, 524288], P('tensor')
- param_step: float32 [16, 524288], P('tensor')
Inputs may be any that keep to these rules, and one draw needn't show every extreme that they name: offsets[0] is 0; the entries strictly increase and are multiples of 128; the last entry is 524160. `variance`: positive entries.
All inputs are finite; a program needn't handle non-finite values. Where the computation divides by a largest or mean magnitude, that divisor is 1e-20 or more.
Results may differ from a plain program's by a relative error of at most 0.013.
Values may be sent and summed in bfloat16 or wider, within the bound.
No kernel may reach another device: no remote copies, remote signals or barrier semaphores. Data moves between devices by JAX's collectives and lax.ppermute only.
A program may use at most 64 MiB of HBM per device.

v0:
```python
import jax
import jax.numpy as jnp
from jax import lax
from jax.sharding import PartitionSpec as P

QB = 128


BETA_ONE = 0.9
BETA_TWO = 0.999
ADAM_EPS = 1e-08
DECAY = 0.1
CLIP_RMS = 2.0


def encode(values):
    scales = (jnp.max(jnp.abs(values), axis=-1) + 1e-06).astype(jnp.bfloat16)
    levels = (values / scales.astype(jnp.float32)[..., None]).astype(jnp.bfloat16)
    return (levels, scales)


def decode(levels, scales):
    return levels.astype(jnp.float32) * scales.astype(jnp.float32)[..., None]


def membership(offsets, total_blocks, count):
    starts = offsets // QB
    ends = jnp.concatenate([starts[1:], jnp.full((1,), total_blocks, jnp.int32)])
    index = jnp.arange(count, dtype=jnp.int32)
    member = ((index[None, :] >= starts[:, None]) & (index[None, :] < ends[:, None])).astype(
        jnp.float32
    )
    return (member, (ends - starts).astype(jnp.float32))


def body(grad, worker_err, momentum, variance, params, server_err, offsets, step_count):
    groups = lax.axis_size("dp")
    shards = lax.axis_size("tensor")
    bucket_len = momentum.shape[1]
    total_blocks = bucket_len // QB
    share_blocks = total_blocks // groups
    worker_in = (
        BETA_ONE * momentum[0]
        + (1.0 - BETA_ONE) * grad[0, 0].astype(jnp.float32)
        + worker_err[0, 0].astype(jnp.float32)
    )
    levels, scales = encode(worker_in.reshape(groups, share_blocks, QB))
    averaged = (
        jnp.sum(
            decode(
                lax.all_to_all(levels, "dp", split_axis=0, concat_axis=0, tiled=True),
                lax.all_to_all(scales, "dp", split_axis=0, concat_axis=0, tiled=True),
            ),
            axis=0,
        )
        / groups
    )
    server_in = averaged + server_err[0].reshape(share_blocks, QB)
    server_levels, server_scales = encode(server_in)
    steps = step_count[0].astype(jnp.float32)
    first = 1.0 - jnp.power(jnp.float32(BETA_ONE), steps)
    second = 1.0 - jnp.power(jnp.float32(BETA_TWO), steps)
    all_levels, all_scales = (
        lax.all_gather(server_levels, "dp", axis=0, tiled=True),
        lax.all_gather(server_scales, "dp", axis=0, tiled=True),
    )
    momentum_new = decode(all_levels, all_scales).reshape(bucket_len)
    direction = momentum_new / first / (jnp.sqrt(variance[0] / second) + ADAM_EPS)
    member, counts = membership(offsets, total_blocks, total_blocks)
    squares = jnp.sum((direction * direction).reshape(total_blocks, QB), axis=1)
    partial_value = jnp.dot(member, squares, precision=lax.Precision.HIGHEST)
    totals = lax.psum(partial_value, "tensor")
    root_mean = jnp.sqrt(totals / (counts * QB * shards) + 1e-06)
    factor = jnp.maximum(1.0, root_mean / CLIP_RMS)
    per_block = jnp.dot(factor, member, precision=lax.Precision.HIGHEST)
    shaped = direction.reshape(total_blocks, QB) / per_block[:, None]
    param_step = shaped.reshape(bucket_len) + DECAY * params[0].astype(jnp.float32)
    return (momentum_new[None, :], param_step[None, :])


def solution(mesh):
    placed = (
        P("dp", "tensor", None),
        P("dp", "tensor", None),
        P("tensor", None),
        P("tensor", None),
        P("tensor", None),
        P("tensor", "dp"),
        P(),
        P(),
    )
    return jax.shard_map(
        body,
        mesh=mesh,
        in_specs=placed,
        out_specs=(P("tensor", None), P("tensor", None)),
        check_vma=False,
    )
```

profile of v0, /device:TPU:1, one launch (start us, length us, event | category | flops | bytes accessed | tf_op | source)
XLA Modules:
  0.0 169.8 jit_solution(12595754985624767760)
XLA Ops:
  7.2 3.9 %broadcast_multiply_fusion = f32[1,524288]{1,0:T(1,128)S(1)} fusion(f32[1,524288]{1,0:T(1,128)} %param.10), kind=kLoop, calls=%fused_computation.11 | loop fusion | flops 524288 | bytes 4194304 | tf_op jit(solution)/shard_map/mul | solution.py:43
  11.1 2.9 %convert_multiply_fusion.1 = f32[1,1,524288]{2,1,0:T(1,128)S(1)} fusion(bf16[1,1,524288]{2,1,0:T(2,128)(2,1)S(1)} %copy-done.4), kind=kLoop, calls=%fused_computation.9 | loop fusion | flops 1048576 | bytes 3145728 | tf_op jit(solution)/shard_map/mul | solution.py:44
  14.1 2.2 %convert_element_type.113 = f32[1,1,524288]{2,1,0:T(1,128)S(1)} convert(bf16[1,1,524288]{2,1,0:T(2,128)(2,1)S(1)} %copy-done.5) | non-fusion elementwise | flops 524288 | bytes 3145728 | tf_op jit(solution)/shard_map/convert_element_type | solution.py:45
  16.4 0.6 abs_reduce_fusion
  17.0 0.7 copy-done.1
  17.7 0.5 broadcast.103
  18.2 0.6 reduce
  18.7 0.6 reshape.101
  19.3 11.7 %all-to-all-start.1 = ((bf16[16,2,128]{2,1,0:T(2,128)(2,1)}), bf16[16,2,128]{2,1,0:T(2,128)(2,1)S(1)}, u32[]{:S(2)}, u32[]{:S(2)}) async-start(bf16[16,2,128]{2,1,0:T(2,128)(2,1)} %reshape.101), calls=%async_computation.1 | async-start | bytes 16384 | tf_op jit(solution)/shard_map/all_to_all | solution.py:52
  31.1 3.3 %divide_convert_fusion = bf16[16,256,128]{2,1,0:T(8,128)(2,1)} fusion(f32[16,256]{1,0:T(8,128)S(1)} %get-tuple-element.7, f32[16,256,128]{2,1,0:T(8,128)} %bitcast.30, f32[16,256,128]{2,1,0:T(8,128)S(1)} %bitcast.26, f32[16,256,128]{2,1,0:T(8,128)} %bitcast.28), kind=kLoop, calls=%fused_computation.6 | loop fusion | flops 2097152 | bytes 7356416 | tf_op jit(solution)/shard_map/convert_element_type | solution.py:18
  34.5 5.5 %all-to-all-done.1 = bf16[16,2,128]{2,1,0:T(2,128)(2,1)S(1)} async-done(((bf16[16,2,128]{2,1,0:T(2,128)(2,1)}), bf16[16,2,128]{2,1,0:T(2,128)(2,1)S(1)}, u32[]{:S(2)}, u32[]{:S(2)}) %all-to-all-start.1) | async-done | bytes 8224 | tf_op jit(solution)/shard_map/all_to_all | solution.py:52
  39.9 3.7 %all-to-all-start = ((bf16[16,256,128]{2,1,0:T(8,128)(2,1)}), bf16[16,256,128]{2,1,0:T(8,128)(2,1)S(1)}, u32[]{:S(2)}, u32[]{:S(2)}) async-start(bf16[16,256,128]{2,1,0:T(8,128)(2,1)} %divide_convert_fusion), calls=%async_computation | async-start | bytes 2097152 | tf_op jit(solution)/shard_map/all_to_all | solution.py:51
  44.5 23.6 %all-to-all-done = bf16[16,256,128]{2,1,0:T(8,128)(2,1)S(1)} async-done(((bf16[16,256,128]{2,1,0:T(8,128)(2,1)}), bf16[16,256,128]{2,1,0:T(8,128)(2,1)S(1)}, u32[]{:S(2)}, u32[]{:S(2)}) %all-to-all-start) | async-done | bytes 1048608 | tf_op jit(solution)/shard_map/all_to_all | solution.py:51
  68.0 0.7 multiply_reduce_fusion.1
  68.9 0.7 divide_convert_fusion.1
  69.6 6.5 %add_multiply_fusion = f32[1,524288]{1,0:T(1,128)S(1)} fusion(f32[1,524288]{1,0:T(1,128)} %param.11, f32[]{:T(128)} %bitcast.8, f32[]{:T(128)} %bitcast.7), kind=kLoop, calls=%fused_computation.3 | loop fusion | flops 1572864 | bytes 4194312 | tf_op jit(solution)/shard_map/multiply.12
  76.4 36.1 %all-gather = bf16[16,1,256]{2,1,0:T(2,128)(2,1)S(1)} all-gather(bf16[1,1,256]{2,1,0:T(2,128)(2,1)S(1)} %reshape.94), channel_id=1, replica_groups=mesh['dp'=16,'tensor'=16] {'dp'}, dimensions={0}, use_global_device_ids=true | all-gather | bytes 8704 | tf_op jit(solution)/shard_map/all_gather | solution.py:65
  112.5 11.0 %all-gather.3.cloned.1.call-done = bf16[4096,128]{1,0:T(8,128)(2,1)} async-done(((bf16[256,128]{1,0:T(8,128)(2,1)}), bf16[4096,128]{1,0:T(8,128)(2,1)}) %all-gather.3.cloned.1.call-update) | async-done | bytes 1048592 | tf_op jit(solution)/shard_map/all_gather | solution.py:64
  123.5 2.4 %multiply_reduce_fusion = f32[4096]{0:T(1024)S(1)} fusion(f32[4096,128]{1,0:T(8,128)S(1)} %bitcast.23, f32[4096]{0:T(1024)S(1)} %bitcast.35, bf16[4096,128]{1,0:T(8,128)(2,1)} %all-gather.3.cloned.1.call-done), kind=kLoop, calls=%fused_computation.2 | loop fusion | flops 2617344 | bytes 3178496 | tf_op jit(solution)/shard_map/reduce_sum | solution.py:70
  125.9 0.3 convolution_bitcast_fusion
  126.2 28.7 %psum.7 = f32[4]{0:T(128)S(1)} all-reduce(f32[4]{0:T(128)S(1)} %convolution_bitcast_fusion), channel_id=1, replica_groups=mesh['dp'=16,'tensor'=16] {'tensor'}, use_global_device_ids=true, to_apply=%region_4.5 | all-reduce | flops 4 | bytes 32 | tf_op jit(solution)/shard_map/psum | solution.py:72
  154.9 0.3 fusion.1
  155.2 3.3 %multiply_divide_fusion = (f32[4096,128]{1,0:T(8,128)S(1)}, f32[4096,128]{1,0:T(8,128)}) fusion(f32[4096,128]{1,0:T(8,128)S(1)} %bitcast.24, f32[4096]{0:T(1024)S(1)} %bitcast.38, f32[4096]{0:T(1024)S(1)} %bitcast.36, bf16[4096,128]{1,0:T(8,128)(2,1)S(1)} %copy-done.2), kind=kLoop, calls=%fused_computation.1 | loop fusion | flops 2097152 | bytes 7372800 | tf_op jit(solution)/shard_map/div | solution.py:76
  158.5 4.4 %multiply_add_fusion = f32[1,524288]{1,0:T(1,128)} fusion(f32[1,524288]{1,0:T(1,128)S(1)} %bitcast.31, bf16[1,524288]{1,0:T(2,128)(2,1)S(1)} %copy-done.3), kind=kLoop, calls=%fused_computation | loop fusion | flops 1572864 | bytes 5242880 | tf_op jit(solution)/shard_map/add | solution.py:77
  (27 shorter events, 0.4 us)
Async XLA Ops:
  7.2 3.9 %copy-start.4 = (bf16[1,1,524288]{2,1,0:T(2,128)(2,1)S(1)}, bf16[1,1,524288]{2,1,0:T(2,128)(2,1)}, u32[]{:S(2)}) copy-start(bf16[1,1,524288]{2,1,0:T(2,128)(2,1)} %param.8) | copy-start | bytes 3145732
  11.1 3.0 %copy-start.5 = (bf16[1,1,524288]{2,1,0:T(2,128)(2,1)S(1)}, bf16[1,1,524288]{2,1,0:T(2,128)(2,1)}, u32[]{:S(2)}) copy-start(bf16[1,1,524288]{2,1,0:T(2,128)(2,1)} %param.9) | copy-start | bytes 3145732
  14.1 2.3 %copy-start = (f32[1,1,524288]{2,1,0:T(1,128)}, f32[1,1,524288]{2,1,0:T(1,128)S(1)}, u32[]{:S(2)}) copy-start(f32[1,1,524288]{2,1,0:T(1,128)S(1)} %convert_multiply_fusion.1) | copy-start | bytes 6291460
  16.3 1.3 copy-start.1
  19.3 20.6 %all-to-all-start.1 = ((bf16[16,2,128]{2,1,0:T(2,128)(2,1)}), bf16[16,2,128]{2,1,0:T(2,128)(2,1)S(1)}, u32[]{:S(2)}, u32[]{:S(2)}) async-start(bf16[16,2,128]{2,1,0:T(2,128)(2,1)} %reshape.101), calls=%async_computation.1 | async-start | bytes 16384 | tf_op jit(solution)/shard_map/all_to_all | solution.py:52
  34.5 34.3 %copy-start.6 = (f32[1,32768]{1,0:T(1,128)S(1)}, f32[1,32768]{1,0:T(1,128)}, u32[]{:S(2)}) copy-start(f32[1,32768]{1,0:T(1,128)} %param.13) | copy-start | bytes 393220
  39.9 28.1 %all-to-all-start = ((bf16[16,256,128]{2,1,0:T(8,128)(2,1)}), bf16[16,256,128]{2,1,0:T(8,128)(2,1)S(1)}, u32[]{:S(2)}, u32[]{:S(2)}) async-start(bf16[16,256,128]{2,1,0:T(8,128)(2,1)} %divide_convert_fusion), calls=%async_computation | async-start | bytes 2097152 | tf_op jit(solution)/shard_map/all_to_all | solution.py:51
  43.7 79.8 %all-gather.3.cloned.1.call-start = ((), (), s32[]{:S(2)}) async-start(), calls=%async_computation.2 | async-start | bytes 1114112 | tf_op jit(solution)/shard_map/all_gather | solution.py:64
  69.6 6.6 %copy-start.7 = (s32[4]{0:T(128)S(1)}, s32[4]{0:T(128)}, u32[]{:S(2)}) copy-start(s32[4]{0:T(128)} %param.14) | copy-start | bytes 52
  123.5 31.7 %copy-start.2 = (bf16[4096,128]{1,0:T(8,128)(2,1)S(1)}, bf16[4096,128]{1,0:T(8,128)(2,1)}, u32[]{:S(2)}) copy-start(bf16[4096,128]{1,0:T(8,128)(2,1)} %all-gather.3.cloned.1.call-done) | copy-start | bytes 3145732
  155.2 3.3 %copy-start.3 = (bf16[1,524288]{1,0:T(2,128)(2,1)S(1)}, bf16[1,524288]{1,0:T(2,128)(2,1)}, u32[]{:S(2)}) copy-start(bf16[1,524288]{1,0:T(2,128)(2,1)} %param.12) | copy-start | bytes 3145732
Sparse Core Ops, SparseCore 0:
  69.8 53.6 all-gather.2
where the time goes:
time: 170 us
  blocking collectives  64.8 us (38%)
  waiting for transfers between devices  40.1 us (24%)
  other arithmetic  32 us (19%)
  starting transfers between devices  15.5 us (9%)
  between operations  15 us (9%)
  local copies, waits for them, and re-layouts  1.92 us (1%)
    all_gather x1, blocking collectives, body(): lax.all_gather(server_scales, 'dp', axis=0, tiled=True)  36.1 us
    psum x1, blocking collectives, body(): totals = lax.psum(partial_value, 'tensor')  28.7 us
    all_to_all x1, waiting for transfers between devices, body(): lax.all_to_all(levels, 'dp', split_axis=0, concat_axis=0, tiled=True)  23.6 us
    all_to_all x1, starting transfers between devices, body(): lax.all_to_all(scales, 'dp', split_axis=0, concat_axis=0, tiled=True)  11.7 us
    all_gather x1, waiting for transfers between devices, body(): lax.all_gather(server_levels, 'dp', axis=0, tiled=True)  11 us
    another operation x1, other arithmetic  6.54 us
    all_to_all x1, waiting for transfers between devices, body(): lax.all_to_all(scales, 'dp', split_axis=0, concat_axis=0, tiled=True)  5.47 us
    add x1, other arithmetic, body(): shaped.reshape(bucket_len) + DECAY * params[0].astype(jnp.float32)  4.43 us
  transfers between devices with their start and end apart: 3, of which 3 were waited for; matrix products, arithmetic and copies ran while one was open for 6% of the time, Pallas kernels for 0%

commit v1 on v0

v1 whole, which is shorter than its diff:
```python
import jax
import jax.numpy as jnp
from jax import lax
from jax.experimental import pallas as pl
from jax.experimental.pallas import tpu as pltpu
from jax.sharding import PartitionSpec as P

QB = 128
BETA_ONE = 0.9
BETA_TWO = 0.999
ADAM_EPS = 1e-08
DECAY = 0.1
CLIP_RMS = 2.0

BUCKET = 524288
SEGS = 4
N_Z = 4
N_Y = 4
N_DP = N_Z * N_Y
N_TENSOR = 16
SHARE = BUCKET // N_DP
ROWS = SHARE // QB
BLOCKS = BUCKET // QB
F32 = jnp.float32
BF16 = jnp.bfloat16
VMEM_LIMIT = 48 * 1024 * 1024


def params_of(**kwargs):
    return pltpu.CompilerParams(vmem_limit_bytes=VMEM_LIMIT, **kwargs)


def whole(shape):
    return pl.BlockSpec(shape, lambda i, *_: (0,) * len(shape))


def rows_of(values):
    return values.reshape(values.shape[-1] // QB, QB)


def prepare_kernel(place, grad, err, *outs):
    y = place[1]
    for k in range(N_Y):
        start = pl.multiple_of((y ^ k) * SHARE, SHARE)
        g = grad[0, :, pl.ds(start, SHARE)].astype(F32)
        e = err[0, :, pl.ds(start, SHARE)].astype(F32)
        outs[k][0] = rows_of((1.0 - BETA_ONE) * g + e).astype(BF16)


def prepare(place, grad, err):
    quarter = pl.BlockSpec((1, 1, N_Y * SHARE), lambda i, *_: (0, 0, i))
    out = jax.ShapeDtypeStruct((N_Z, ROWS, QB), BF16)
    return pl.pallas_call(
        prepare_kernel,
        grid_spec=pltpu.PrefetchScalarGridSpec(
            num_scalar_prefetch=1,
            grid=(N_Z,),
            in_specs=[quarter, quarter],
            out_specs=[pl.BlockSpec((1, ROWS, QB), lambda i, *_: (i, 0, 0))] * N_Y,
        ),
        out_shape=(out,) * N_Y,
        compiler_params=params_of(),
    )(place, grad, err)


def reduce_y_kernel(place, *refs):
    ins, outs = refs[:N_Y], refs[N_Y:]
    z = place[0]
    for k in range(N_Z):
        total = ins[0][z ^ k].astype(F32)
        for ref in ins[1:]:
            total = total + ref[z ^ k].astype(F32)
        outs[k][...] = total.astype(BF16)


def reduce_y(place, pieces):
    out = jax.ShapeDtypeStruct((ROWS, QB), BF16)
    return pl.pallas_call(
        reduce_y_kernel,
        grid_spec=pltpu.PrefetchScalarGridSpec(
            num_scalar_prefetch=1,
            grid=(1,),
            in_specs=[whole((N_Z, ROWS, QB))] * N_Y,
            out_specs=[whole((ROWS, QB))] * N_Z,
        ),
        out_shape=(out,) * N_Z,
        compiler_params=params_of(),
    )(place, *pieces)


def row_masks(starts, first_row, rows):
    index = first_row + lax.broadcasted_iota(jnp.int32, (rows, QB), 0)
    return [index >= starts[k] for k in range(1, SEGS)]


def server_kernel(place, starts, bias, *refs):
    ins = refs[:N_Z]
    momentum, variance, server_err, out = refs[N_Z:]
    total = ins[0][...].astype(F32)
    for ref in ins[1:]:
        total = total + ref[...].astype(F32)
    value = total * (1.0 / N_DP) + BETA_ONE * rows_of(momentum[...]) + rows_of(server_err[...])
    sent = value.astype(BF16)
    out[:ROWS, :] = sent
    kept = sent.astype(F32)
    direction = kept * bias[0] / (jnp.sqrt(rows_of(variance[...]) * bias[1]) + ADAM_EPS)
    squares = direction * direction
    masks = row_masks(starts, (place[0] * N_Y + place[1]) * ROWS, ROWS)
    seg = []
    for k in range(SEGS):
        picked = squares
        if k > 0:
            picked = jnp.where(masks[k - 1], picked, 0.0)
        if k < SEGS - 1:
            picked = jnp.where(masks[k], 0.0, picked)
        seg.append(jnp.sum(picked, axis=0, keepdims=True))
    sums = jnp.concatenate(seg + [jnp.zeros((8 - SEGS, QB), F32)], axis=0)
    high = sums.astype(BF16).astype(F32)
    low = sums - high
    out[ROWS:, :] = jnp.concatenate([high, low], axis=0).astype(BF16)


def server(place, starts, bias, pieces, momentum, variance, server_err):
    mine = pl.BlockSpec((1, SHARE), lambda i, place, *_: (0, place[0] * N_Y + place[1]))
    return pl.pallas_call(
        server_kernel,
        grid_spec=pltpu.PrefetchScalarGridSpec(
            num_scalar_prefetch=3,
            grid=(1,),
            in_specs=[whole((ROWS, QB))] * N_Z + [mine, mine, whole((1, SHARE))],
            out_specs=whole((ROWS + 16, QB)),
        ),
        out_shape=jax.ShapeDtypeStruct((ROWS + 16, QB), BF16),
        compiler_params=params_of(),
    )(place, starts, bias, *pieces, momentum, variance, server_err)


def join_kernel(*refs):
    ins, (out, sums) = refs[:N_Z], refs[N_Z:]
    total = jnp.zeros((8, QB), F32)
    for k, ref in enumerate(ins):
        out[k] = ref[:ROWS, :]
        tail = ref[ROWS:, :].astype(F32)
        total = total + (tail[:8] + tail[8:])
    sums[...] = jnp.broadcast_to(total[None], sums.shape)


def join(pieces):
    return pl.pallas_call(
        join_kernel,
        grid=(1,),
        in_specs=[whole((ROWS + 16, QB))] * N_Z,
        out_specs=[whole((N_Z, ROWS, QB)), whole((N_TENSOR, 8, QB))],
        out_shape=(
            jax.ShapeDtypeStruct((N_Z, ROWS, QB), BF16),
            jax.ShapeDtypeStruct((N_TENSOR, 8, QB), F32),
        ),
        compiler_params=params_of(),
    )(*pieces)


def final_kernel(place, starts, bias, *refs):
    pieces = refs[:N_Y]
    totals = refs[N_Y : 2 * N_Y]
    variance, weights, momentum_out, step_out = refs[2 * N_Y :]
    z, y = place[0], place[1]
    part = pl.program_id(0)
    total = totals[0][...]
    for ref in totals[1:]:
        total = total + ref[...]
    total = jnp.sum(total, axis=1, keepdims=True)
    inverse = []
    for k in range(SEGS):
        end = starts[k + 1] if k + 1 < SEGS else BLOCKS
        entries = (end - starts[k]).astype(F32) * (QB * N_TENSOR)
        root_mean = jnp.sqrt(total[k : k + 1] / entries + 1e-06)
        inverse.append(1.0 / jnp.maximum(1.0, root_mean / CLIP_RMS))
    for k in range(N_Y):
        row = pl.multiple_of((y ^ k) * ROWS, ROWS)
        col = pl.multiple_of((y ^ k) * SHARE, SHARE)
        kept = pieces[k][part ^ z].astype(F32)
        momentum_out[pl.ds(row, ROWS), :] = kept
        spread = jnp.sqrt(rows_of(variance[:, pl.ds(col, SHARE)]) * bias[1]) + ADAM_EPS
        direction = kept * bias[0] / spread
        factor = jnp.broadcast_to(inverse[0], (ROWS, QB))
        for seg, mask in enumerate(row_masks(starts, part * (N_Y * ROWS) + row, ROWS)):
            factor = jnp.where(mask, inverse[seg + 1], factor)
        decayed = DECAY * rows_of(weights[:, pl.ds(col, SHARE)].astype(F32))
        step_out[pl.ds(row, ROWS), :] = direction * factor + decayed


def final(place, starts, bias, pieces, totals, variance, weights):
    quarter = pl.BlockSpec((1, N_Y * SHARE), lambda i, *_: (0, i))
    out = jax.ShapeDtypeStruct((BLOCKS, QB), F32)
    return pl.pallas_call(
        final_kernel,
        grid_spec=pltpu.PrefetchScalarGridSpec(
            num_scalar_prefetch=3,
            grid=(N_Z,),
            in_specs=[whole((N_Z, ROWS, QB))] * N_Y + [whole((8, QB))] * N_Y + [quarter, quarter],
            out_specs=[pl.BlockSpec((N_Y * ROWS, QB), lambda i, *_: (i, 0))] * 2,
        ),
        out_shape=(out, out),
        compiler_params=params_of(),
    )(place, starts, bias, *pieces, *totals, variance, weights)


def exchange(value, mask):
    return lax.ppermute(value, "dp", [(i, i ^ mask) for i in range(N_DP)])


def body(grad, worker_err, momentum, variance, params, server_err, offsets, step_count):
    me = lax.axis_index("dp")
    place = jnp.stack([me // N_Y, me % N_Y]).astype(jnp.int32)
    starts = (offsets // QB).astype(jnp.int32)
    steps = step_count[0].astype(F32)
    first = 1.0 - jnp.power(F32(BETA_ONE), steps)
    second = 1.0 - jnp.power(F32(BETA_TWO), steps)
    bias = jnp.stack([1.0 / first, 1.0 / second])

    to_y = prepare(place, grad, worker_err)
    pieces = [to_y[0]] + [exchange(to_y[k], k) for k in range(1, N_Y)]
    to_z = reduce_y(place, pieces)
    pieces = [to_z[0]] + [exchange(to_z[k], k * N_Y) for k in range(1, N_Z)]
    mine = server(place, starts, bias, pieces, momentum, variance, server_err)
    column, sums = join([mine] + [exchange(mine, k * N_Y) for k in range(1, N_Z)])
    columns = [column] + [exchange(column, k) for k in range(1, N_Y)]
    sums = jnp.sum(lax.all_to_all(sums, "tensor", split_axis=0, concat_axis=0, tiled=True), axis=0)
    totals = [sums] + [exchange(sums, k) for k in range(1, N_Y)]
    momentum_new, param_step = final(place, starts, bias, columns, totals, variance, params)
    return (momentum_new.reshape(1, BUCKET), param_step.reshape(1, BUCKET))


def solution(mesh):
    placed = (
        P("dp", "tensor", None),
        P("dp", "tensor", None),
        P("tensor", None),
        P("tensor", None),
        P("tensor", None),
        P("tensor", "dp"),
        P(),
        P(),
    )
    return jax.shard_map(
        body,
        mesh=mesh,
        in_specs=placed,
        out_specs=(P("tensor", None), P("tensor", None)),
        check_vma=False,
    )
```

time: 170 us -> 81.1 us (0.48)
  blocking collectives: 64.8 us -> 15.1 us
  other arithmetic: 32 us -> 0.18 us
  between operations: 15 us -> 1.56 us
  waiting for transfers between devices: 40.1 us -> 28.1 us
  starting transfers between devices: 15.5 us -> 23.9 us
  Pallas kernels: 0 us -> 6.99 us
  local copies, waits for them, and re-layouts: 1.92 us -> 4.78 us
    all_gather x1 -> x0, blocking collectives: 36.1 us -> none  [body(): lax.all_gather(server_scales, 'dp', axis=0, tiled=True)]
    all_to_all x2 -> x0, waiting for transfers between devices: 29 us -> none  [the longest x1 23.6 us: body(): lax.all_to_all(levels, 'dp', split_axis=0, concat_axis=0, tiled=True)]
    psum x1 -> x0, blocking collectives: 28.7 us -> none  [body(): totals = lax.psum(partial_value, 'tensor')]
    ppermute x0 -> x15, waiting for transfers between devices: none -> 28.1 us  [exchange(): return lax.ppermute(value, 'dp', [(i, i ^ mask) for i in range(N_DP)])]
    ppermute x0 -> x15, starting transfers between devices: none -> 23.9 us  [exchange(): return lax.ppermute(value, 'dp', [(i, i ^ mask) for i in range(N_DP)])]
    all_to_all x2 -> x0, starting transfers between devices: 15.5 us -> none  [the longest x1 11.7 us: body(): lax.all_to_all(scales, 'dp', split_axis=0, concat_axis=0, tiled=True)]
    all_to_all x0 -> x1, blocking collectives: none -> 15.1 us  [body(): lax.all_to_all(sums, 'tensor', split_axis=0, concat_axis=0, tiled=True)]
    all_gather x1 -> x0, waiting for transfers between devices: 11 us -> none  [body(): lax.all_gather(server_levels, 'dp', axis=0, tiled=True)]
  transfers between devices with their start and end apart: 3 -> 15, of which waited for: 3 -> 10; matrix products, arithmetic and copies ran while one was open for 6% -> 0% of each run, Pallas kernels for 0% -> 0%
where the time goes in v1:
time: 81.1 us; the launch traced here: 80.7 us
  waiting for transfers between devices  28.1 us (35%)
  starting transfers between devices  23.9 us (29%)
  blocking collectives  15.1 us (19%)
  Pallas kernels  6.99 us (9%)
  local copies, waits for them, and re-layouts  4.78 us (6%)
  between operations  1.56 us (2%)
    ppermute x15, waiting for transfers between devices, exchange(): return lax.ppermute(value, 'dp', [(i, i ^ mask) for i in range(N_DP)])  28.1 us
    ppermute x15, starting transfers between devices, exchange(): return lax.ppermute(value, 'dp', [(i, i ^ mask) for i in range(N_DP)])  23.9 us
    all_to_all x1, blocking collectives, body(): lax.all_to_all(sums, 'tensor', split_axis=0, concat_axis=0, tiled=True)  15.1 us
    unnamed x14, local copies, waits for them, and re-layouts  4.78 us
    pallas_call x1, Pallas kernels, final(): pl.pallas_call(final_kernel, grid_spec=pltpu.PrefetchScalarGridSpec(num_s...  4.14 us
  transfers between devices with their start and end apart: 15, of which 10 were waited for; matrix products, arithmetic and copies ran while one was open for 0% of the time, Pallas kernels for 0%

profile of v1, /device:TPU:1, one launch (start us, length us, event | category | flops | bytes accessed | tf_op | source)
XLA Modules:
  0.0 80.7 jit_solution(15479604625099478645)
XLA Ops:
  0.7 1.6 %copy-done.2 = bf16[1,1,524288]{2,1,0:T(2,128)(2,1)S(1)} copy-done((bf16[1,1,524288]{2,1,0:T(2,128)(2,1)S(1)}, bf16[1,1,524288]{2,1,0:T(2,128)(2,1)}, u32[]{:S(2)}) %copy-start.2) | copy-done | bytes 1048600
  2.3 1.6 %copy-done.3 = bf16[1,1,524288]{2,1,0:T(2,128)(2,1)S(1)} copy-done((bf16[1,1,524288]{2,1,0:T(2,128)(2,1)S(1)}, bf16[1,1,524288]{2,1,0:T(2,128)(2,1)}, u32[]{:S(2)}) %copy-start.3) | copy-done | bytes 1048600
  3.9 1.4 %shard_map.95 = (bf16[4,256,128]{2,1,0:T(8,128)(2,1)S(1)}, bf16[4,256,128]{2,1,0:T(8,128)(2,1)S(1)}, bf16[4,256,128]{2,1,0:T(8,128)(2,1)S(1)}, bf16[4,256,128]{2,1,0:T(8,128)(2,1)S(1)}) custom-call(s32[2]{0:T(128)S(1)} %pad_add_fusion.place, bf16[1,1,524288]{2,1,0:T(2,128)(2,1)S(1)} %copy-done.2, bf16[1,1,524288]{2,1,0:T(2,128)(2,1)S(1)} %copy-done.3), custom_call_target="tpu_custom_call" | custom-call | tf_op jit(solution)/shard_map/pallas_call | solution.py:53
  5.3 2.2 %collective-permute-start = (bf16[4,256,128]{2,1,0:T(8,128)(2,1)S(1)}, bf16[4,256,128]{2,1,0:T(8,128)(2,1)S(1)}, u32[]{:S(2)}, u32[]{:S(2)}) collective-permute-start(bf16[4,256,128]{2,1,0:T(8,128)(2,1)S(1)} %get-tuple-element.15), channel_id=1, source_target_pairs={{0,16},{16,0},{32,48},{48,32},{64,80},{80,64},{96,112},{112,96},{1... | collective-permute-start | bytes 786440 | tf_op jit(solution)/shard_map/ppermute | solution.py:209
  7.5 2.6 %collective-permute-start.1 = (bf16[4,256,128]{2,1,0:T(8,128)(2,1)S(1)}, bf16[4,256,128]{2,1,0:T(8,128)(2,1)S(1)}, u32[]{:S(2)}, u32[]{:S(2)}) collective-permute-start(bf16[4,256,128]{2,1,0:T(8,128)(2,1)S(1)} %get-tuple-element.16), channel_id=1, source_target_pairs={{0,32},{16,48},{32,0},{48,16},{64,96},{80,112},{96,64},{112,80},{1... | collective-permute-start | bytes 786440 | tf_op jit(solution)/shard_map/ppermute | solution.py:209
  11.0 1.3 %collective-permute-done.refs_1_ = bf16[4,256,128]{2,1,0:T(8,128)(2,1)S(1)} collective-permute-done((bf16[4,256,128]{2,1,0:T(8,128)(2,1)S(1)}, bf16[4,256,128]{2,1,0:T(8,128)(2,1)S(1)}, u32[]{:S(2)}, u32[]{:S(2)}) %collective-permute-start) | collective-permute-done | bytes 262176 | tf_op jit(solution)/shard_map/ppermute | solution.py:209
  12.3 9.2 %collective-permute-done.1.refs_2_ = bf16[4,256,128]{2,1,0:T(8,128)(2,1)S(1)} collective-permute-done((bf16[4,256,128]{2,1,0:T(8,128)(2,1)S(1)}, bf16[4,256,128]{2,1,0:T(8,128)(2,1)S(1)}, u32[]{:S(2)}, u32[]{:S(2)}) %collective-permute-start.1) | collective-permute-done | bytes 262176 | tf_op jit(solution)/shard_map/ppermute | solution.py:209
  21.5 2.0 %collective-permute-done.2.refs_3_ = bf16[4,256,128]{2,1,0:T(8,128)(2,1)S(1)} collective-permute-done((bf16[4,256,128]{2,1,0:T(8,128)(2,1)S(1)}, bf16[4,256,128]{2,1,0:T(8,128)(2,1)S(1)}, u32[]{:S(2)}, u32[]{:S(2)}) %collective-permute-start.2) | collective-permute-done | bytes 262176 | tf_op jit(solution)/shard_map/ppermute | solution.py:209
  24.2 3.1 %collective-permute-start.3 = (bf16[256,128]{1,0:T(8,128)(2,1)S(1)}, bf16[256,128]{1,0:T(8,128)(2,1)S(1)}, u32[]{:S(2)}, u32[]{:S(2)}) collective-permute-start(bf16[256,128]{1,0:T(8,128)(2,1)S(1)} %get-tuple-element.19), channel_id=1, source_target_pairs={{0,64},{16,80},{32,96},{48,112},{64,0},{80,16},{96,32},{112,48},{1... | collective-permute-start | bytes 196616 | tf_op jit(solution)/shard_map/ppermute | solution.py:209
  27.3 5.1 %collective-permute-start.4 = (bf16[256,128]{1,0:T(8,128)(2,1)S(1)}, bf16[256,128]{1,0:T(8,128)(2,1)S(1)}, u32[]{:S(2)}, u32[]{:S(2)}) collective-permute-start(bf16[256,128]{1,0:T(8,128)(2,1)S(1)} %get-tuple-element.20), channel_id=1, source_target_pairs={{0,128},{16,144},{32,160},{48,176},{64,192},{80,208},{96,224},{112... | collective-permute-start | bytes 196616 | tf_op jit(solution)/shard_map/ppermute | solution.py:209
  32.5 2.4 %collective-permute-done.4.refs_2_ = bf16[256,128]{1,0:T(8,128)(2,1)S(1)} collective-permute-done((bf16[256,128]{1,0:T(8,128)(2,1)S(1)}, bf16[256,128]{1,0:T(8,128)(2,1)S(1)}, u32[]{:S(2)}, u32[]{:S(2)}) %collective-permute-start.4) | collective-permute-done | bytes 65568 | tf_op jit(solution)/shard_map/ppermute | solution.py:209
  34.9 3.5 %collective-permute-done.5.refs_3_ = bf16[256,128]{1,0:T(8,128)(2,1)S(1)} collective-permute-done((bf16[256,128]{1,0:T(8,128)(2,1)S(1)}, bf16[256,128]{1,0:T(8,128)(2,1)S(1)}, u32[]{:S(2)}, u32[]{:S(2)}) %collective-permute-start.5) | collective-permute-done | bytes 65568 | tf_op jit(solution)/shard_map/ppermute | solution.py:209
  38.4 0.8 shard_map.97.refs_0_
  39.1 1.5 %collective-permute-start.8 = (bf16[272,128]{1,0:T(8,128)(2,1)S(1)}, bf16[272,128]{1,0:T(8,128)(2,1)S(1)}, u32[]{:S(2)}, u32[]{:S(2)}) collective-permute-start(bf16[272,128]{1,0:T(8,128)(2,1)S(1)} %shard_map.97.refs_0_), channel_id=1, source_target_pairs={{0,192},{16,208},{32,224},{48,240},{64,128},{80,144},{96,160},{112... | collective-permute-start | bytes 208904 | tf_op jit(solution)/shard_map/ppermute | solution.py:209
  40.6 4.5 %collective-permute-start.7 = (bf16[272,128]{1,0:T(8,128)(2,1)S(1)}, bf16[272,128]{1,0:T(8,128)(2,1)S(1)}, u32[]{:S(2)}, u32[]{:S(2)}) collective-permute-start(bf16[272,128]{1,0:T(8,128)(2,1)S(1)} %shard_map.97.refs_0_), channel_id=1, source_target_pairs={{0,128},{16,144},{32,160},{48,176},{64,192},{80,208},{96,224},{112... | collective-permute-start | bytes 208904 | tf_op jit(solution)/shard_map/ppermute | solution.py:209
  45.1 2.8 %collective-permute-done.7.refs_2_ = bf16[272,128]{1,0:T(8,128)(2,1)S(1)} collective-permute-done((bf16[272,128]{1,0:T(8,128)(2,1)S(1)}, bf16[272,128]{1,0:T(8,128)(2,1)S(1)}, u32[]{:S(2)}, u32[]{:S(2)}) %collective-permute-start.7) | collective-permute-done | bytes 69664 | tf_op jit(solution)/shard_map/ppermute | solution.py:209
  47.9 2.3 %collective-permute-done.6.refs_1_ = bf16[272,128]{1,0:T(8,128)(2,1)S(1)} collective-permute-done((bf16[272,128]{1,0:T(8,128)(2,1)S(1)}, bf16[272,128]{1,0:T(8,128)(2,1)S(1)}, u32[]{:S(2)}, u32[]{:S(2)}) %collective-permute-start.6) | collective-permute-done | bytes 69664 | tf_op jit(solution)/shard_map/ppermute | solution.py:209
  50.4 3.1 %collective-permute-start.9 = (bf16[4,256,128]{2,1,0:T(8,128)(2,1)S(1)}, bf16[4,256,128]{2,1,0:T(8,128)(2,1)S(1)}, u32[]{:S(2)}, u32[]{:S(2)}) collective-permute-start(bf16[4,256,128]{2,1,0:T(8,128)(2,1)S(1)} %get-tuple-element.22.refs_0_), channel_id=1, source_target_pairs={{0,16},{16,0},{32,48},{48,32},{64,80},{80,64},{96,112},{112,96},{1... | collective-permute-start | bytes 786440 | tf_op jit(solution)/shard_map/ppermute | solution.py:209
  53.6 15.1 %all_to_all.5 = f32[16,8,128]{2,1,0:T(8,128)S(1)} all-to-all(f32[16,8,128]{2,1,0:T(8,128)S(1)} %get-tuple-element.23), channel_id=1, replica_groups=mesh['dp'=16,'tensor'=16] {'tensor'}, dimensions={0} | all-to-all | bytes 131072 | tf_op jit(solution)/shard_map/all_to_all | solution.py:228
  68.8 1.5 %collective-permute-start.13 = (f32[8,128]{1,0:T(8,128)S(1)}, f32[8,128]{1,0:T(8,128)S(1)}, u32[]{:S(2)}, u32[]{:S(2)}) collective-permute-start(f32[8,128]{1,0:T(8,128)S(1)} %reduce_sum.9.refs_4_), channel_id=1, source_target_pairs={{0,32},{16,48},{32,0},{48,16},{64,96},{80,112},{96,64},{112,80},{1... | collective-permute-start | bytes 12296 | tf_op jit(solution)/shard_map/ppermute | solution.py:209
  70.3 2.2 %collective-permute-done.14.refs_7_ = f32[8,128]{1,0:T(8,128)S(1)} collective-permute-done((f32[8,128]{1,0:T(8,128)S(1)}, f32[8,128]{1,0:T(8,128)S(1)}, u32[]{:S(2)}, u32[]{:S(2)}) %collective-permute-start.14) | collective-permute-done | bytes 4128 | tf_op jit(solution)/shard_map/ppermute | solution.py:209
  72.8 2.1 %collective-permute-done.12.refs_5_ = f32[8,128]{1,0:T(8,128)S(1)} collective-permute-done((f32[8,128]{1,0:T(8,128)S(1)}, f32[8,128]{1,0:T(8,128)S(1)}, u32[]{:S(2)}, u32[]{:S(2)}) %collective-permute-start.12) | collective-permute-done | bytes 4128 | tf_op jit(solution)/shard_map/ppermute | solution.py:209
  74.9 1.6 %copy-done.4 = bf16[1,524288]{1,0:T(2,128)(2,1)S(1)} copy-done((bf16[1,524288]{1,0:T(2,128)(2,1)S(1)}, bf16[1,524288]{1,0:T(2,128)(2,1)}, u32[]{:S(2)}) %copy-start.4) | copy-done | bytes 1048600
  76.5 4.1 %shard_map.99 = (f32[4096,128]{1,0:T(8,128)}, f32[4096,128]{1,0:T(8,128)}) custom-call(s32[2]{0:T(128)S(1)} %pad_add_fusion.place, s32[4]{0:T(128)S(1)} %and_select_fusion.starts, f32[2]{0:T(128)S(1)} %pad_maximum_fusion.bias, bf16[4,256,128]{2,1,0:T(8,128)(2,1)S(1)} %get-tuple-element.22.refs_0_, bf16[4,256,128]{2,1,0:T(8,128)(2,1)S(1)} %collective-permute-done.9.refs_1_, ...), custom_call_target="tpu_custom_call" | custom-call | tf_op jit(solution)/shard_map/pallas_call | solution.py:195
  (30 shorter events, 1.6 us)
Async XLA Ops:
  0.6 10.4 %copy-start.6 = (s32[4]{0:T(128)S(1)}, s32[4]{0:T(128)}, u32[]{:S(2)}) copy-start(s32[4]{0:T(128)} %param.14) | copy-start | bytes 52
  0.7 1.6 %copy-start.2 = (bf16[1,1,524288]{2,1,0:T(2,128)(2,1)S(1)}, bf16[1,1,524288]{2,1,0:T(2,128)(2,1)}, u32[]{:S(2)}) copy-start(bf16[1,1,524288]{2,1,0:T(2,128)(2,1)} %grad.1) | copy-start | bytes 3145732
  2.3 1.6 %copy-start.3 = (bf16[1,1,524288]{2,1,0:T(2,128)(2,1)S(1)}, bf16[1,1,524288]{2,1,0:T(2,128)(2,1)}, u32[]{:S(2)}) copy-start(bf16[1,1,524288]{2,1,0:T(2,128)(2,1)} %err.1) | copy-start | bytes 3145732
  3.9 34.4 %copy-start = (f32[1,524288]{1,0:T(1,128)S(1)}, f32[1,524288]{1,0:T(1,128)}, u32[]{:S(2)}) copy-start(f32[1,524288]{1,0:T(1,128)} %refs_8_.1) | copy-start | bytes 6291460
  3.9 34.4 %copy-start.1 = (f32[1,524288]{1,0:T(1,128)S(1)}, f32[1,524288]{1,0:T(1,128)}, u32[]{:S(2)}) copy-start(f32[1,524288]{1,0:T(1,128)} %refs_4_.1) | copy-start | bytes 6291460
  3.9 34.4 %copy-start.5 = (f32[1,32768]{1,0:T(1,128)S(1)}, f32[1,32768]{1,0:T(1,128)}, u32[]{:S(2)}) copy-start(f32[1,32768]{1,0:T(1,128)} %refs_6_.1) | copy-start | bytes 393220
  5.3 7.0 %collective-permute-start = (bf16[4,256,128]{2,1,0:T(8,128)(2,1)S(1)}, bf16[4,256,128]{2,1,0:T(8,128)(2,1)S(1)}, u32[]{:S(2)}, u32[]{:S(2)}) collective-permute-start(bf16[4,256,128]{2,1,0:T(8,128)(2,1)S(1)} %get-tuple-element.15), channel_id=1, source_target_pairs={{0,16},{16,0},{32,48},{48,32},{64,80},{80,64},{96,112},{112,96},{1... | collective-permute-start | bytes 786440 | tf_op jit(solution)/shard_map/ppermute | solution.py:209
  7.5 14.0 %collective-permute-start.1 = (bf16[4,256,128]{2,1,0:T(8,128)(2,1)S(1)}, bf16[4,256,128]{2,1,0:T(8,128)(2,1)S(1)}, u32[]{:S(2)}, u32[]{:S(2)}) collective-permute-start(bf16[4,256,128]{2,1,0:T(8,128)(2,1)S(1)} %get-tuple-element.16), channel_id=1, source_target_pairs={{0,32},{16,48},{32,0},{48,16},{64,96},{80,112},{96,64},{112,80},{1... | collective-permute-start | bytes 786440 | tf_op jit(solution)/shard_map/ppermute | solution.py:209
  10.2 13.4 %collective-permute-start.2 = (bf16[4,256,128]{2,1,0:T(8,128)(2,1)S(1)}, bf16[4,256,128]{2,1,0:T(8,128)(2,1)S(1)}, u32[]{:S(2)}, u32[]{:S(2)}) collective-permute-start(bf16[4,256,128]{2,1,0:T(8,128)(2,1)S(1)} %get-tuple-element.17), channel_id=1, source_target_pairs={{0,48},{16,32},{32,16},{48,0},{64,112},{80,96},{96,80},{112,64},{1... | collective-permute-start | bytes 786440 | tf_op jit(solution)/shard_map/ppermute | solution.py:209
  24.2 8.3 %collective-permute-start.3 = (bf16[256,128]{1,0:T(8,128)(2,1)S(1)}, bf16[256,128]{1,0:T(8,128)(2,1)S(1)}, u32[]{:S(2)}, u32[]{:S(2)}) collective-permute-start(bf16[256,128]{1,0:T(8,128)(2,1)S(1)} %get-tuple-element.19), channel_id=1, source_target_pairs={{0,64},{16,80},{32,96},{48,112},{64,0},{80,16},{96,32},{112,48},{1... | collective-permute-start | bytes 196616 | tf_op jit(solution)/shard_map/ppermute | solution.py:209
  27.3 7.6 %collective-permute-start.4 = (bf16[256,128]{1,0:T(8,128)(2,1)S(1)}, bf16[256,128]{1,0:T(8,128)(2,1)S(1)}, u32[]{:S(2)}, u32[]{:S(2)}) collective-permute-start(bf16[256,128]{1,0:T(8,128)(2,1)S(1)} %get-tuple-element.20), channel_id=1, source_target_pairs={{0,128},{16,144},{32,160},{48,176},{64,192},{80,208},{96,224},{112... | collective-permute-start | bytes 196616 | tf_op jit(solution)/shard_map/ppermute | solution.py:209
  32.4 5.9 %collective-permute-start.5 = (bf16[256,128]{1,0:T(8,128)(2,1)S(1)}, bf16[256,128]{1,0:T(8,128)(2,1)S(1)}, u32[]{:S(2)}, u32[]{:S(2)}) collective-permute-start(bf16[256,128]{1,0:T(8,128)(2,1)S(1)} %get-tuple-element.21), channel_id=1, source_target_pairs={{0,192},{16,208},{32,224},{48,240},{64,128},{80,144},{96,160},{112... | collective-permute-start | bytes 196616 | tf_op jit(solution)/shard_map/ppermute | solution.py:209
  39.1 6.0 %collective-permute-start.8 = (bf16[272,128]{1,0:T(8,128)(2,1)S(1)}, bf16[272,128]{1,0:T(8,128)(2,1)S(1)}, u32[]{:S(2)}, u32[]{:S(2)}) collective-permute-start(bf16[272,128]{1,0:T(8,128)(2,1)S(1)} %shard_map.97.refs_0_), channel_id=1, source_target_pairs={{0,192},{16,208},{32,224},{48,240},{64,128},{80,144},{96,160},{112... | collective-permute-start | bytes 208904 | tf_op jit(solution)/shard_map/ppermute | solution.py:209
  40.6 7.2 %collective-permute-start.7 = (bf16[272,128]{1,0:T(8,128)(2,1)S(1)}, bf16[272,128]{1,0:T(8,128)(2,1)S(1)}, u32[]{:S(2)}, u32[]{:S(2)}) collective-permute-start(bf16[272,128]{1,0:T(8,128)(2,1)S(1)} %shard_map.97.refs_0_), channel_id=1, source_target_pairs={{0,128},{16,144},{32,160},{48,176},{64,192},{80,208},{96,224},{112... | collective-permute-start | bytes 208904 | tf_op jit(solution)/shard_map/ppermute | solution.py:209
  45.1 5.1 %collective-permute-start.6 = (bf16[272,128]{1,0:T(8,128)(2,1)S(1)}, bf16[272,128]{1,0:T(8,128)(2,1)S(1)}, u32[]{:S(2)}, u32[]{:S(2)}) collective-permute-start(bf16[272,128]{1,0:T(8,128)(2,1)S(1)} %shard_map.97.refs_0_), channel_id=1, source_target_pairs={{0,64},{16,80},{32,96},{48,112},{64,0},{80,16},{96,32},{112,48},{1... | collective-permute-start | bytes 208904 | tf_op jit(solution)/shard_map/ppermute | solution.py:209
  50.2 24.7 %collective-permute-start.11 = (bf16[4,256,128]{2,1,0:T(8,128)(2,1)S(1)}, bf16[4,256,128]{2,1,0:T(8,128)(2,1)S(1)}, u32[]{:S(2)}, u32[]{:S(2)}) collective-permute-start(bf16[4,256,128]{2,1,0:T(8,128)(2,1)S(1)} %get-tuple-element.22.refs_0_), channel_id=1, source_target_pairs={{0,48},{16,32},{32,16},{48,0},{64,112},{80,96},{96,80},{112,64},{1... | collective-permute-start | bytes 786440 | tf_op jit(solution)/shard_map/ppermute | solution.py:209
  50.4 24.5 %collective-permute-start.10 = (bf16[4,256,128]{2,1,0:T(8,128)(2,1)S(1)}, bf16[4,256,128]{2,1,0:T(8,128)(2,1)S(1)}, u32[]{:S(2)}, u32[]{:S(2)}) collective-permute-start(bf16[4,256,128]{2,1,0:T(8,128)(2,1)S(1)} %get-tuple-element.22.refs_0_), channel_id=1, source_target_pairs={{0,32},{16,48},{32,0},{48,16},{64,96},{80,112},{96,64},{112,80},{1... | collective-permute-start | bytes 786440 | tf_op jit(solution)/shard_map/ppermute | solution.py:209
  50.4 24.5 %collective-permute-start.9 = (bf16[4,256,128]{2,1,0:T(8,128)(2,1)S(1)}, bf16[4,256,128]{2,1,0:T(8,128)(2,1)S(1)}, u32[]{:S(2)}, u32[]{:S(2)}) collective-permute-start(bf16[4,256,128]{2,1,0:T(8,128)(2,1)S(1)} %get-tuple-element.22.refs_0_), channel_id=1, source_target_pairs={{0,16},{16,0},{32,48},{48,32},{64,80},{80,64},{96,112},{112,96},{1... | collective-permute-start | bytes 786440 | tf_op jit(solution)/shard_map/ppermute | solution.py:209
  68.7 3.8 %collective-permute-start.14 = (f32[8,128]{1,0:T(8,128)S(1)}, f32[8,128]{1,0:T(8,128)S(1)}, u32[]{:S(2)}, u32[]{:S(2)}) collective-permute-start(f32[8,128]{1,0:T(8,128)S(1)} %reduce_sum.9.refs_4_), channel_id=1, source_target_pairs={{0,48},{16,32},{32,16},{48,0},{64,112},{80,96},{96,80},{112,64},{1... | collective-permute-start | bytes 12296 | tf_op jit(solution)/shard_map/ppermute | solution.py:209
  68.8 4.0 %collective-permute-start.13 = (f32[8,128]{1,0:T(8,128)S(1)}, f32[8,128]{1,0:T(8,128)S(1)}, u32[]{:S(2)}, u32[]{:S(2)}) collective-permute-start(f32[8,128]{1,0:T(8,128)S(1)} %reduce_sum.9.refs_4_), channel_id=1, source_target_pairs={{0,32},{16,48},{32,0},{48,16},{64,96},{80,112},{96,64},{112,80},{1... | collective-permute-start | bytes 12296 | tf_op jit(solution)/shard_map/ppermute | solution.py:209
  72.5 2.5 %collective-permute-start.12 = (f32[8,128]{1,0:T(8,128)S(1)}, f32[8,128]{1,0:T(8,128)S(1)}, u32[]{:S(2)}, u32[]{:S(2)}) collective-permute-start(f32[8,128]{1,0:T(8,128)S(1)} %reduce_sum.9.refs_4_), channel_id=1, source_target_pairs={{0,16},{16,0},{32,48},{48,32},{64,80},{80,64},{96,112},{112,96},{1... | collective-permute-start | bytes 12296 | tf_op jit(solution)/shard_map/ppermute | solution.py:209
  74.9 1.6 %copy-start.4 = (bf16[1,524288]{1,0:T(2,128)(2,1)S(1)}, bf16[1,524288]{1,0:T(2,128)(2,1)}, u32[]{:S(2)}) copy-start(bf16[1,524288]{1,0:T(2,128)(2,1)} %refs_9_.1) | copy-start | bytes 3145732

commit v2 on v0

v2 whole, which is shorter than its diff:
```python
import jax
import jax.numpy as jnp
from jax import lax
from jax.experimental import pallas as pl
from jax.experimental.pallas import tpu as pltpu
from jax.sharding import Mesh, PartitionSpec as P

QB = 128
BETA_ONE = 0.9
BETA_TWO = 0.999
ADAM_EPS = 1e-08
DECAY = 0.1
CLIP_RMS = 2.0

BUCKET = 524288
SEGS = 4
N_Z = 4
N_Y = 4
N_DP = N_Z * N_Y
N_TENSOR = 16
SHARE = BUCKET // N_DP
ROWS = SHARE // QB
BLOCKS = BUCKET // QB
HALF = N_Z // 2
F32 = jnp.float32
BF16 = jnp.bfloat16
MIB = 1024 * 1024
PREPARE_LIMIT = 60
STEP_ROWS = 512
ORDER = (2, 1, 3)
LAST_ORDER = (3, 1, 2)


def on_chip(count):
    return [pl.BlockSpec(memory_space=pltpu.VMEM)] * count


def anywhere(count):
    return [pl.BlockSpec(memory_space=pl.ANY)] * count


def like(shape, dtype):
    return jax.ShapeDtypeStruct(shape, dtype)


def rows_of(values):
    return values.reshape(values.shape[-1] // QB, QB)


def call(kernel, scalars, arrays, in_specs, out_specs, out_shape, scratch=(), limit=16):
    return pl.pallas_call(
        kernel,
        in_specs=[pl.BlockSpec(memory_space=pltpu.SMEM)] * len(scalars) + in_specs,
        out_specs=out_specs,
        out_shape=out_shape,
        scratch_shapes=scratch,
        compiler_params=pltpu.CompilerParams(vmem_limit_bytes=limit * MIB),
    )(*scalars, *arrays)


def my_z():
    return lax.axis_index("z")


def my_y():
    return lax.axis_index("y")


def share_of(ref, block):
    return rows_of(ref[:, pl.ds(pl.multiple_of(block * SHARE, SHARE), SHARE)])


def rows_at(block):
    return pl.ds(pl.multiple_of(block * ROWS, ROWS), ROWS)


def prepare_kernel(grad, err, *refs):
    outs, (held_grad, held_err, sems) = refs[:N_Y], refs[N_Y:]
    y = my_y()
    copies = []
    for s in range(N_Z):
        block = pl.ds(s * N_Y * SHARE, N_Y * SHARE)
        copies.append(
            (
                pltpu.make_async_copy(grad.at[:, :, block], held_grad.at[:, :, block], sems.at[0, s]),
                pltpu.make_async_copy(err.at[:, :, block], held_err.at[:, :, block], sems.at[1, s]),
            )
        )
    for pair in copies:
        for copy in pair:
            copy.start()
    for s in range(N_Z):
        for copy in copies[s]:
            copy.wait()
        for k in range(N_Y):
            block = pl.ds(pl.multiple_of((s * N_Y + (y ^ k)) * SHARE, SHARE), SHARE)
            g = held_grad[0, :, block].astype(F32)
            e = held_err[0, :, block].astype(F32)
            outs[k][s] = rows_of((1.0 - BETA_ONE) * g + e).astype(BF16)


def prepare(grad, err):
    held = pltpu.VMEM((1, 1, BUCKET), BF16)
    return call(
        prepare_kernel,
        (),
        (grad, err),
        anywhere(2),
        on_chip(N_Y),
        (like((N_Z, ROWS, QB), BF16),) * N_Y,
        scratch=[held, held, pltpu.SemaphoreType.DMA((2, N_Z))],
        limit=PREPARE_LIMIT,
    )


def reduce_y_kernel(*refs):
    ins, server_err, outs = refs[:N_Y], refs[N_Y], refs[-2:]
    mine = rows_of(server_err[...])
    z = my_z()
    for s in range(N_Z):
        total = ins[0][s].astype(F32)
        for ref in ins[1:]:
            total = total + ref[s].astype(F32)
        total = total * (1.0 / N_DP) + jnp.where(z == s, mine, 0.0)
        outs[s // HALF][s % HALF] = total.astype(BF16)


def reduce_y(pieces, server_err, *staged):
    return call(
        reduce_y_kernel,
        (),
        (*pieces, server_err, *staged),
        on_chip(N_Y + 1) + anywhere(len(staged)),
        on_chip(2),
        (like((HALF, ROWS, QB), BF16),) * 2,
    )


def add_kernel(ours, theirs, out):
    out[...] = (ours[...].astype(F32) + theirs[...].astype(F32)).astype(BF16)


def add(ours, theirs):
    (out,) = call(add_kernel, (), (ours, theirs), on_chip(2), on_chip(1), [like((HALF, ROWS, QB), BF16)])
    return out


def row_masks(offsets, first_row, rows):
    entry = (first_row + lax.broadcasted_iota(jnp.int32, (rows, QB), 0)) * QB
    return [entry >= offsets[k] for k in range(1, SEGS)]


def server_kernel(offsets, low, high, other_low, other_high, momentum, spread, column, out):
    y = my_y()
    seg = [jnp.zeros((1, QB), F32)] * SEGS
    for s in range(N_Z):
        ours, theirs = (low, other_low) if s < HALF else (high, other_high)
        total = ours[s % HALF].astype(F32) + theirs[s % HALF].astype(F32)
        block = s * N_Y + y
        sent = (total + BETA_ONE * share_of(momentum, block)).astype(BF16)
        column[s] = sent
        direction = sent.astype(F32) * spread[s]
        squares = direction * direction
        masks = row_masks(offsets, block * ROWS, ROWS)
        for k in range(SEGS):
            picked = squares
            if k > 0:
                picked = jnp.where(masks[k - 1], picked, 0.0)
            if k < SEGS - 1:
                picked = jnp.where(masks[k], 0.0, picked)
            seg[k] = seg[k] + jnp.sum(picked, axis=0, keepdims=True)
    sums = jnp.concatenate(seg + [jnp.zeros((8 - SEGS, QB), F32)], axis=0)
    sums = sums + pltpu.roll(sums, QB // 2, 1)
    sums = sums + pltpu.roll(sums, QB // 4, 1)
    lane = lax.broadcasted_iota(jnp.int32, (8, QB), 1) // (QB // SEGS)
    mine = jnp.where(lane == lax.broadcasted_iota(jnp.int32, (8, QB), 0), sums, 0.0)
    out[...] = jnp.broadcast_to(jnp.sum(mine, axis=0, keepdims=True)[None], out.shape)


def server(offsets, halves, momentum, spread):
    return call(
        server_kernel,
        (offsets,),
        (*halves, momentum, spread),
        on_chip(6),
        on_chip(2),
        (like((N_Z, ROWS, QB), BF16), like((N_Y * N_TENSOR, 1, QB), F32)),
    )


def stage_kernel(bias, variance, weights, spread, column_spread, dense, held, sems):
    copies = []
    for block in range(N_DP):
        rows = pl.ds(block * ROWS, ROWS)
        root = jnp.sqrt(share_of(variance, block) * bias[1]) + ADAM_EPS
        held[rows, :] = bias[0] / root
        dense[rows, :] = share_of(weights, block).astype(BF16)
        if block % N_Y == N_Y - 1:
            rows = pl.ds((block + 1 - N_Y) * ROWS, N_Y * ROWS)
            copies.append(pltpu.make_async_copy(held.at[rows], spread.at[rows], sems.at[block // N_Y]))
            copies[-1].start()
    for s in range(N_Z):
        column_spread[s] = held[rows_at(s * N_Y + my_y()), :]
    for copy in copies:
        copy.wait()


def stage(bias, variance, weights):
    return call(
        stage_kernel,
        (bias,),
        (variance, weights),
        on_chip(2),
        anywhere(1) + on_chip(2),
        (like((BLOCKS, QB), F32), like((N_Z, ROWS, QB), F32), like((BLOCKS, QB), BF16)),
        scratch=[pltpu.VMEM((BLOCKS, QB), F32), pltpu.SemaphoreType.DMA((N_Z,))],
    )


def momentum_kernel(*refs):
    pieces, (spread, out, direction, held, held_spread, sems) = refs[:N_Y], refs[N_Y:]
    y = my_y()
    parts = [pl.ds(s * N_Y * ROWS, N_Y * ROWS) for s in range(N_Z)]
    loads = [pltpu.make_async_copy(spread.at[rows], held_spread.at[rows], sems.at[0, s]) for s, rows in enumerate(parts)]
    stores = [pltpu.make_async_copy(held.at[rows], out.at[rows], sems.at[1, s]) for s, rows in enumerate(parts)]
    for load in loads:
        load.start()
    for s in range(N_Z):
        loads[s].wait()
        for k, piece in zip((0, *LAST_ORDER), pieces):
            rows = rows_at(s * N_Y + (y ^ k))
            kept = piece[s].astype(F32)
            held[rows, :] = kept
            direction[rows, :] = (kept * held_spread[rows, :]).astype(BF16)
        stores[s].start()
    for store in stores:
        store.wait()


def momentum_of(pieces, spread):
    held = pltpu.VMEM((BLOCKS, QB), F32)
    return call(
        momentum_kernel,
        (),
        (*pieces, spread),
        on_chip(N_Y) + anywhere(1),
        anywhere(1) + on_chip(1),
        (like((BLOCKS, QB), F32), like((BLOCKS, QB), BF16)),
        scratch=[held, held, pltpu.SemaphoreType.DMA((2, N_Z))],
    )


def step_kernel(offsets, totals, direction, dense, out, held, sems):
    total = jnp.sum(totals[...], axis=0)
    lane = lax.broadcasted_iota(jnp.int32, (1, QB), 1) // (QB // SEGS)
    inverse = []
    for k in range(SEGS):
        end = offsets[k + 1] if k + 1 < SEGS else BUCKET
        entries = (end - offsets[k]).astype(F32) * N_TENSOR
        squares = jnp.sum(jnp.where(lane == k, total, 0.0), axis=1, keepdims=True)
        inverse.append(1.0 / jnp.maximum(1.0, jnp.sqrt(squares / entries + 1e-06) / CLIP_RMS))
    count = STEP_ROWS
    copies = []
    for part in range(BLOCKS // count):
        rows = pl.ds(part * count, count)
        factor = jnp.broadcast_to(inverse[0], (count, QB))
        for seg, mask in enumerate(row_masks(offsets, part * count, count)):
            factor = jnp.where(mask, inverse[seg + 1], factor)
        held[rows, :] = direction[rows, :].astype(F32) * factor + DECAY * dense[rows, :].astype(F32)
        copies.append(pltpu.make_async_copy(held.at[rows], out.at[rows], sems.at[part]))
        copies[-1].start()
    for copy in copies:
        copy.wait()


def step_of(offsets, totals, direction, dense):
    (out,) = call(
        step_kernel,
        (offsets,),
        (totals, direction, dense),
        on_chip(3),
        anywhere(1),
        [like((BLOCKS, QB), F32)],
        scratch=[pltpu.VMEM((BLOCKS, QB), F32), pltpu.SemaphoreType.DMA((BLOCKS // STEP_ROWS,))],
    )
    return out


def exchange(value, axis, mask):
    return lax.ppermute(value, axis, [(i, i ^ mask) for i in range(lax.axis_size(axis))])


def body(grad, worker_err, momentum, variance, params, server_err, offsets, step_count):
    steps = step_count[0].astype(F32)
    first = 1.0 - jnp.power(F32(BETA_ONE), steps)
    second = 1.0 - jnp.power(F32(BETA_TWO), steps)
    bias = jnp.stack([1.0 / first, 1.0 / second])

    to_y = prepare(grad, worker_err)
    pieces = [to_y[0]] + [exchange(to_y[k], "y", k) for k in ORDER]
    spread, column_spread, dense = stage(bias, variance, params)
    low, high = reduce_y(pieces, server_err, column_spread)
    low, high = add(low, exchange(low, "z", 1)), add(high, exchange(high, "z", 3))
    halves = (low, high, exchange(low, "z", 3), exchange(high, "z", 1))
    column, squares = server(offsets, halves, momentum, column_spread)
    columns = [column] + [exchange(column, "y", k) for k in LAST_ORDER]
    totals = lax.all_to_all(squares, ("y", "tensor"), split_axis=0, concat_axis=0, tiled=True)
    momentum_new, direction = momentum_of(columns, spread)
    param_step = step_of(offsets, totals, direction, dense)
    return (momentum_new.reshape(1, BUCKET), param_step.reshape(1, BUCKET))


def solution(mesh):
    split = Mesh(mesh.devices.reshape(N_Z, N_Y, N_TENSOR), ("z", "y", "tensor"))
    dp = ("z", "y")
    placed = (
        P(dp, "tensor", None),
        P(dp, "tensor", None),
        P("tensor", None),
        P("tensor", None),
        P("tensor", None),
        P("tensor", dp),
        P(),
        P(),
    )
    return jax.shard_map(
        body,
        mesh=split,
        in_specs=placed,
        out_specs=(P("tensor", None), P("tensor", None)),
        check_vma=False,
    )
```

time: 170 us -> 71 us (0.42)
  blocking collectives: 64.8 us -> 0 us
  other arithmetic: 32 us -> 0.08 us
  waiting for transfers between devices: 40.1 us -> 16.9 us
  starting transfers between devices: 15.5 us -> 33.8 us
  between operations: 15 us -> 1.54 us
  Pallas kernels: 0 us -> 12.9 us
  local copies, waits for them, and re-layouts: 1.92 us -> 5.39 us
    all_gather x1 -> x0, blocking collectives: 36.1 us -> none  [body(): lax.all_gather(server_scales, 'dp', axis=0, tiled=True)]
    psum x1 -> x0, blocking collectives: 28.7 us -> none  [body(): totals = lax.psum(partial_value, 'tensor')]
    all_to_all x2 -> x1, waiting for transfers between devices: 29 us -> 2.83 us  [body(): lax.all_to_all(squares, ('y', 'tensor'), split_axis=0, concat_axis=0, til...]
    ppermute x0 -> x10, starting transfers between devices: none -> 23.4 us  [exchange(): lax.ppermute(value, axis, [(i, i ^ mask) for i in range(lax.axis_size(axi...]
    ppermute x0 -> x10, waiting for transfers between devices: none -> 14.1 us  [exchange(): lax.ppermute(value, axis, [(i, i ^ mask) for i in range(lax.axis_size(axi...]
    pallas_call x0 -> x8, Pallas kernels: none -> 12.9 us  [call(): pl.pallas_call(kernel, in_specs=[pl.BlockSpec(memory_space=pltpu.SMEM)] *...]
    all_gather x1 -> x0, waiting for transfers between devices: 11 us -> none  [body(): lax.all_gather(server_levels, 'dp', axis=0, tiled=True)]
    convert_element_type x7 -> x0, other arithmetic: 6.9 us -> none  [the longest x2 4.09 us: encode(): (values / scales.astype(jnp.float32)[..., None]).astype(jnp.bfloat16)]
  transfers between devices with their start and end apart: 3 -> 11, of which waited for: 3 -> 7; matrix products, arithmetic and copies ran while one was open for 6% -> 0% of each run, Pallas kernels for 0% -> 6%
where the time goes in v2:
time: 71 us; the launch traced here: 70.7 us
  starting transfers between devices  33.8 us (48%)
  waiting for transfers between devices  16.9 us (24%)
  Pallas kernels  12.9 us (18%)
  local copies, waits for them, and re-layouts  5.39 us (8%)
  between operations  1.54 us (2%)
    ppermute x10, starting transfers between devices, exchange(): lax.ppermute(value, axis, [(i, i ^ mask) for i in range(lax.axis_size(axi...  23.4 us
    ppermute x10, waiting for transfers between devices, exchange(): lax.ppermute(value, axis, [(i, i ^ mask) for i in range(lax.axis_size(axi...  14.1 us
    pallas_call x8, Pallas kernels, call(): pl.pallas_call(kernel, in_specs=[pl.BlockSpec(memory_space=pltpu.SMEM)] *...  12.9 us
    all_to_all x1, starting transfers between devices, body(): lax.all_to_all(squares, ('y', 'tensor'), split_axis=0, concat_axis=0, til...  10.4 us
    unnamed x16, local copies, waits for them, and re-layouts  5.39 us
    all_to_all x1, waiting for transfers between devices, body(): lax.all_to_all(squares, ('y', 'tensor'), split_axis=0, concat_axis=0, til...  2.83 us
  transfers between devices with their start and end apart: 11, of which 7 were waited for; matrix products, arithmetic and copies ran while one was open for 0% of the time, Pallas kernels for 6%

profile of v2, /device:TPU:1, one launch (start us, length us, event | category | flops | bytes accessed | tf_op | source)
XLA Modules:
  0.0 70.7 jit_solution(15178536779880059885)
XLA Ops:
  0.6 3.2 %shard_map.95 = (bf16[4,256,128]{2,1,0:T(8,128)(2,1)}, bf16[4,256,128]{2,1,0:T(8,128)(2,1)}, bf16[4,256,128]{2,1,0:T(8,128)(2,1)}, bf16[4,256,128]{2,1,0:T(8,128)(2,1)}) custom-call(bf16[1,1,524288]{2,1,0:T(2,128)(2,1)} %grad.1, bf16[1,1,524288]{2,1,0:T(2,128)(2,1)} %err.1), custom_call_target="tpu_custom_call" | custom-call | tf_op jit(solution)/shard_map/pallas_call | solution.py:51
  3.9 3.8 %collective-permute-start = (bf16[4,256,128]{2,1,0:T(8,128)(2,1)}, bf16[4,256,128]{2,1,0:T(8,128)(2,1)S(1)}, u32[]{:S(2)}, u32[]{:S(2)}) collective-permute-start(bf16[4,256,128]{2,1,0:T(8,128)(2,1)} %get-tuple-element.16), channel_id=1, source_target_pairs={{0,32},{16,48},{32,0},{48,16},{1,33},{17,49},{33,1},{49,17},{2,34}... | collective-permute-start | bytes 786440 | tf_op jit(solution)/shard_map/ppermute | solution.py:290
  7.7 0.4 collective-permute-start.1
  9.4 1.6 %copy-done = f32[1,524288]{1,0:T(1,128)S(1)} copy-done((f32[1,524288]{1,0:T(1,128)S(1)}, f32[1,524288]{1,0:T(1,128)}, u32[]{:S(2)}) %copy-start) | copy-done | bytes 2097176
  11.0 1.6 %copy-done.1 = bf16[1,524288]{1,0:T(2,128)(2,1)S(1)} copy-done((bf16[1,524288]{1,0:T(2,128)(2,1)S(1)}, bf16[1,524288]{1,0:T(2,128)(2,1)}, u32[]{:S(2)}) %copy-start.1) | copy-done | bytes 1048600
  12.6 1.7 %shard_map.96 = (f32[4096,128]{1,0:T(8,128)S(1)}, f32[4,256,128]{2,1,0:T(8,128)S(1)}, bf16[4096,128]{1,0:T(8,128)(2,1)S(1)}) custom-call(f32[2]{0:T(128)S(1)} %pad_maximum_fusion.bias, f32[1,524288]{1,0:T(1,128)S(1)} %copy-done, bf16[1,524288]{1,0:T(2,128)(2,1)S(1)} %copy-done.1), custom_call_target="tpu_custom_call" | custom-call | tf_op jit(solution)/shard_map/pallas_call | solution.py:51
  14.3 5.4 %collective-permute-done.1.refs_2_ = bf16[4,256,128]{2,1,0:T(8,128)(2,1)S(1)} collective-permute-done((bf16[4,256,128]{2,1,0:T(8,128)(2,1)}, bf16[4,256,128]{2,1,0:T(8,128)(2,1)S(1)}, u32[]{:S(2)}, u32[]{:S(2)}) %collective-permute-start.1) | collective-permute-done | bytes 262176 | tf_op jit(solution)/shard_map/ppermute | solution.py:290
  20.0 3.6 %collective-permute-start.3 = (bf16[2,256,128]{2,1,0:T(8,128)(2,1)S(1)}, bf16[2,256,128]{2,1,0:T(8,128)(2,1)S(1)}, u32[]{:S(2)}, u32[]{:S(2)}) collective-permute-start(bf16[2,256,128]{2,1,0:T(8,128)(2,1)S(1)} %get-tuple-element.20.ours), channel_id=1, source_target_pairs={{0,64},{64,0},{128,192},{192,128},{1,65},{65,1},{129,193},{193,129... | collective-permute-start | bytes 393224 | tf_op jit(solution)/shard_map/ppermute | solution.py:290
  23.6 4.2 %collective-permute-start.4 = (bf16[2,256,128]{2,1,0:T(8,128)(2,1)S(1)}, bf16[2,256,128]{2,1,0:T(8,128)(2,1)S(1)}, u32[]{:S(2)}, u32[]{:S(2)}) collective-permute-start(bf16[2,256,128]{2,1,0:T(8,128)(2,1)S(1)} %get-tuple-element.21.ours), channel_id=1, source_target_pairs={{0,192},{64,128},{128,64},{192,0},{1,193},{65,129},{129,65},{193,1... | collective-permute-start | bytes 393224 | tf_op jit(solution)/shard_map/ppermute | solution.py:290
  27.8 1.5 %collective-permute-done.3.theirs = bf16[2,256,128]{2,1,0:T(8,128)(2,1)S(1)} collective-permute-done((bf16[2,256,128]{2,1,0:T(8,128)(2,1)S(1)}, bf16[2,256,128]{2,1,0:T(8,128)(2,1)S(1)}, u32[]{:S(2)}, u32[]{:S(2)}) %collective-permute-start.3) | collective-permute-done | bytes 131104 | tf_op jit(solution)/shard_map/ppermute | solution.py:290
  29.4 4.1 %collective-permute-start.5 = (bf16[2,256,128]{2,1,0:T(8,128)(2,1)S(1)}, bf16[2,256,128]{2,1,0:T(8,128)(2,1)S(1)}, u32[]{:S(2)}, u32[]{:S(2)}) collective-permute-start(bf16[2,256,128]{2,1,0:T(8,128)(2,1)S(1)} %shard_map.98.low), channel_id=1, source_target_pairs={{0,192},{64,128},{128,64},{192,0},{1,193},{65,129},{129,65},{193,1... | collective-permute-start | bytes 393224 | tf_op jit(solution)/shard_map/ppermute | solution.py:290
  33.5 3.2 %collective-permute-start.6 = (bf16[2,256,128]{2,1,0:T(8,128)(2,1)S(1)}, bf16[2,256,128]{2,1,0:T(8,128)(2,1)S(1)}, u32[]{:S(2)}, u32[]{:S(2)}) collective-permute-start(bf16[2,256,128]{2,1,0:T(8,128)(2,1)S(1)} %shard_map.99.high), channel_id=1, source_target_pairs={{0,64},{64,0},{128,192},{192,128},{1,65},{65,1},{129,193},{193,129... | collective-permute-start | bytes 393224 | tf_op jit(solution)/shard_map/ppermute | solution.py:290
  36.7 5.8 %collective-permute-done.6.other_high = bf16[2,256,128]{2,1,0:T(8,128)(2,1)S(1)} collective-permute-done((bf16[2,256,128]{2,1,0:T(8,128)(2,1)S(1)}, bf16[2,256,128]{2,1,0:T(8,128)(2,1)S(1)}, u32[]{:S(2)}, u32[]{:S(2)}) %collective-permute-start.6) | collective-permute-done | bytes 131104 | tf_op jit(solution)/shard_map/ppermute | solution.py:290
  42.4 2.0 %shard_map.100 = (bf16[4,256,128]{2,1,0:T(8,128)(2,1)S(1)}, f32[64,1,128]{2,1,0:T(1,128)}) custom-call(s32[4]{0:T(128)S(1)} %copy-done.7, bf16[2,256,128]{2,1,0:T(8,128)(2,1)S(1)} %shard_map.98.low, bf16[2,256,128]{2,1,0:T(8,128)(2,1)S(1)} %shard_map.99.high, bf16[2,256,128]{2,1,0:T(8,128)(2,1)S(1)} %collective-permute-done.5.other_low, ...), custom_call_target="tpu_custom_call" | custom-call | tf_op jit(solution)/shard_map/pallas_call | solution.py:51
  44.4 2.9 %collective-permute-start.9 = (bf16[4,256,128]{2,1,0:T(8,128)(2,1)S(1)}, bf16[4,256,128]{2,1,0:T(8,128)(2,1)}, u32[]{:S(2)}, u32[]{:S(2)}) collective-permute-start(bf16[4,256,128]{2,1,0:T(8,128)(2,1)S(1)} %get-tuple-element.22.refs_0_), channel_id=1, source_target_pairs={{0,32},{16,48},{32,0},{48,16},{1,33},{17,49},{33,1},{49,17},{2,34}... | collective-permute-start | bytes 786440 | tf_op jit(solution)/shard_map/ppermute | solution.py:290
  47.4 0.4 collective-permute-start.8
  48.2 10.4 %all-to-all-start = ((f32[64,1,128]{2,1,0:T(1,128)}), f32[64,1,128]{2,1,0:T(1,128)S(1)}, u32[]{:S(2)}, u32[]{:S(2)}) async-start(f32[64,1,128]{2,1,0:T(1,128)} %get-tuple-element.25), calls=%async_computation | async-start | bytes 65536 | tf_op jit(solution)/shard_map/all_to_all | solution.py:307
  58.6 0.8 %collective-permute-done.8.refs_2_ = bf16[4,256,128]{2,1,0:T(8,128)(2,1)} collective-permute-done((bf16[4,256,128]{2,1,0:T(8,128)(2,1)S(1)}, bf16[4,256,128]{2,1,0:T(8,128)(2,1)}, u32[]{:S(2)}, u32[]{:S(2)}) %collective-permute-start.8) | collective-permute-done | bytes 262176 | tf_op jit(solution)/shard_map/ppermute | solution.py:290
  59.5 0.4 collective-permute-done.7.refs_1_
  59.9 2.7 %shard_map.101 = (f32[4096,128]{1,0:T(8,128)}, bf16[4096,128]{1,0:T(8,128)(2,1)S(1)}) custom-call(bf16[4,256,128]{2,1,0:T(8,128)(2,1)S(1)} %get-tuple-element.22.refs_0_, bf16[4,256,128]{2,1,0:T(8,128)(2,1)} %collective-permute-done.7.refs_1_, bf16[4,256,128]{2,1,0:T(8,128)(2,1)} %collective-permute-done.8.refs_2_, ...), custom_call_target="tpu_custom_call" | custom-call | tf_op jit(solution)/shard_map/pallas_call | solution.py:51
  62.6 1.0 %copy-done.3 = bf16[4096,128]{1,0:T(8,128)(2,1)} copy-done((bf16[4096,128]{1,0:T(8,128)(2,1)}, bf16[4096,128]{1,0:T(8,128)(2,1)S(1)}, u32[]{:S(2)}) %copy-start.3) | copy-done | bytes 1048600
  63.6 2.8 %all-to-all-done.totals = f32[64,1,128]{2,1,0:T(1,128)S(1)} async-done(((f32[64,1,128]{2,1,0:T(1,128)}), f32[64,1,128]{2,1,0:T(1,128)S(1)}, u32[]{:S(2)}, u32[]{:S(2)}) %all-to-all-start) | async-done | bytes 32800 | tf_op jit(solution)/shard_map/all_to_all | solution.py:307
  66.4 1.2 %copy-done.4 = bf16[4096,128]{1,0:T(8,128)(2,1)S(1)} copy-done((bf16[4096,128]{1,0:T(8,128)(2,1)S(1)}, bf16[4096,128]{1,0:T(8,128)(2,1)}, u32[]{:S(2)}) %copy-start.4) | copy-done | bytes 1048600
  67.6 3.1 %shard_map.102 = f32[4096,128]{1,0:T(8,128)} custom-call(s32[4]{0:T(128)S(1)} %copy-done.7, f32[64,1,128]{2,1,0:T(1,128)S(1)} %all-to-all-done.totals, bf16[4096,128]{1,0:T(8,128)(2,1)S(1)} %copy-done.4, bf16[4096,128]{1,0:T(8,128)(2,1)S(1)} %get-tuple-element.27.dense), custom_call_target="tpu_custom_call" | custom-call | tf_op jit(solution)/shard_map/pallas_call | solution.py:51
  (23 shorter events, 1.2 us)
Async XLA Ops:
  3.9 10.4 %collective-permute-start = (bf16[4,256,128]{2,1,0:T(8,128)(2,1)}, bf16[4,256,128]{2,1,0:T(8,128)(2,1)S(1)}, u32[]{:S(2)}, u32[]{:S(2)}) collective-permute-start(bf16[4,256,128]{2,1,0:T(8,128)(2,1)} %get-tuple-element.16), channel_id=1, source_target_pairs={{0,32},{16,48},{32,0},{48,16},{1,33},{17,49},{33,1},{49,17},{2,34}... | collective-permute-start | bytes 786440 | tf_op jit(solution)/shard_map/ppermute | solution.py:290
  7.7 12.0 %collective-permute-start.1 = (bf16[4,256,128]{2,1,0:T(8,128)(2,1)}, bf16[4,256,128]{2,1,0:T(8,128)(2,1)S(1)}, u32[]{:S(2)}, u32[]{:S(2)}) collective-permute-start(bf16[4,256,128]{2,1,0:T(8,128)(2,1)} %get-tuple-element.17), channel_id=1, source_target_pairs={{0,16},{16,0},{32,48},{48,32},{1,17},{17,1},{33,49},{49,33},{2,18}... | collective-permute-start | bytes 786440 | tf_op jit(solution)/shard_map/ppermute | solution.py:290
  8.1 11.7 %collective-permute-start.2 = (bf16[4,256,128]{2,1,0:T(8,128)(2,1)}, bf16[4,256,128]{2,1,0:T(8,128)(2,1)S(1)}, u32[]{:S(2)}, u32[]{:S(2)}) collective-permute-start(bf16[4,256,128]{2,1,0:T(8,128)(2,1)} %get-tuple-element.18), channel_id=1, source_target_pairs={{0,48},{16,32},{32,16},{48,0},{1,49},{17,33},{33,17},{49,1},{2,50}... | collective-permute-start | bytes 786440 | tf_op jit(solution)/shard_map/ppermute | solution.py:290
  9.4 1.6 %copy-start = (f32[1,524288]{1,0:T(1,128)S(1)}, f32[1,524288]{1,0:T(1,128)}, u32[]{:S(2)}) copy-start(f32[1,524288]{1,0:T(1,128)} %variance.1) | copy-start | bytes 6291460
  11.0 1.6 %copy-start.1 = (bf16[1,524288]{1,0:T(2,128)(2,1)S(1)}, bf16[1,524288]{1,0:T(2,128)(2,1)}, u32[]{:S(2)}) copy-start(bf16[1,524288]{1,0:T(2,128)(2,1)} %weights.1) | copy-start | bytes 3145732
  12.6 7.2 %copy-start.5 = (bf16[4,256,128]{2,1,0:T(8,128)(2,1)S(1)}, bf16[4,256,128]{2,1,0:T(8,128)(2,1)}, u32[]{:S(2)}) copy-start(bf16[4,256,128]{2,1,0:T(8,128)(2,1)} %get-tuple-element.15.refs_0_) | copy-start | bytes 786436
  12.6 7.2 %copy-start.6 = (f32[1,32768]{1,0:T(1,128)S(1)}, f32[1,32768]{1,0:T(1,128)}, u32[]{:S(2)}) copy-start(f32[1,32768]{1,0:T(1,128)} %refs_4_.1) | copy-start | bytes 393220
  14.2 28.2 %copy-start.2 = (f32[1,524288]{1,0:T(1,128)S(1)}, f32[1,524288]{1,0:T(1,128)}, u32[]{:S(2)}) copy-start(f32[1,524288]{1,0:T(1,128)} %momentum.1) | copy-start | bytes 6291460
  14.2 28.2 %copy-start.7 = (s32[4]{0:T(128)S(1)}, s32[4]{0:T(128)}, u32[]{:S(2)}) copy-start(s32[4]{0:T(128)} %offsets.3) | copy-start | bytes 52
  20.0 9.4 %collective-permute-start.3 = (bf16[2,256,128]{2,1,0:T(8,128)(2,1)S(1)}, bf16[2,256,128]{2,1,0:T(8,128)(2,1)S(1)}, u32[]{:S(2)}, u32[]{:S(2)}) collective-permute-start(bf16[2,256,128]{2,1,0:T(8,128)(2,1)S(1)} %get-tuple-element.20.ours), channel_id=1, source_target_pairs={{0,64},{64,0},{128,192},{192,128},{1,65},{65,1},{129,193},{193,129... | collective-permute-start | bytes 393224 | tf_op jit(solution)/shard_map/ppermute | solution.py:290
  23.6 9.9 %collective-permute-start.4 = (bf16[2,256,128]{2,1,0:T(8,128)(2,1)S(1)}, bf16[2,256,128]{2,1,0:T(8,128)(2,1)S(1)}, u32[]{:S(2)}, u32[]{:S(2)}) collective-permute-start(bf16[2,256,128]{2,1,0:T(8,128)(2,1)S(1)} %get-tuple-element.21.ours), channel_id=1, source_target_pairs={{0,192},{64,128},{128,64},{192,0},{1,193},{65,129},{129,65},{193,1... | collective-permute-start | bytes 393224 | tf_op jit(solution)/shard_map/ppermute | solution.py:290
  29.4 7.3 %collective-permute-start.5 = (bf16[2,256,128]{2,1,0:T(8,128)(2,1)S(1)}, bf16[2,256,128]{2,1,0:T(8,128)(2,1)S(1)}, u32[]{:S(2)}, u32[]{:S(2)}) collective-permute-start(bf16[2,256,128]{2,1,0:T(8,128)(2,1)S(1)} %shard_map.98.low), channel_id=1, source_target_pairs={{0,192},{64,128},{128,64},{192,0},{1,193},{65,129},{129,65},{193,1... | collective-permute-start | bytes 393224 | tf_op jit(solution)/shard_map/ppermute | solution.py:290
  33.5 8.9 %collective-permute-start.6 = (bf16[2,256,128]{2,1,0:T(8,128)(2,1)S(1)}, bf16[2,256,128]{2,1,0:T(8,128)(2,1)S(1)}, u32[]{:S(2)}, u32[]{:S(2)}) collective-permute-start(bf16[2,256,128]{2,1,0:T(8,128)(2,1)S(1)} %shard_map.99.high), channel_id=1, source_target_pairs={{0,64},{64,0},{128,192},{192,128},{1,65},{65,1},{129,193},{193,129... | collective-permute-start | bytes 393224 | tf_op jit(solution)/shard_map/ppermute | solution.py:290
  44.4 14.2 %collective-permute-start.9 = (bf16[4,256,128]{2,1,0:T(8,128)(2,1)S(1)}, bf16[4,256,128]{2,1,0:T(8,128)(2,1)}, u32[]{:S(2)}, u32[]{:S(2)}) collective-permute-start(bf16[4,256,128]{2,1,0:T(8,128)(2,1)S(1)} %get-tuple-element.22.refs_0_), channel_id=1, source_target_pairs={{0,32},{16,48},{32,0},{48,16},{1,33},{17,49},{33,1},{49,17},{2,34}... | collective-permute-start | bytes 786440 | tf_op jit(solution)/shard_map/ppermute | solution.py:290
  47.4 12.1 %collective-permute-start.8 = (bf16[4,256,128]{2,1,0:T(8,128)(2,1)S(1)}, bf16[4,256,128]{2,1,0:T(8,128)(2,1)}, u32[]{:S(2)}, u32[]{:S(2)}) collective-permute-start(bf16[4,256,128]{2,1,0:T(8,128)(2,1)S(1)} %get-tuple-element.22.refs_0_), channel_id=1, source_target_pairs={{0,16},{16,0},{32,48},{48,32},{1,17},{17,1},{33,49},{49,33},{2,18}... | collective-permute-start | bytes 786440 | tf_op jit(solution)/shard_map/ppermute | solution.py:290
  47.8 12.1 %collective-permute-start.7 = (bf16[4,256,128]{2,1,0:T(8,128)(2,1)S(1)}, bf16[4,256,128]{2,1,0:T(8,128)(2,1)}, u32[]{:S(2)}, u32[]{:S(2)}) collective-permute-start(bf16[4,256,128]{2,1,0:T(8,128)(2,1)S(1)} %get-tuple-element.22.refs_0_), channel_id=1, source_target_pairs={{0,48},{16,32},{32,16},{48,0},{1,49},{17,33},{33,17},{49,1},{2,50}... | collective-permute-start | bytes 786440 | tf_op jit(solution)/shard_map/ppermute | solution.py:290
  48.2 18.2 %all-to-all-start = ((f32[64,1,128]{2,1,0:T(1,128)}), f32[64,1,128]{2,1,0:T(1,128)S(1)}, u32[]{:S(2)}, u32[]{:S(2)}) async-start(f32[64,1,128]{2,1,0:T(1,128)} %get-tuple-element.25), calls=%async_computation | async-start | bytes 65536 | tf_op jit(solution)/shard_map/all_to_all | solution.py:307
  62.6 1.0 %copy-start.3 = (bf16[4096,128]{1,0:T(8,128)(2,1)}, bf16[4096,128]{1,0:T(8,128)(2,1)S(1)}, u32[]{:S(2)}) copy-start(bf16[4096,128]{1,0:T(8,128)(2,1)S(1)} %get-tuple-element.26.direction) | copy-start | bytes 3145732
  66.4 1.2 %copy-start.4 = (bf16[4096,128]{1,0:T(8,128)(2,1)S(1)}, bf16[4096,128]{1,0:T(8,128)(2,1)}, u32[]{:S(2)}) copy-start(bf16[4096,128]{1,0:T(8,128)(2,1)} %copy-done.3) | copy-start | bytes 3145732

commit v3 on v2

--- a/solution.py
+++ b/solution.py
@@ -1,3 +1,5 @@
+import functools
+
 import jax
 import jax.numpy as jnp
 from jax import lax
@@ -22,6 +24,7 @@
 ROWS = SHARE // QB
 BLOCKS = BUCKET // QB
 HALF = N_Z // 2
+HALF_SHAPE = (HALF, ROWS, QB)
 F32 = jnp.float32
 BF16 = jnp.bfloat16
 MIB = 1024 * 1024
@@ -47,13 +50,14 @@
     return values.reshape(values.shape[-1] // QB, QB)
 
 
-def call(kernel, scalars, arrays, in_specs, out_specs, out_shape, scratch=(), limit=16):
+def call(kernel, scalars, arrays, in_specs, out_specs, out_shape, scratch=(), limit=16, aliases=None):
     return pl.pallas_call(
         kernel,
         in_specs=[pl.BlockSpec(memory_space=pltpu.SMEM)] * len(scalars) + in_specs,
         out_specs=out_specs,
         out_shape=out_shape,
         scratch_shapes=scratch,
+        input_output_aliases=aliases or {},
         compiler_params=pltpu.CompilerParams(vmem_limit_bytes=limit * MIB),
     )(*scalars, *arrays)
 
@@ -74,22 +78,24 @@
     return pl.ds(pl.multiple_of(block * ROWS, ROWS), ROWS)
 
 
-def prepare_kernel(grad, err, *refs):
+def prepare_kernel(half, grad, err, *refs):
     outs, (held_grad, held_err, sems) = refs[:N_Y], refs[N_Y:]
     y = my_y()
+    width = N_Y * SHARE
     copies = []
-    for s in range(N_Z):
-        block = pl.ds(s * N_Y * SHARE, N_Y * SHARE)
+    for s in range(HALF):
+        here = pl.ds((half * HALF + s) * width, width)
+        there = pl.ds(s * width, width)
         copies.append(
             (
-                pltpu.make_async_copy(grad.at[:, :, block], held_grad.at[:, :, block], sems.at[0, s]),
-                pltpu.make_async_copy(err.at[:, :, block], held_err.at[:, :, block], sems.at[1, s]),
+                pltpu.make_async_copy(grad.at[:, :, here], held_grad.at[:, :, there], sems.at[0, s]),
+                pltpu.make_async_copy(err.at[:, :, here], held_err.at[:, :, there], sems.at[1, s]),
             )
         )
     for pair in copies:
         for copy in pair:
             copy.start()
-    for s in range(N_Z):
+    for s in range(HALF):
         for copy in copies[s]:
             copy.wait()
         for k in range(N_Y):
@@ -99,49 +105,58 @@
             outs[k][s] = rows_of((1.0 - BETA_ONE) * g + e).astype(BF16)
 
 
-def prepare(grad, err):
-    held = pltpu.VMEM((1, 1, BUCKET), BF16)
+def prepare(half, grad, err):
+    held = pltpu.VMEM((1, 1, BUCKET // 2), BF16)
     return call(
-        prepare_kernel,
+        functools.partial(prepare_kernel, half),
         (),
         (grad, err),
         anywhere(2),
         on_chip(N_Y),
-        (like((N_Z, ROWS, QB), BF16),) * N_Y,
-        scratch=[held, held, pltpu.SemaphoreType.DMA((2, N_Z))],
+        (like(HALF_SHAPE, BF16),) * N_Y,
+        scratch=[held, held, pltpu.SemaphoreType.DMA((2, HALF))],
         limit=PREPARE_LIMIT,
     )
 
 
-def reduce_y_kernel(*refs):
-    ins, server_err, outs = refs[:N_Y], refs[N_Y], refs[-2:]
+def reduce_y_kernel(half, *refs):
+    ins, server_err, out = refs[:N_Y], refs[N_Y], refs[-1]
     mine = rows_of(server_err[...])
     z = my_z()
-    for s in range(N_Z):
+    for s in range(HALF):
         total = ins[0][s].astype(F32)
         for ref in ins[1:]:
             total = total + ref[s].astype(F32)
-        total = total * (1.0 / N_DP) + jnp.where(z == s, mine, 0.0)
-        outs[s // HALF][s % HALF] = total.astype(BF16)
-
-
-def reduce_y(pieces, server_err, *staged):
-    return call(
-        reduce_y_kernel,
+        total = total * (1.0 / N_DP) + jnp.where(z == half * HALF + s, mine, 0.0)
+        out[s] = total.astype(BF16)
+
+
+def reduce_y(half, pieces, server_err, *staged):
+    (out,) = call(
+        functools.partial(reduce_y_kernel, half),
         (),
         (*pieces, server_err, *staged),
         on_chip(N_Y + 1) + anywhere(len(staged)),
-        on_chip(2),
-        (like((HALF, ROWS, QB), BF16),) * 2,
-    )
-
-
-def add_kernel(ours, theirs, out):
+        on_chip(1),
+        [like(HALF_SHAPE, BF16)],
+    )
+    return out
+
+
+def add_kernel(ours, theirs, *refs):
+    out = refs[-1]
     out[...] = (ours[...].astype(F32) + theirs[...].astype(F32)).astype(BF16)
 
 
-def add(ours, theirs):
-    (out,) = call(add_kernel, (), (ours, theirs), on_chip(2), on_chip(1), [like((HALF, ROWS, QB), BF16)])
+def add(ours, theirs, *staged):
+    (out,) = call(
+        add_kernel,
+        (),
+        (ours, theirs, *staged),
+        on_chip(2) + anywhere(len(staged)),
+        on_chip(1),
+        [like(HALF_SHAPE, BF16)],
+    )
     return out
 
 
@@ -188,65 +203,63 @@
     )
 
 
-def stage_kernel(bias, variance, weights, spread, column_spread, dense, held, sems):
-    copies = []
+def spread_kernel(bias, variance, spread, column_spread):
     for block in range(N_DP):
-        rows = pl.ds(block * ROWS, ROWS)
         root = jnp.sqrt(share_of(variance, block) * bias[1]) + ADAM_EPS
-        held[rows, :] = bias[0] / root
-        dense[rows, :] = share_of(weights, block).astype(BF16)
-        if block % N_Y == N_Y - 1:
-            rows = pl.ds((block + 1 - N_Y) * ROWS, N_Y * ROWS)
-            copies.append(pltpu.make_async_copy(held.at[rows], spread.at[rows], sems.at[block // N_Y]))
-            copies[-1].start()
+        spread[block * ROWS : (block + 1) * ROWS, :] = bias[0] / root
     for s in range(N_Z):
-        column_spread[s] = held[rows_at(s * N_Y + my_y()), :]
-    for copy in copies:
-        copy.wait()
-
-
-def stage(bias, variance, weights):
+        column_spread[s] = spread[rows_at(s * N_Y + my_y()), :]
+
+
+def spread_of(bias, variance):
     return call(
-        stage_kernel,
+        spread_kernel,
         (bias,),
-        (variance, weights),
+        (variance,),
+        on_chip(1),
         on_chip(2),
-        anywhere(1) + on_chip(2),
-        (like((BLOCKS, QB), F32), like((N_Z, ROWS, QB), F32), like((BLOCKS, QB), BF16)),
-        scratch=[pltpu.VMEM((BLOCKS, QB), F32), pltpu.SemaphoreType.DMA((N_Z,))],
-    )
+        (like((BLOCKS, QB), F32), like((N_Z, ROWS, QB), F32)),
+    )
+
+
+def dense_kernel(weights, out):
+    for block in range(N_DP):
+        out[block * ROWS : (block + 1) * ROWS, :] = share_of(weights, block).astype(BF16)
+
+
+def dense_of(weights):
+    (out,) = call(dense_kernel, (), (weights,), on_chip(1), on_chip(1), [like((BLOCKS, QB), BF16)])
+    return out
 
 
 def momentum_kernel(*refs):
-    pieces, (spread, out, direction, held, held_spread, sems) = refs[:N_Y], refs[N_Y:]
+    pieces, (spread, out, direction, held, sems) = refs[:N_Y], refs[N_Y:]
     y = my_y()
-    parts = [pl.ds(s * N_Y * ROWS, N_Y * ROWS) for s in range(N_Z)]
-    loads = [pltpu.make_async_copy(spread.at[rows], held_spread.at[rows], sems.at[0, s]) for s, rows in enumerate(parts)]
-    stores = [pltpu.make_async_copy(held.at[rows], out.at[rows], sems.at[1, s]) for s, rows in enumerate(parts)]
-    for load in loads:
-        load.start()
+    stores = []
     for s in range(N_Z):
-        loads[s].wait()
         for k, piece in zip((0, *LAST_ORDER), pieces):
             rows = rows_at(s * N_Y + (y ^ k))
             kept = piece[s].astype(F32)
             held[rows, :] = kept
-            direction[rows, :] = (kept * held_spread[rows, :]).astype(BF16)
-        stores[s].start()
+            direction[rows, :] = kept * spread[rows, :]
+        rows = pl.ds(s * N_Y * ROWS, N_Y * ROWS)
+        stores.append(pltpu.make_async_copy(held.at[rows], out.at[rows], sems.at[s]))
+        stores[-1].start()
     for store in stores:
         store.wait()
 
 
 def momentum_of(pieces, spread):
-    held = pltpu.VMEM((BLOCKS, QB), F32)
+    out = like((BLOCKS, QB), F32)
     return call(
         momentum_kernel,
         (),
         (*pieces, spread),
-        on_chip(N_Y) + anywhere(1),
+        on_chip(N_Y + 1),
         anywhere(1) + on_chip(1),
-        (like((BLOCKS, QB), F32), like((BLOCKS, QB), BF16)),
-        scratch=[held, held, pltpu.SemaphoreType.DMA((2, N_Z))],
+        (out, out),
+        scratch=[pltpu.VMEM((BLOCKS, QB), F32), pltpu.SemaphoreType.DMA((N_Z,))],
+        aliases={N_Y: 1},
     )
 
 
@@ -266,7 +279,7 @@
         factor = jnp.broadcast_to(inverse[0], (count, QB))
         for seg, mask in enumerate(row_masks(offsets, part * count, count)):
             factor = jnp.where(mask, inverse[seg + 1], factor)
-        held[rows, :] = direction[rows, :].astype(F32) * factor + DECAY * dense[rows, :].astype(F32)
+        held[rows, :] = direction[rows, :] * factor + DECAY * dense[rows, :].astype(F32)
         copies.append(pltpu.make_async_copy(held.at[rows], out.at[rows], sems.at[part]))
         copies[-1].start()
     for copy in copies:
@@ -290,18 +303,31 @@
     return lax.ppermute(value, axis, [(i, i ^ mask) for i in range(lax.axis_size(axis))])
 
 
+def exchange_z(value, even, odd):
+    pairs = [
+        (z * N_TENSOR + t, (z ^ (odd if t % 2 else even)) * N_TENSOR + t)
+        for z in range(N_Z)
+        for t in range(N_TENSOR)
+    ]
+    return lax.ppermute(value, ("z", "tensor"), pairs)
+
+
 def body(grad, worker_err, momentum, variance, params, server_err, offsets, step_count):
     steps = step_count[0].astype(F32)
     first = 1.0 - jnp.power(F32(BETA_ONE), steps)
     second = 1.0 - jnp.power(F32(BETA_TWO), steps)
     bias = jnp.stack([1.0 / first, 1.0 / second])
 
-    to_y = prepare(grad, worker_err)
-    pieces = [to_y[0]] + [exchange(to_y[k], "y", k) for k in ORDER]
-    spread, column_spread, dense = stage(bias, variance, params)
-    low, high = reduce_y(pieces, server_err, column_spread)
-    low, high = add(low, exchange(low, "z", 1)), add(high, exchange(high, "z", 3))
-    halves = (low, high, exchange(low, "z", 3), exchange(high, "z", 1))
+    spread, column_spread = spread_of(bias, variance)
+    dense = dense_of(params)
+    low_y, high_y = prepare(0, grad, worker_err), prepare(1, grad, worker_err)
+    low = [low_y[0]] + [exchange(low_y[k], "y", k) for k in ORDER]
+    high = [high_y[0]] + [exchange(high_y[k], "y", k) for k in ORDER]
+    low = reduce_y(0, low, server_err)
+    high = reduce_y(1, high, server_err, dense)
+    low = add(low, exchange_z(low, 1, 3))
+    high = add(high, exchange_z(high, 1, 3), column_spread)
+    halves = (low, high, exchange_z(low, 3, 1), exchange_z(high, 3, 1))
     column, squares = server(offsets, halves, momentum, column_spread)
     columns = [column] + [exchange(column, "y", k) for k in LAST_ORDER]
     totals = lax.all_to_all(squares, ("y", "tensor"), split_axis=0, concat_axis=0, tiled=True)

time: 71 us -> 65.2 us (0.918)
  local copies, waits for them, and re-layouts: 5.39 us -> 0.04 us
  waiting for transfers between devices: 16.9 us -> 14.4 us
  Pallas kernels: 12.9 us -> 14.4 us
    ppermute x10 -> x9, starting transfers between devices: 23.4 us -> 11.2 us  [exchange(): lax.ppermute(value, axis, [(i, i ^ mask) for i in range(lax.axis_size(axi...]
    ppermute x0 -> x4, starting transfers between devices: none -> 11.5 us  [exchange_z(): return lax.ppermute(value, ('z', 'tensor'), pairs)]
    ppermute x10 -> x9, waiting for transfers between devices: 14.1 us -> 2.79 us  [exchange(): lax.ppermute(value, axis, [(i, i ^ mask) for i in range(lax.axis_size(axi...]
    ppermute x0 -> x4, waiting for transfers between devices: none -> 6.45 us  [exchange_z(): return lax.ppermute(value, ('z', 'tensor'), pairs)]
    unnamed x16 -> x14, local copies, waits for them, and re-layouts: 5.39 us -> 0.04 us
    all_to_all x1, waiting for transfers between devices: 2.83 us -> 5.14 us  [body(): lax.all_to_all(squares, ('y', 'tensor'), split_axis=0, concat_axis=0, til...]
    pallas_call x8 -> x11, Pallas kernels: 12.9 us -> 14.4 us  [call(): pl.pallas_call(kernel, in_specs=[pl.BlockSpec(memory_space=pltpu.SMEM)] *...]
    all_to_all x1, starting transfers between devices: 10.4 us -> 11.8 us  [body(): lax.all_to_all(squares, ('y', 'tensor'), split_axis=0, concat_axis=0, til...]
  transfers between devices with their start and end apart: 11 -> 14, of which waited for: 7 -> 5; matrix products, arithmetic and copies ran while one was open for 0% -> 0% of each run, Pallas kernels for 6% -> 11%
where the time goes in v3:
time: 65.2 us; the launch traced here: 65 us
  starting transfers between devices  34.5 us (53%)
  Pallas kernels  14.4 us (22%)
  waiting for transfers between devices  14.4 us (22%)
  between operations  1.6 us (2%)
    pallas_call x11, Pallas kernels, call(): pl.pallas_call(kernel, in_specs=[pl.BlockSpec(memory_space=pltpu.SMEM)] *...  14.4 us
    all_to_all x1, starting transfers between devices, body(): lax.all_to_all(squares, ('y', 'tensor'), split_axis=0, concat_axis=0, til...  11.8 us
    ppermute x4, starting transfers between devices, exchange_z(): return lax.ppermute(value, ('z', 'tensor'), pairs)  11.5 us
    ppermute x9, starting transfers between devices, exchange(): lax.ppermute(value, axis, [(i, i ^ mask) for i in range(lax.axis_size(axi...  11.2 us
    ppermute x4, waiting for transfers between devices, exchange_z(): return lax.ppermute(value, ('z', 'tensor'), pairs)  6.45 us
    all_to_all x1, waiting for transfers between devices, body(): lax.all_to_all(squares, ('y', 'tensor'), split_axis=0, concat_axis=0, til...  5.14 us
    ppermute x9, waiting for transfers between devices, exchange(): lax.ppermute(value, axis, [(i, i ^ mask) for i in range(lax.axis_size(axi...  2.79 us
  transfers between devices with their start and end apart: 14, of which 5 were waited for; matrix products, arithmetic and copies ran while one was open for 0% of the time, Pallas kernels for 11%

profile of v3, /device:TPU:1, one launch (start us, length us, event | category | flops | bytes accessed | tf_op | source)
XLA Modules:
  0.0 65.0 jit_solution(415276367353492826)
XLA Ops:
  0.6 2.4 %shard_map.95 = (bf16[2,256,128]{2,1,0:T(8,128)(2,1)}, bf16[2,256,128]{2,1,0:T(8,128)(2,1)}, bf16[2,256,128]{2,1,0:T(8,128)(2,1)}, bf16[2,256,128]{2,1,0:T(8,128)(2,1)}) custom-call(bf16[1,1,524288]{2,1,0:T(2,128)(2,1)} %grad.3, bf16[1,1,524288]{2,1,0:T(2,128)(2,1)} %err.3), custom_call_target="tpu_custom_call" | custom-call | tf_op jit(solution)/shard_map/pallas_call | solution.py:54
  3.0 3.8 %collective-permute-start = (bf16[2,256,128]{2,1,0:T(8,128)(2,1)}, bf16[2,256,128]{2,1,0:T(8,128)(2,1)S(1)}, u32[]{:S(2)}, u32[]{:S(2)}) collective-permute-start(bf16[2,256,128]{2,1,0:T(8,128)(2,1)} %get-tuple-element.17), channel_id=1, source_target_pairs={{0,32},{16,48},{32,0},{48,16},{1,33},{17,49},{33,1},{49,17},{2,34}... | collective-permute-start | bytes 393224 | tf_op jit(solution)/shard_map/ppermute | solution.py:303
  6.9 0.4 collective-permute-start.1
  7.3 0.4 collective-permute-start.2
  7.6 2.6 %shard_map.98 = (bf16[2,256,128]{2,1,0:T(8,128)(2,1)}, bf16[2,256,128]{2,1,0:T(8,128)(2,1)}, bf16[2,256,128]{2,1,0:T(8,128)(2,1)}, bf16[2,256,128]{2,1,0:T(8,128)(2,1)}) custom-call(bf16[1,1,524288]{2,1,0:T(2,128)(2,1)} %grad.3, bf16[1,1,524288]{2,1,0:T(2,128)(2,1)} %err.3), custom_call_target="tpu_custom_call" | custom-call | tf_op jit(solution)/shard_map/pallas_call | solution.py:54
  10.3 2.4 %collective-permute-start.4 = (bf16[2,256,128]{2,1,0:T(8,128)(2,1)}, bf16[2,256,128]{2,1,0:T(8,128)(2,1)S(1)}, u32[]{:S(2)}, u32[]{:S(2)}) collective-permute-start(bf16[2,256,128]{2,1,0:T(8,128)(2,1)} %get-tuple-element.21), channel_id=1, source_target_pairs={{0,32},{16,48},{32,0},{48,16},{1,33},{17,49},{33,1},{49,17},{2,34}... | collective-permute-start | bytes 393224 | tf_op jit(solution)/shard_map/ppermute | solution.py:303
  12.6 0.4 collective-permute-start.5
  13.1 0.6 collective-permute-start.6
  13.8 2.6 %collective-permute-done.2.refs_3_ = bf16[2,256,128]{2,1,0:T(8,128)(2,1)S(1)} collective-permute-done((bf16[2,256,128]{2,1,0:T(8,128)(2,1)}, bf16[2,256,128]{2,1,0:T(8,128)(2,1)S(1)}, u32[]{:S(2)}, u32[]{:S(2)}) %collective-permute-start.2) | collective-permute-done | bytes 131104 | tf_op jit(solution)/shard_map/ppermute | solution.py:303
  16.5 3.5 %collective-permute-start.3 = (bf16[2,256,128]{2,1,0:T(8,128)(2,1)S(1)}, bf16[2,256,128]{2,1,0:T(8,128)(2,1)S(1)}, u32[]{:S(2)}, u32[]{:S(2)}) collective-permute-start(bf16[2,256,128]{2,1,0:T(8,128)(2,1)S(1)} %shard_map.96.ours), channel_id=1, source_target_pairs={{0,64},{1,193},{2,66},{3,195},{4,68},{5,197},{6,70},{7,199},{8,72}... | collective-permute-start | bytes 393224 | tf_op jit(solution)/shard_map/ppermute | solution.py:312
  20.3 5.3 %collective-permute-start.7 = (bf16[2,256,128]{2,1,0:T(8,128)(2,1)S(1)}, bf16[2,256,128]{2,1,0:T(8,128)(2,1)S(1)}, u32[]{:S(2)}, u32[]{:S(2)}) collective-permute-start(bf16[2,256,128]{2,1,0:T(8,128)(2,1)S(1)} %shard_map.100.ours), channel_id=1, source_target_pairs={{0,64},{1,193},{2,66},{3,195},{4,68},{5,197},{6,70},{7,199},{8,72}... | collective-permute-start | bytes 393224 | tf_op jit(solution)/shard_map/ppermute | solution.py:312
  26.5 1.4 %shard_map.101 = (f32[4096,128]{1,0:T(8,128)S(1)}, f32[4,256,128]{2,1,0:T(8,128)S(1)}) custom-call(f32[2]{0:T(128)S(1)} %pad_maximum_fusion.bias, f32[1,524288]{1,0:T(1,128)S(1)} %copy-done.1), custom_call_target="tpu_custom_call" | custom-call | tf_op jit(solution)/shard_map/pallas_call | solution.py:54
  28.0 1.3 %collective-permute-start.8 = (bf16[2,256,128]{2,1,0:T(8,128)(2,1)S(1)}, bf16[2,256,128]{2,1,0:T(8,128)(2,1)S(1)}, u32[]{:S(2)}, u32[]{:S(2)}) collective-permute-start(bf16[2,256,128]{2,1,0:T(8,128)(2,1)S(1)} %shard_map.97.low), channel_id=1, source_target_pairs={{0,192},{1,65},{2,194},{3,67},{4,196},{5,69},{6,198},{7,71},{8,200... | collective-permute-start | bytes 393224 | tf_op jit(solution)/shard_map/ppermute | solution.py:312
  29.3 1.4 %collective-permute-start.9 = (bf16[2,256,128]{2,1,0:T(8,128)(2,1)S(1)}, bf16[2,256,128]{2,1,0:T(8,128)(2,1)S(1)}, u32[]{:S(2)}, u32[]{:S(2)}) collective-permute-start(bf16[2,256,128]{2,1,0:T(8,128)(2,1)S(1)} %shard_map.102.high), channel_id=1, source_target_pairs={{0,192},{1,65},{2,194},{3,67},{4,196},{5,69},{6,198},{7,71},{8,200... | collective-permute-start | bytes 393224 | tf_op jit(solution)/shard_map/ppermute | solution.py:312
  30.7 4.1 %collective-permute-done.8.other_low = bf16[2,256,128]{2,1,0:T(8,128)(2,1)S(1)} collective-permute-done((bf16[2,256,128]{2,1,0:T(8,128)(2,1)S(1)}, bf16[2,256,128]{2,1,0:T(8,128)(2,1)S(1)}, u32[]{:S(2)}, u32[]{:S(2)}) %collective-permute-start.8) | collective-permute-done | bytes 131104 | tf_op jit(solution)/shard_map/ppermute | solution.py:312
  34.7 2.4 %collective-permute-done.9.other_high = bf16[2,256,128]{2,1,0:T(8,128)(2,1)S(1)} collective-permute-done((bf16[2,256,128]{2,1,0:T(8,128)(2,1)S(1)}, bf16[2,256,128]{2,1,0:T(8,128)(2,1)S(1)}, u32[]{:S(2)}, u32[]{:S(2)}) %collective-permute-start.9) | collective-permute-done | bytes 131104 | tf_op jit(solution)/shard_map/ppermute | solution.py:312
  37.1 2.0 %shard_map.103 = (bf16[4,256,128]{2,1,0:T(8,128)(2,1)S(1)}, f32[64,1,128]{2,1,0:T(1,128)}) custom-call(s32[4]{0:T(128)S(1)} %copy-done.6, bf16[2,256,128]{2,1,0:T(8,128)(2,1)S(1)} %shard_map.97.low, bf16[2,256,128]{2,1,0:T(8,128)(2,1)S(1)} %shard_map.102.high, bf16[2,256,128]{2,1,0:T(8,128)(2,1)S(1)} %collective-permute-done.8.other_low, ...), custom_call_target="tpu_custom_call" | custom-call | tf_op jit(solution)/shard_map/pallas_call | solution.py:54
  39.1 2.2 %collective-permute-start.12 = (bf16[4,256,128]{2,1,0:T(8,128)(2,1)S(1)}, bf16[4,256,128]{2,1,0:T(8,128)(2,1)}, u32[]{:S(2)}, u32[]{:S(2)}) collective-permute-start(bf16[4,256,128]{2,1,0:T(8,128)(2,1)S(1)} %get-tuple-element.25.refs_0_), channel_id=1, source_target_pairs={{0,32},{16,48},{32,0},{48,16},{1,33},{17,49},{33,1},{49,17},{2,34}... | collective-permute-start | bytes 786440 | tf_op jit(solution)/shard_map/ppermute | solution.py:303
  41.3 0.4 collective-permute-start.11
  41.7 0.7 %collective-permute-start.10 = (bf16[4,256,128]{2,1,0:T(8,128)(2,1)S(1)}, bf16[4,256,128]{2,1,0:T(8,128)(2,1)}, u32[]{:S(2)}, u32[]{:S(2)}) collective-permute-start(bf16[4,256,128]{2,1,0:T(8,128)(2,1)S(1)} %get-tuple-element.25.refs_0_), channel_id=1, source_target_pairs={{0,48},{16,32},{32,16},{48,0},{1,49},{17,33},{33,17},{49,1},{2,50}... | collective-permute-start | bytes 786440 | tf_op jit(solution)/shard_map/ppermute | solution.py:303
  42.4 11.8 %all-to-all-start = ((f32[64,1,128]{2,1,0:T(1,128)}), f32[64,1,128]{2,1,0:T(1,128)S(1)}, u32[]{:S(2)}, u32[]{:S(2)}) async-start(f32[64,1,128]{2,1,0:T(1,128)} %get-tuple-element.28), calls=%async_computation | async-start | bytes 65536 | tf_op jit(solution)/shard_map/all_to_all | solution.py:333
  54.2 2.5 %shard_map.104 = (f32[4096,128]{1,0:T(8,128)}, f32[4096,128]{1,0:T(8,128)S(1)}) custom-call(bf16[4,256,128]{2,1,0:T(8,128)(2,1)S(1)} %get-tuple-element.25.refs_0_, bf16[4,256,128]{2,1,0:T(8,128)(2,1)} %collective-permute-done.10.refs_1_, bf16[4,256,128]{2,1,0:T(8,128)(2,1)} %collective-permute-done.11.refs_2_, ...), custom_call_target="tpu_custom_call", output_to_operand_aliasing={{1}: (4, {})} | custom-call | tf_op jit(solution)/shard_map/pallas_call | solution.py:54
  56.8 5.1 %all-to-all-done.totals = f32[64,1,128]{2,1,0:T(1,128)S(1)} async-done(((f32[64,1,128]{2,1,0:T(1,128)}), f32[64,1,128]{2,1,0:T(1,128)S(1)}, u32[]{:S(2)}, u32[]{:S(2)}) %all-to-all-start) | async-done | bytes 32800 | tf_op jit(solution)/shard_map/all_to_all | solution.py:333
  61.9 3.1 %shard_map.105 = f32[4096,128]{1,0:T(8,128)} custom-call(s32[4]{0:T(128)S(1)} %copy-done.6, f32[64,1,128]{2,1,0:T(1,128)S(1)} %all-to-all-done.totals, f32[4096,128]{1,0:T(8,128)S(1)} %get-tuple-element.29.direction, bf16[4096,128]{1,0:T(8,128)(2,1)S(1)} %shard_map.99.refs_5_.dense), custom_call_target="tpu_custom_call" | custom-call | tf_op jit(solution)/shard_map/pallas_call | solution.py:54
  (30 shorter events, 0.7 us)
Async XLA Ops:
  3.0 10.0 %collective-permute-start = (bf16[2,256,128]{2,1,0:T(8,128)(2,1)}, bf16[2,256,128]{2,1,0:T(8,128)(2,1)S(1)}, u32[]{:S(2)}, u32[]{:S(2)}) collective-permute-start(bf16[2,256,128]{2,1,0:T(8,128)(2,1)} %get-tuple-element.17), channel_id=1, source_target_pairs={{0,32},{16,48},{32,0},{48,16},{1,33},{17,49},{33,1},{49,17},{2,34}... | collective-permute-start | bytes 393224 | tf_op jit(solution)/shard_map/ppermute | solution.py:303
  6.9 6.9 %collective-permute-start.1 = (bf16[2,256,128]{2,1,0:T(8,128)(2,1)}, bf16[2,256,128]{2,1,0:T(8,128)(2,1)S(1)}, u32[]{:S(2)}, u32[]{:S(2)}) collective-permute-start(bf16[2,256,128]{2,1,0:T(8,128)(2,1)} %get-tuple-element.18), channel_id=1, source_target_pairs={{0,16},{16,0},{32,48},{48,32},{1,17},{17,1},{33,49},{49,33},{2,18}... | collective-permute-start | bytes 393224 | tf_op jit(solution)/shard_map/ppermute | solution.py:303
  7.3 6.4 %copy-start = (bf16[1,524288]{1,0:T(2,128)(2,1)S(1)}, bf16[1,524288]{1,0:T(2,128)(2,1)}, u32[]{:S(2)}) copy-start(bf16[1,524288]{1,0:T(2,128)(2,1)} %weights.1) | copy-start | bytes 3145732
  7.3 9.1 %collective-permute-start.2 = (bf16[2,256,128]{2,1,0:T(8,128)(2,1)}, bf16[2,256,128]{2,1,0:T(8,128)(2,1)S(1)}, u32[]{:S(2)}, u32[]{:S(2)}) collective-permute-start(bf16[2,256,128]{2,1,0:T(8,128)(2,1)} %get-tuple-element.19), channel_id=1, source_target_pairs={{0,48},{16,32},{32,16},{48,0},{1,49},{17,33},{33,17},{49,1},{2,50}... | collective-permute-start | bytes 393224 | tf_op jit(solution)/shard_map/ppermute | solution.py:303
  10.2 6.2 %copy-start.3 = (f32[1,32768]{1,0:T(1,128)S(1)}, f32[1,32768]{1,0:T(1,128)}, u32[]{:S(2)}) copy-start(f32[1,32768]{1,0:T(1,128)} %refs_4_.3) | copy-start | bytes 393220
  10.3 6.2 %copy-start.5 = (bf16[2,256,128]{2,1,0:T(8,128)(2,1)S(1)}, bf16[2,256,128]{2,1,0:T(8,128)(2,1)}, u32[]{:S(2)}) copy-start(bf16[2,256,128]{2,1,0:T(8,128)(2,1)} %get-tuple-element.16.refs_0_) | copy-start | bytes 393220
  10.3 9.9 %copy-start.4 = (bf16[2,256,128]{2,1,0:T(8,128)(2,1)S(1)}, bf16[2,256,128]{2,1,0:T(8,128)(2,1)}, u32[]{:S(2)}) copy-start(bf16[2,256,128]{2,1,0:T(8,128)(2,1)} %get-tuple-element.20.refs_0_) | copy-start | bytes 393220
  10.3 9.8 %collective-permute-start.4 = (bf16[2,256,128]{2,1,0:T(8,128)(2,1)}, bf16[2,256,128]{2,1,0:T(8,128)(2,1)S(1)}, u32[]{:S(2)}, u32[]{:S(2)}) collective-permute-start(bf16[2,256,128]{2,1,0:T(8,128)(2,1)} %get-tuple-element.21), channel_id=1, source_target_pairs={{0,32},{16,48},{32,0},{48,16},{1,33},{17,49},{33,1},{49,17},{2,34}... | collective-permute-start | bytes 393224 | tf_op jit(solution)/shard_map/ppermute | solution.py:303
  12.6 7.4 %collective-permute-start.5 = (bf16[2,256,128]{2,1,0:T(8,128)(2,1)}, bf16[2,256,128]{2,1,0:T(8,128)(2,1)S(1)}, u32[]{:S(2)}, u32[]{:S(2)}) collective-permute-start(bf16[2,256,128]{2,1,0:T(8,128)(2,1)} %get-tuple-element.22), channel_id=1, source_target_pairs={{0,16},{16,0},{32,48},{48,32},{1,17},{17,1},{33,49},{49,33},{2,18}... | collective-permute-start | bytes 393224 | tf_op jit(solution)/shard_map/ppermute | solution.py:303
  13.1 7.1 %collective-permute-start.6 = (bf16[2,256,128]{2,1,0:T(8,128)(2,1)}, bf16[2,256,128]{2,1,0:T(8,128)(2,1)S(1)}, u32[]{:S(2)}, u32[]{:S(2)}) collective-permute-start(bf16[2,256,128]{2,1,0:T(8,128)(2,1)} %get-tuple-element.23), channel_id=1, source_target_pairs={{0,48},{16,32},{32,16},{48,0},{1,49},{17,33},{33,17},{49,1},{2,50}... | collective-permute-start | bytes 393224 | tf_op jit(solution)/shard_map/ppermute | solution.py:303
  13.8 12.7 %copy-start.1 = (f32[1,524288]{1,0:T(1,128)S(1)}, f32[1,524288]{1,0:T(1,128)}, u32[]{:S(2)}) copy-start(f32[1,524288]{1,0:T(1,128)} %variance.1) | copy-start | bytes 6291460
  16.5 11.4 %collective-permute-start.3 = (bf16[2,256,128]{2,1,0:T(8,128)(2,1)S(1)}, bf16[2,256,128]{2,1,0:T(8,128)(2,1)S(1)}, u32[]{:S(2)}, u32[]{:S(2)}) collective-permute-start(bf16[2,256,128]{2,1,0:T(8,128)(2,1)S(1)} %shard_map.96.ours), channel_id=1, source_target_pairs={{0,64},{1,193},{2,66},{3,195},{4,68},{5,197},{6,70},{7,199},{8,72}... | collective-permute-start | bytes 393224 | tf_op jit(solution)/shard_map/ppermute | solution.py:312
  20.3 16.8 %copy-start.2 = (f32[1,524288]{1,0:T(1,128)S(1)}, f32[1,524288]{1,0:T(1,128)}, u32[]{:S(2)}) copy-start(f32[1,524288]{1,0:T(1,128)} %momentum.1) | copy-start | bytes 6291460
  20.3 16.8 %copy-start.6 = (s32[4]{0:T(128)S(1)}, s32[4]{0:T(128)}, u32[]{:S(2)}) copy-start(s32[4]{0:T(128)} %offsets.3) | copy-start | bytes 52
  20.3 8.9 %collective-permute-start.7 = (bf16[2,256,128]{2,1,0:T(8,128)(2,1)S(1)}, bf16[2,256,128]{2,1,0:T(8,128)(2,1)S(1)}, u32[]{:S(2)}, u32[]{:S(2)}) collective-permute-start(bf16[2,256,128]{2,1,0:T(8,128)(2,1)S(1)} %shard_map.100.ours), channel_id=1, source_target_pairs={{0,64},{1,193},{2,66},{3,195},{4,68},{5,197},{6,70},{7,199},{8,72}... | collective-permute-start | bytes 393224 | tf_op jit(solution)/shard_map/ppermute | solution.py:312
  28.0 6.8 %collective-permute-start.8 = (bf16[2,256,128]{2,1,0:T(8,128)(2,1)S(1)}, bf16[2,256,128]{2,1,0:T(8,128)(2,1)S(1)}, u32[]{:S(2)}, u32[]{:S(2)}) collective-permute-start(bf16[2,256,128]{2,1,0:T(8,128)(2,1)S(1)} %shard_map.97.low), channel_id=1, source_target_pairs={{0,192},{1,65},{2,194},{3,67},{4,196},{5,69},{6,198},{7,71},{8,200... | collective-permute-start | bytes 393224 | tf_op jit(solution)/shard_map/ppermute | solution.py:312
  29.3 7.9 %collective-permute-start.9 = (bf16[2,256,128]{2,1,0:T(8,128)(2,1)S(1)}, bf16[2,256,128]{2,1,0:T(8,128)(2,1)S(1)}, u32[]{:S(2)}, u32[]{:S(2)}) collective-permute-start(bf16[2,256,128]{2,1,0:T(8,128)(2,1)S(1)} %shard_map.102.high), channel_id=1, source_target_pairs={{0,192},{1,65},{2,194},{3,67},{4,196},{5,69},{6,198},{7,71},{8,200... | collective-permute-start | bytes 393224 | tf_op jit(solution)/shard_map/ppermute | solution.py:312
  39.1 15.1 %collective-permute-start.12 = (bf16[4,256,128]{2,1,0:T(8,128)(2,1)S(1)}, bf16[4,256,128]{2,1,0:T(8,128)(2,1)}, u32[]{:S(2)}, u32[]{:S(2)}) collective-permute-start(bf16[4,256,128]{2,1,0:T(8,128)(2,1)S(1)} %get-tuple-element.25.refs_0_), channel_id=1, source_target_pairs={{0,32},{16,48},{32,0},{48,16},{1,33},{17,49},{33,1},{49,17},{2,34}... | collective-permute-start | bytes 786440 | tf_op jit(solution)/shard_map/ppermute | solution.py:303
  41.3 12.9 %collective-permute-start.11 = (bf16[4,256,128]{2,1,0:T(8,128)(2,1)S(1)}, bf16[4,256,128]{2,1,0:T(8,128)(2,1)}, u32[]{:S(2)}, u32[]{:S(2)}) collective-permute-start(bf16[4,256,128]{2,1,0:T(8,128)(2,1)S(1)} %get-tuple-element.25.refs_0_), channel_id=1, source_target_pairs={{0,16},{16,0},{32,48},{48,32},{1,17},{17,1},{33,49},{49,33},{2,18}... | collective-permute-start | bytes 786440 | tf_op jit(solution)/shard_map/ppermute | solution.py:303
  41.7 12.5 %collective-permute-start.10 = (bf16[4,256,128]{2,1,0:T(8,128)(2,1)S(1)}, bf16[4,256,128]{2,1,0:T(8,128)(2,1)}, u32[]{:S(2)}, u32[]{:S(2)}) collective-permute-start(bf16[4,256,128]{2,1,0:T(8,128)(2,1)S(1)} %get-tuple-element.25.refs_0_), channel_id=1, source_target_pairs={{0,48},{16,32},{32,16},{48,0},{1,49},{17,33},{33,17},{49,1},{2,50}... | collective-permute-start | bytes 786440 | tf_op jit(solution)/shard_map/ppermute | solution.py:303
  42.4 19.5 %all-to-all-start = ((f32[64,1,128]{2,1,0:T(1,128)}), f32[64,1,128]{2,1,0:T(1,128)S(1)}, u32[]{:S(2)}, u32[]{:S(2)}) async-start(f32[64,1,128]{2,1,0:T(1,128)} %get-tuple-element.28), calls=%async_computation | async-start | bytes 65536 | tf_op jit(solution)/shard_map/all_to_all | solution.py:333

commit v4 on v3

--- a/solution.py
+++ b/solution.py
@@ -28,8 +28,7 @@
 F32 = jnp.float32
 BF16 = jnp.bfloat16
 MIB = 1024 * 1024
-PREPARE_LIMIT = 60
-STEP_ROWS = 512
+PREPARE_LIMIT = 54
 ORDER = (2, 1, 3)
 LAST_ORDER = (3, 1, 2)
 
@@ -165,9 +164,15 @@
     return [entry >= offsets[k] for k in range(1, SEGS)]
 
 
-def server_kernel(offsets, low, high, other_low, other_high, momentum, spread, column, out):
+def has_boundary(offsets, first_row, rows):
+    inside = [(offsets[k] > first_row * QB) & (offsets[k] < (first_row + rows) * QB) for k in range(1, SEGS)]
+    return inside[0] | inside[1] | inside[2]
+
+
+def server_kernel(offsets, low, high, other_low, other_high, momentum, spread, column, out, sums):
     y = my_y()
-    seg = [jnp.zeros((1, QB), F32)] * SEGS
+    lane_row = lax.broadcasted_iota(jnp.int32, (8, QB), 0)
+    sums[...] = jnp.zeros((8, QB), F32)
     for s in range(N_Z):
         ours, theirs = (low, other_low) if s < HALF else (high, other_high)
         total = ours[s % HALF].astype(F32) + theirs[s % HALF].astype(F32)
@@ -176,19 +181,29 @@
         column[s] = sent
         direction = sent.astype(F32) * spread[s]
         squares = direction * direction
-        masks = row_masks(offsets, block * ROWS, ROWS)
-        for k in range(SEGS):
-            picked = squares
-            if k > 0:
-                picked = jnp.where(masks[k - 1], picked, 0.0)
-            if k < SEGS - 1:
-                picked = jnp.where(masks[k], 0.0, picked)
-            seg[k] = seg[k] + jnp.sum(picked, axis=0, keepdims=True)
-    sums = jnp.concatenate(seg + [jnp.zeros((8 - SEGS, QB), F32)], axis=0)
-    sums = sums + pltpu.roll(sums, QB // 2, 1)
-    sums = sums + pltpu.roll(sums, QB // 4, 1)
+        first = block * ROWS
+        mixed = has_boundary(offsets, first, ROWS)
+
+        @pl.when(jnp.logical_not(mixed))
+        def _(squares=squares, first=first):
+            tensor = sum((first * QB >= offsets[k]).astype(jnp.int32) for k in range(1, SEGS))
+            sums[...] += jnp.where(lane_row == tensor, jnp.sum(squares, axis=0, keepdims=True), 0.0)
+
+        @pl.when(mixed)
+        def _(squares=squares, first=first):
+            masks = row_masks(offsets, first, ROWS)
+            for k in range(SEGS):
+                picked = squares
+                if k > 0:
+                    picked = jnp.where(masks[k - 1], picked, 0.0)
+                if k < SEGS - 1:
+                    picked = jnp.where(masks[k], 0.0, picked)
+                sums[k : k + 1, :] += jnp.sum(picked, axis=0, keepdims=True)
+    folded = sums[...]
+    folded = folded + pltpu.roll(folded, QB // 2, 1)
+    folded = folded + pltpu.roll(folded, QB // 4, 1)
     lane = lax.broadcasted_iota(jnp.int32, (8, QB), 1) // (QB // SEGS)
-    mine = jnp.where(lane == lax.broadcasted_iota(jnp.int32, (8, QB), 0), sums, 0.0)
+    mine = jnp.where(lane == lane_row, folded, 0.0)
     out[...] = jnp.broadcast_to(jnp.sum(mine, axis=0, keepdims=True)[None], out.shape)
 
 
@@ -200,6 +215,7 @@
         on_chip(6),
         on_chip(2),
         (like((N_Z, ROWS, QB), BF16), like((N_Y * N_TENSOR, 1, QB), F32)),
+        scratch=[pltpu.VMEM((8, QB), F32)],
     )
 
 
@@ -272,14 +288,26 @@
         entries = (end - offsets[k]).astype(F32) * N_TENSOR
         squares = jnp.sum(jnp.where(lane == k, total, 0.0), axis=1, keepdims=True)
         inverse.append(1.0 / jnp.maximum(1.0, jnp.sqrt(squares / entries + 1e-06) / CLIP_RMS))
-    count = STEP_ROWS
     copies = []
-    for part in range(BLOCKS // count):
-        rows = pl.ds(part * count, count)
-        factor = jnp.broadcast_to(inverse[0], (count, QB))
-        for seg, mask in enumerate(row_masks(offsets, part * count, count)):
-            factor = jnp.where(mask, inverse[seg + 1], factor)
-        held[rows, :] = direction[rows, :] * factor + DECAY * dense[rows, :].astype(F32)
+    for part in range(BLOCKS // ROWS):
+        first = part * ROWS
+        rows = pl.ds(first, ROWS)
+        mixed = has_boundary(offsets, first, ROWS)
+
+        @pl.when(jnp.logical_not(mixed))
+        def _(rows=rows, first=first):
+            factor = inverse[0]
+            for k in range(1, SEGS):
+                factor = jnp.where(first * QB >= offsets[k], inverse[k], factor)
+            held[rows, :] = direction[rows, :] * factor + DECAY * dense[rows, :].astype(F32)
+
+        @pl.when(mixed)
+        def _(rows=rows, first=first):
+            factor = jnp.broadcast_to(inverse[0], (ROWS, QB))
+            for k, mask in enumerate(row_masks(offsets, first, ROWS)):
+                factor = jnp.where(mask, inverse[k + 1], factor)
+            held[rows, :] = direction[rows, :] * factor + DECAY * dense[rows, :].astype(F32)
+
         copies.append(pltpu.make_async_copy(held.at[rows], out.at[rows], sems.at[part]))
         copies[-1].start()
     for copy in copies:
@@ -294,7 +322,7 @@
         on_chip(3),
         anywhere(1),
         [like((BLOCKS, QB), F32)],
-        scratch=[pltpu.VMEM((BLOCKS, QB), F32), pltpu.SemaphoreType.DMA((BLOCKS // STEP_ROWS,))],
+        scratch=[pltpu.VMEM((BLOCKS, QB), F32), pltpu.SemaphoreType.DMA((BLOCKS // ROWS,))],
     )
     return out
 
@@ -326,8 +354,8 @@
     low = reduce_y(0, low, server_err)
     high = reduce_y(1, high, server_err, dense)
     low = add(low, exchange_z(low, 1, 3))
-    high = add(high, exchange_z(high, 1, 3), column_spread)
-    halves = (low, high, exchange_z(low, 3, 1), exchange_z(high, 3, 1))
+    high = add(high, exchange_z(high, 3, 1))
+    halves = (low, high, exchange_z(low, 3, 1), exchange_z(high, 1, 3))
     column, squares = server(offsets, halves, momentum, column_spread)
     columns = [column] + [exchange(column, "y", k) for k in LAST_ORDER]
     totals = lax.all_to_all(squares, ("y", "tensor"), split_axis=0, concat_axis=0, tiled=True)

time: 65.2 us -> 61.7 us (0.946)
  waiting for transfers between devices: 14.4 us -> 12.8 us
  Pallas kernels: 14.4 us -> 13.1 us
  starting transfers between devices: 34.5 us -> 33.8 us
    all_to_all x1, starting transfers between devices: 11.8 us -> 9.6 us  [body(): lax.all_to_all(squares, ('y', 'tensor'), split_axis=0, concat_axis=0, til...]
    ppermute x4, waiting for transfers between devices: 6.45 us -> 4.86 us  [exchange_z(): return lax.ppermute(value, ('z', 'tensor'), pairs)]
    ppermute x4, starting transfers between devices: 11.5 us -> 12.9 us  [exchange_z(): return lax.ppermute(value, ('z', 'tensor'), pairs)]
    pallas_call x11, Pallas kernels: 14.4 us -> 13.1 us  [call(): pl.pallas_call(kernel, in_specs=[pl.BlockSpec(memory_space=pltpu.SMEM)] *...]
    ppermute x9, waiting for transfers between devices: 2.79 us -> 3.52 us  [exchange(): lax.ppermute(value, axis, [(i, i ^ mask) for i in range(lax.axis_size(axi...]
    all_to_all x1, waiting for transfers between devices: 5.14 us -> 4.41 us  [body(): lax.all_to_all(squares, ('y', 'tensor'), split_axis=0, concat_axis=0, til...]
  transfers between devices with their start and end apart: 14 -> 14, of which waited for: 5 -> 7; matrix products, arithmetic and copies ran while one was open for 0% -> 0% of each run, Pallas kernels for 11% -> 11%
where the time goes in v4:
time: 61.7 us; the launch traced here: 61.4 us
  starting transfers between devices  33.8 us (55%)
  Pallas kernels  13.1 us (21%)
  waiting for transfers between devices  12.8 us (21%)
  between operations  1.58 us (3%)
    pallas_call x11, Pallas kernels, call(): pl.pallas_call(kernel, in_specs=[pl.BlockSpec(memory_space=pltpu.SMEM)] *...  13.1 us
    ppermute x4, starting transfers between devices, exchange_z(): return lax.ppermute(value, ('z', 'tensor'), pairs)  12.9 us
    ppermute x9, starting transfers between devices, exchange(): lax.ppermute(value, axis, [(i, i ^ mask) for i in range(lax.axis_size(axi...  11.4 us
    all_to_all x1, starting transfers between devices, body(): lax.all_to_all(squares, ('y', 'tensor'), split_axis=0, concat_axis=0, til...  9.6 us
    ppermute x4, waiting for transfers between devices, exchange_z(): return lax.ppermute(value, ('z', 'tensor'), pairs)  4.86 us
    all_to_all x1, waiting for transfers between devices, body(): lax.all_to_all(squares, ('y', 'tensor'), split_axis=0, concat_axis=0, til...  4.41 us
    ppermute x9, waiting for transfers between devices, exchange(): lax.ppermute(value, axis, [(i, i ^ mask) for i in range(lax.axis_size(axi...  3.52 us
  transfers between devices with their start and end apart: 14, of which 7 were waited for; matrix products, arithmetic and copies ran while one was open for 0% of the time, Pallas kernels for 11%

profile of v4, /device:TPU:1, one launch (start us, length us, event | category | flops | bytes accessed | tf_op | source)
XLA Modules:
  0.0 61.4 jit_solution(9982132966319147675)
XLA Ops:
  0.6 2.4 %shard_map.95 = (bf16[2,256,128]{2,1,0:T(8,128)(2,1)}, bf16[2,256,128]{2,1,0:T(8,128)(2,1)}, bf16[2,256,128]{2,1,0:T(8,128)(2,1)}, bf16[2,256,128]{2,1,0:T(8,128)(2,1)}) custom-call(bf16[1,1,524288]{2,1,0:T(2,128)(2,1)} %grad.3, bf16[1,1,524288]{2,1,0:T(2,128)(2,1)} %err.3), custom_call_target="tpu_custom_call" | custom-call | tf_op jit(solution)/shard_map/pallas_call | solution.py:53
  3.0 3.8 %collective-permute-start = (bf16[2,256,128]{2,1,0:T(8,128)(2,1)}, bf16[2,256,128]{2,1,0:T(8,128)(2,1)S(1)}, u32[]{:S(2)}, u32[]{:S(2)}) collective-permute-start(bf16[2,256,128]{2,1,0:T(8,128)(2,1)} %get-tuple-element.17), channel_id=1, source_target_pairs={{0,32},{16,48},{32,0},{48,16},{1,33},{17,49},{33,1},{49,17},{2,34}... | collective-permute-start | bytes 393224 | tf_op jit(solution)/shard_map/ppermute | solution.py:331
  6.9 0.4 collective-permute-start.1
  7.6 2.6 %shard_map.98 = (bf16[2,256,128]{2,1,0:T(8,128)(2,1)}, bf16[2,256,128]{2,1,0:T(8,128)(2,1)}, bf16[2,256,128]{2,1,0:T(8,128)(2,1)}, bf16[2,256,128]{2,1,0:T(8,128)(2,1)}) custom-call(bf16[1,1,524288]{2,1,0:T(2,128)(2,1)} %grad.3, bf16[1,1,524288]{2,1,0:T(2,128)(2,1)} %err.3), custom_call_target="tpu_custom_call" | custom-call | tf_op jit(solution)/shard_map/pallas_call | solution.py:53
  10.3 2.4 %collective-permute-start.4 = (bf16[2,256,128]{2,1,0:T(8,128)(2,1)}, bf16[2,256,128]{2,1,0:T(8,128)(2,1)S(1)}, u32[]{:S(2)}, u32[]{:S(2)}) collective-permute-start(bf16[2,256,128]{2,1,0:T(8,128)(2,1)} %get-tuple-element.21), channel_id=1, source_target_pairs={{0,32},{16,48},{32,0},{48,16},{1,33},{17,49},{33,1},{49,17},{2,34}... | collective-permute-start | bytes 393224 | tf_op jit(solution)/shard_map/ppermute | solution.py:331
  12.6 0.4 collective-permute-start.5
  13.1 0.6 collective-permute-start.6
  13.8 2.6 %collective-permute-done.2.refs_3_ = bf16[2,256,128]{2,1,0:T(8,128)(2,1)S(1)} collective-permute-done((bf16[2,256,128]{2,1,0:T(8,128)(2,1)}, bf16[2,256,128]{2,1,0:T(8,128)(2,1)S(1)}, u32[]{:S(2)}, u32[]{:S(2)}) %collective-permute-start.2) | collective-permute-done | bytes 131104 | tf_op jit(solution)/shard_map/ppermute | solution.py:331
  16.5 3.5 %collective-permute-start.3 = (bf16[2,256,128]{2,1,0:T(8,128)(2,1)S(1)}, bf16[2,256,128]{2,1,0:T(8,128)(2,1)S(1)}, u32[]{:S(2)}, u32[]{:S(2)}) collective-permute-start(bf16[2,256,128]{2,1,0:T(8,128)(2,1)S(1)} %shard_map.96.ours), channel_id=1, source_target_pairs={{0,64},{1,193},{2,66},{3,195},{4,68},{5,197},{6,70},{7,199},{8,72}... | collective-permute-start | bytes 393224 | tf_op jit(solution)/shard_map/ppermute | solution.py:340
  20.3 2.3 %collective-permute-start.7 = (bf16[2,256,128]{2,1,0:T(8,128)(2,1)S(1)}, bf16[2,256,128]{2,1,0:T(8,128)(2,1)S(1)}, u32[]{:S(2)}, u32[]{:S(2)}) collective-permute-start(bf16[2,256,128]{2,1,0:T(8,128)(2,1)S(1)} %shard_map.100.ours), channel_id=1, source_target_pairs={{0,192},{1,65},{2,194},{3,67},{4,196},{5,69},{6,198},{7,71},{8,200... | collective-permute-start | bytes 393224 | tf_op jit(solution)/shard_map/ppermute | solution.py:340
  22.7 2.4 %collective-permute-start.8 = (bf16[2,256,128]{2,1,0:T(8,128)(2,1)S(1)}, bf16[2,256,128]{2,1,0:T(8,128)(2,1)S(1)}, u32[]{:S(2)}, u32[]{:S(2)}) collective-permute-start(bf16[2,256,128]{2,1,0:T(8,128)(2,1)S(1)} %shard_map.97.low), channel_id=1, source_target_pairs={{0,192},{1,65},{2,194},{3,67},{4,196},{5,69},{6,198},{7,71},{8,200... | collective-permute-start | bytes 393224 | tf_op jit(solution)/shard_map/ppermute | solution.py:340
  25.1 1.8 %collective-permute-done.7.theirs = bf16[2,256,128]{2,1,0:T(8,128)(2,1)S(1)} collective-permute-done((bf16[2,256,128]{2,1,0:T(8,128)(2,1)S(1)}, bf16[2,256,128]{2,1,0:T(8,128)(2,1)S(1)}, u32[]{:S(2)}, u32[]{:S(2)}) %collective-permute-start.7) | collective-permute-done | bytes 131104 | tf_op jit(solution)/shard_map/ppermute | solution.py:340
  26.9 4.7 %collective-permute-start.9 = (bf16[2,256,128]{2,1,0:T(8,128)(2,1)S(1)}, bf16[2,256,128]{2,1,0:T(8,128)(2,1)S(1)}, u32[]{:S(2)}, u32[]{:S(2)}) collective-permute-start(bf16[2,256,128]{2,1,0:T(8,128)(2,1)S(1)} %shard_map.101.high), channel_id=1, source_target_pairs={{0,64},{1,193},{2,66},{3,195},{4,68},{5,197},{6,70},{7,199},{8,72}... | collective-permute-start | bytes 393224 | tf_op jit(solution)/shard_map/ppermute | solution.py:340
  32.5 1.4 %shard_map.102 = (f32[4096,128]{1,0:T(8,128)S(1)}, f32[4,256,128]{2,1,0:T(8,128)S(1)}) custom-call(f32[2]{0:T(128)S(1)} %pad_maximum_fusion.bias, f32[1,524288]{1,0:T(1,128)S(1)} %copy-done.1), custom_call_target="tpu_custom_call" | custom-call | tf_op jit(solution)/shard_map/pallas_call | solution.py:53
  33.9 3.0 %collective-permute-done.9.other_high = bf16[2,256,128]{2,1,0:T(8,128)(2,1)S(1)} collective-permute-done((bf16[2,256,128]{2,1,0:T(8,128)(2,1)S(1)}, bf16[2,256,128]{2,1,0:T(8,128)(2,1)S(1)}, u32[]{:S(2)}, u32[]{:S(2)}) %collective-permute-start.9) | collective-permute-done | bytes 131104 | tf_op jit(solution)/shard_map/ppermute | solution.py:340
  36.9 1.7 %shard_map.103 = (bf16[4,256,128]{2,1,0:T(8,128)(2,1)S(1)}, f32[64,1,128]{2,1,0:T(1,128)}) custom-call(s32[4]{0:T(128)S(1)} %copy-done.6, bf16[2,256,128]{2,1,0:T(8,128)(2,1)S(1)} %shard_map.97.low, bf16[2,256,128]{2,1,0:T(8,128)(2,1)S(1)} %shard_map.101.high, bf16[2,256,128]{2,1,0:T(8,128)(2,1)S(1)} %collective-permute-done.8.other_low, ...), custom_call_target="tpu_custom_call" | custom-call | tf_op jit(solution)/shard_map/pallas_call | solution.py:53
  38.6 1.9 %collective-permute-start.12 = (bf16[4,256,128]{2,1,0:T(8,128)(2,1)S(1)}, bf16[4,256,128]{2,1,0:T(8,128)(2,1)}, u32[]{:S(2)}, u32[]{:S(2)}) collective-permute-start(bf16[4,256,128]{2,1,0:T(8,128)(2,1)S(1)} %get-tuple-element.25.refs_0_), channel_id=1, source_target_pairs={{0,32},{16,48},{32,0},{48,16},{1,33},{17,49},{33,1},{49,17},{2,34}... | collective-permute-start | bytes 786440 | tf_op jit(solution)/shard_map/ppermute | solution.py:331
  40.5 0.4 collective-permute-start.11
  40.9 1.1 %collective-permute-start.10 = (bf16[4,256,128]{2,1,0:T(8,128)(2,1)S(1)}, bf16[4,256,128]{2,1,0:T(8,128)(2,1)}, u32[]{:S(2)}, u32[]{:S(2)}) collective-permute-start(bf16[4,256,128]{2,1,0:T(8,128)(2,1)S(1)} %get-tuple-element.25.refs_0_), channel_id=1, source_target_pairs={{0,48},{16,32},{32,16},{48,0},{1,49},{17,33},{33,17},{49,1},{2,50}... | collective-permute-start | bytes 786440 | tf_op jit(solution)/shard_map/ppermute | solution.py:331
  42.0 9.6 %all-to-all-start = ((f32[64,1,128]{2,1,0:T(1,128)}), f32[64,1,128]{2,1,0:T(1,128)S(1)}, u32[]{:S(2)}, u32[]{:S(2)}) async-start(f32[64,1,128]{2,1,0:T(1,128)} %get-tuple-element.28), calls=%async_computation | async-start | bytes 65536 | tf_op jit(solution)/shard_map/all_to_all | solution.py:361
  51.6 0.7 %collective-permute-done.10.refs_1_ = bf16[4,256,128]{2,1,0:T(8,128)(2,1)} collective-permute-done((bf16[4,256,128]{2,1,0:T(8,128)(2,1)S(1)}, bf16[4,256,128]{2,1,0:T(8,128)(2,1)}, u32[]{:S(2)}, u32[]{:S(2)}) %collective-permute-start.10) | collective-permute-done | bytes 262176 | tf_op jit(solution)/shard_map/ppermute | solution.py:331
  52.3 2.5 %shard_map.104 = (f32[4096,128]{1,0:T(8,128)}, f32[4096,128]{1,0:T(8,128)S(1)}) custom-call(bf16[4,256,128]{2,1,0:T(8,128)(2,1)S(1)} %get-tuple-element.25.refs_0_, bf16[4,256,128]{2,1,0:T(8,128)(2,1)} %collective-permute-done.10.refs_1_, bf16[4,256,128]{2,1,0:T(8,128)(2,1)} %collective-permute-done.11.refs_2_, ...), custom_call_target="tpu_custom_call", output_to_operand_aliasing={{1}: (4, {})} | custom-call | tf_op jit(solution)/shard_map/pallas_call | solution.py:53
  54.9 4.4 %all-to-all-done.totals = f32[64,1,128]{2,1,0:T(1,128)S(1)} async-done(((f32[64,1,128]{2,1,0:T(1,128)}), f32[64,1,128]{2,1,0:T(1,128)S(1)}, u32[]{:S(2)}, u32[]{:S(2)}) %all-to-all-start) | async-done | bytes 32800 | tf_op jit(solution)/shard_map/all_to_all | solution.py:361
  59.3 2.2 %shard_map.105 = f32[4096,128]{1,0:T(8,128)} custom-call(s32[4]{0:T(128)S(1)} %copy-done.6, f32[64,1,128]{2,1,0:T(1,128)S(1)} %all-to-all-done.totals, f32[4096,128]{1,0:T(8,128)S(1)} %get-tuple-element.29.direction, bf16[4096,128]{1,0:T(8,128)(2,1)S(1)} %shard_map.99.refs_5_.dense), custom_call_target="tpu_custom_call" | custom-call | tf_op jit(solution)/shard_map/pallas_call | solution.py:53
  (30 shorter events, 1.1 us)
Async XLA Ops:
  3.0 10.0 %collective-permute-start = (bf16[2,256,128]{2,1,0:T(8,128)(2,1)}, bf16[2,256,128]{2,1,0:T(8,128)(2,1)S(1)}, u32[]{:S(2)}, u32[]{:S(2)}) collective-permute-start(bf16[2,256,128]{2,1,0:T(8,128)(2,1)} %get-tuple-element.17), channel_id=1, source_target_pairs={{0,32},{16,48},{32,0},{48,16},{1,33},{17,49},{33,1},{49,17},{2,34}... | collective-permute-start | bytes 393224 | tf_op jit(solution)/shard_map/ppermute | solution.py:331
  6.9 6.9 %collective-permute-start.1 = (bf16[2,256,128]{2,1,0:T(8,128)(2,1)}, bf16[2,256,128]{2,1,0:T(8,128)(2,1)S(1)}, u32[]{:S(2)}, u32[]{:S(2)}) collective-permute-start(bf16[2,256,128]{2,1,0:T(8,128)(2,1)} %get-tuple-element.18), channel_id=1, source_target_pairs={{0,16},{16,0},{32,48},{48,32},{1,17},{17,1},{33,49},{49,33},{2,18}... | collective-permute-start | bytes 393224 | tf_op jit(solution)/shard_map/ppermute | solution.py:331
  7.3 6.4 %copy-start = (bf16[1,524288]{1,0:T(2,128)(2,1)S(1)}, bf16[1,524288]{1,0:T(2,128)(2,1)}, u32[]{:S(2)}) copy-start(bf16[1,524288]{1,0:T(2,128)(2,1)} %weights.1) | copy-start | bytes 3145732
  7.3 9.1 %collective-permute-start.2 = (bf16[2,256,128]{2,1,0:T(8,128)(2,1)}, bf16[2,256,128]{2,1,0:T(8,128)(2,1)S(1)}, u32[]{:S(2)}, u32[]{:S(2)}) collective-permute-start(bf16[2,256,128]{2,1,0:T(8,128)(2,1)} %get-tuple-element.19), channel_id=1, source_target_pairs={{0,48},{16,32},{32,16},{48,0},{1,49},{17,33},{33,17},{49,1},{2,50}... | collective-permute-start | bytes 393224 | tf_op jit(solution)/shard_map/ppermute | solution.py:331
  10.2 6.2 %copy-start.3 = (f32[1,32768]{1,0:T(1,128)S(1)}, f32[1,32768]{1,0:T(1,128)}, u32[]{:S(2)}) copy-start(f32[1,32768]{1,0:T(1,128)} %refs_4_.3) | copy-start | bytes 393220
  10.3 6.2 %copy-start.5 = (bf16[2,256,128]{2,1,0:T(8,128)(2,1)S(1)}, bf16[2,256,128]{2,1,0:T(8,128)(2,1)}, u32[]{:S(2)}) copy-start(bf16[2,256,128]{2,1,0:T(8,128)(2,1)} %get-tuple-element.16.refs_0_) | copy-start | bytes 393220
  10.3 9.9 %copy-start.4 = (bf16[2,256,128]{2,1,0:T(8,128)(2,1)S(1)}, bf16[2,256,128]{2,1,0:T(8,128)(2,1)}, u32[]{:S(2)}) copy-start(bf16[2,256,128]{2,1,0:T(8,128)(2,1)} %get-tuple-element.20.refs_0_) | copy-start | bytes 393220
  10.3 9.8 %collective-permute-start.4 = (bf16[2,256,128]{2,1,0:T(8,128)(2,1)}, bf16[2,256,128]{2,1,0:T(8,128)(2,1)S(1)}, u32[]{:S(2)}, u32[]{:S(2)}) collective-permute-start(bf16[2,256,128]{2,1,0:T(8,128)(2,1)} %get-tuple-element.21), channel_id=1, source_target_pairs={{0,32},{16,48},{32,0},{48,16},{1,33},{17,49},{33,1},{49,17},{2,34}... | collective-permute-start | bytes 393224 | tf_op jit(solution)/shard_map/ppermute | solution.py:331
  12.6 7.4 %collective-permute-start.5 = (bf16[2,256,128]{2,1,0:T(8,128)(2,1)}, bf16[2,256,128]{2,1,0:T(8,128)(2,1)S(1)}, u32[]{:S(2)}, u32[]{:S(2)}) collective-permute-start(bf16[2,256,128]{2,1,0:T(8,128)(2,1)} %get-tuple-element.22), channel_id=1, source_target_pairs={{0,16},{16,0},{32,48},{48,32},{1,17},{17,1},{33,49},{49,33},{2,18}... | collective-permute-start | bytes 393224 | tf_op jit(solution)/shard_map/ppermute | solution.py:331
  13.1 7.1 %collective-permute-start.6 = (bf16[2,256,128]{2,1,0:T(8,128)(2,1)}, bf16[2,256,128]{2,1,0:T(8,128)(2,1)S(1)}, u32[]{:S(2)}, u32[]{:S(2)}) collective-permute-start(bf16[2,256,128]{2,1,0:T(8,128)(2,1)} %get-tuple-element.23), channel_id=1, source_target_pairs={{0,48},{16,32},{32,16},{48,0},{1,49},{17,33},{33,17},{49,1},{2,50}... | collective-permute-start | bytes 393224 | tf_op jit(solution)/shard_map/ppermute | solution.py:331
  13.8 18.7 %copy-start.1 = (f32[1,524288]{1,0:T(1,128)S(1)}, f32[1,524288]{1,0:T(1,128)}, u32[]{:S(2)}) copy-start(f32[1,524288]{1,0:T(1,128)} %variance.1) | copy-start | bytes 6291460
  16.5 6.1 %collective-permute-start.3 = (bf16[2,256,128]{2,1,0:T(8,128)(2,1)S(1)}, bf16[2,256,128]{2,1,0:T(8,128)(2,1)S(1)}, u32[]{:S(2)}, u32[]{:S(2)}) collective-permute-start(bf16[2,256,128]{2,1,0:T(8,128)(2,1)S(1)} %shard_map.96.ours), channel_id=1, source_target_pairs={{0,64},{1,193},{2,66},{3,195},{4,68},{5,197},{6,70},{7,199},{8,72}... | collective-permute-start | bytes 393224 | tf_op jit(solution)/shard_map/ppermute | solution.py:340
  20.2 16.7 %copy-start.2 = (f32[1,524288]{1,0:T(1,128)S(1)}, f32[1,524288]{1,0:T(1,128)}, u32[]{:S(2)}) copy-start(f32[1,524288]{1,0:T(1,128)} %momentum.1) | copy-start | bytes 6291460
  20.2 16.7 %copy-start.6 = (s32[4]{0:T(128)S(1)}, s32[4]{0:T(128)}, u32[]{:S(2)}) copy-start(s32[4]{0:T(128)} %offsets.3) | copy-start | bytes 52
  20.3 6.6 %collective-permute-start.7 = (bf16[2,256,128]{2,1,0:T(8,128)(2,1)S(1)}, bf16[2,256,128]{2,1,0:T(8,128)(2,1)S(1)}, u32[]{:S(2)}, u32[]{:S(2)}) collective-permute-start(bf16[2,256,128]{2,1,0:T(8,128)(2,1)S(1)} %shard_map.100.ours), channel_id=1, source_target_pairs={{0,192},{1,65},{2,194},{3,67},{4,196},{5,69},{6,198},{7,71},{8,200... | collective-permute-start | bytes 393224 | tf_op jit(solution)/shard_map/ppermute | solution.py:340
  22.7 11.2 %collective-permute-start.8 = (bf16[2,256,128]{2,1,0:T(8,128)(2,1)S(1)}, bf16[2,256,128]{2,1,0:T(8,128)(2,1)S(1)}, u32[]{:S(2)}, u32[]{:S(2)}) collective-permute-start(bf16[2,256,128]{2,1,0:T(8,128)(2,1)S(1)} %shard_map.97.low), channel_id=1, source_target_pairs={{0,192},{1,65},{2,194},{3,67},{4,196},{5,69},{6,198},{7,71},{8,200... | collective-permute-start | bytes 393224 | tf_op jit(solution)/shard_map/ppermute | solution.py:340
  26.9 9.9 %collective-permute-start.9 = (bf16[2,256,128]{2,1,0:T(8,128)(2,1)S(1)}, bf16[2,256,128]{2,1,0:T(8,128)(2,1)S(1)}, u32[]{:S(2)}, u32[]{:S(2)}) collective-permute-start(bf16[2,256,128]{2,1,0:T(8,128)(2,1)S(1)} %shard_map.101.high), channel_id=1, source_target_pairs={{0,64},{1,193},{2,66},{3,195},{4,68},{5,197},{6,70},{7,199},{8,72}... | collective-permute-start | bytes 393224 | tf_op jit(solution)/shard_map/ppermute | solution.py:340
  38.6 13.0 %collective-permute-start.12 = (bf16[4,256,128]{2,1,0:T(8,128)(2,1)S(1)}, bf16[4,256,128]{2,1,0:T(8,128)(2,1)}, u32[]{:S(2)}, u32[]{:S(2)}) collective-permute-start(bf16[4,256,128]{2,1,0:T(8,128)(2,1)S(1)} %get-tuple-element.25.refs_0_), channel_id=1, source_target_pairs={{0,32},{16,48},{32,0},{48,16},{1,33},{17,49},{33,1},{49,17},{2,34}... | collective-permute-start | bytes 786440 | tf_op jit(solution)/shard_map/ppermute | solution.py:331
  40.5 11.1 %collective-permute-start.11 = (bf16[4,256,128]{2,1,0:T(8,128)(2,1)S(1)}, bf16[4,256,128]{2,1,0:T(8,128)(2,1)}, u32[]{:S(2)}, u32[]{:S(2)}) collective-permute-start(bf16[4,256,128]{2,1,0:T(8,128)(2,1)S(1)} %get-tuple-element.25.refs_0_), channel_id=1, source_target_pairs={{0,16},{16,0},{32,48},{48,32},{1,17},{17,1},{33,49},{49,33},{2,18}... | collective-permute-start | bytes 786440 | tf_op jit(solution)/shard_map/ppermute | solution.py:331
  40.9 11.4 %collective-permute-start.10 = (bf16[4,256,128]{2,1,0:T(8,128)(2,1)S(1)}, bf16[4,256,128]{2,1,0:T(8,128)(2,1)}, u32[]{:S(2)}, u32[]{:S(2)}) collective-permute-start(bf16[4,256,128]{2,1,0:T(8,128)(2,1)S(1)} %get-tuple-element.25.refs_0_), channel_id=1, source_target_pairs={{0,48},{16,32},{32,16},{48,0},{1,49},{17,33},{33,17},{49,1},{2,50}... | collective-permute-start | bytes 786440 | tf_op jit(solution)/shard_map/ppermute | solution.py:331
  42.0 17.3 %all-to-all-start = ((f32[64,1,128]{2,1,0:T(1,128)}), f32[64,1,128]{2,1,0:T(1,128)S(1)}, u32[]{:S(2)}, u32[]{:S(2)}) async-start(f32[64,1,128]{2,1,0:T(1,128)} %get-tuple-element.28), calls=%async_computation | async-start | bytes 65536 | tf_op jit(solution)/shard_map/all_to_all | solution.py:361

commit v5 on v4

--- a/solution.py
+++ b/solution.py
@@ -20,6 +20,8 @@
 N_Y = 4
 N_DP = N_Z * N_Y
 N_TENSOR = 16
+N_CORE = 2
+N_CHIP = N_TENSOR // N_CORE
 SHARE = BUCKET // N_DP
 ROWS = SHARE // QB
 BLOCKS = BUCKET // QB
@@ -30,7 +32,8 @@
 MIB = 1024 * 1024
 PREPARE_LIMIT = 54
 ORDER = (2, 1, 3)
-LAST_ORDER = (3, 1, 2)
+EARLY, LATE = (0, 2), (1, 3)
+GATHER = (2, 1, 3)
 
 
 def on_chip(count):
@@ -69,6 +72,10 @@
     return lax.axis_index("y")
 
 
+def partner(y, k):
+    return y ^ k ^ (2 * lax.axis_index("core")) if k % 2 else y ^ k
+
+
 def share_of(ref, block):
     return rows_of(ref[:, pl.ds(pl.multiple_of(block * SHARE, SHARE), SHARE)])
 
@@ -78,7 +85,7 @@
 
 
 def prepare_kernel(half, grad, err, *refs):
-    outs, (held_grad, held_err, sems) = refs[:N_Y], refs[N_Y:]
+    outs, (held_grad, held_err, held_out, sems, out_sems) = refs[:N_Y], refs[N_Y:]
     y = my_y()
     width = N_Y * SHARE
     copies = []
@@ -94,14 +101,19 @@
     for pair in copies:
         for copy in pair:
             copy.start()
+    stores = []
     for s in range(HALF):
         for copy in copies[s]:
             copy.wait()
         for k in range(N_Y):
-            block = pl.ds(pl.multiple_of((s * N_Y + (y ^ k)) * SHARE, SHARE), SHARE)
+            block = pl.ds(pl.multiple_of((s * N_Y + partner(y, k)) * SHARE, SHARE), SHARE)
             g = held_grad[0, :, block].astype(F32)
             e = held_err[0, :, block].astype(F32)
-            outs[k][s] = rows_of((1.0 - BETA_ONE) * g + e).astype(BF16)
+            held_out[k, s] = rows_of((1.0 - BETA_ONE) * g + e).astype(BF16)
+            stores.append(pltpu.make_async_copy(held_out.at[k, s], outs[k].at[s], out_sems.at[k, s]))
+            stores[-1].start()
+    for store in stores:
+        store.wait()
 
 
 def prepare(half, grad, err):
@@ -111,9 +123,15 @@
         (),
         (grad, err),
         anywhere(2),
-        on_chip(N_Y),
+        anywhere(N_Y),
         (like(HALF_SHAPE, BF16),) * N_Y,
-        scratch=[held, held, pltpu.SemaphoreType.DMA((2, HALF))],
+        scratch=[
+            held,
+            held,
+            pltpu.VMEM((N_Y, *HALF_SHAPE), BF16),
+            pltpu.SemaphoreType.DMA((2, HALF)),
+            pltpu.SemaphoreType.DMA((N_Y, HALF)),
+        ],
         limit=PREPARE_LIMIT,
     )
 
@@ -204,7 +222,7 @@
     folded = folded + pltpu.roll(folded, QB // 4, 1)
     lane = lax.broadcasted_iota(jnp.int32, (8, QB), 1) // (QB // SEGS)
     mine = jnp.where(lane == lane_row, folded, 0.0)
-    out[...] = jnp.broadcast_to(jnp.sum(mine, axis=0, keepdims=True)[None], out.shape)
+    out[...] = jnp.broadcast_to(jnp.sum(mine, axis=0, keepdims=True), out.shape)
 
 
 def server(offsets, halves, momentum, spread):
@@ -214,9 +232,20 @@
         (*halves, momentum, spread),
         on_chip(6),
         on_chip(2),
-        (like((N_Z, ROWS, QB), BF16), like((N_Y * N_TENSOR, 1, QB), F32)),
+        (like((N_Z, ROWS, QB), BF16), like((512, QB), F32)),
         scratch=[pltpu.VMEM((8, QB), F32)],
     )
+
+
+def pair_kernel(ours, theirs, out):
+    out[...] = jnp.broadcast_to((ours[:1, :] + theirs[:1, :])[None], out.shape)
+
+
+def pair(ours, theirs):
+    (out,) = call(
+        pair_kernel, (), (ours, theirs), on_chip(2), on_chip(1), [like((N_Y * N_CHIP, 1, QB), F32)]
+    )
+    return out
 
 
 def spread_kernel(bias, variance, spread, column_spread):
@@ -248,34 +277,38 @@
     return out
 
 
-def momentum_kernel(*refs):
-    pieces, (spread, out, direction, held, sems) = refs[:N_Y], refs[N_Y:]
+def momentum_kernel(ks, *refs):
+    pieces = refs[: len(ks)]
+    out, direction, held, sems = refs[-4:]
     y = my_y()
     stores = []
     for s in range(N_Z):
-        for k, piece in zip((0, *LAST_ORDER), pieces):
-            rows = rows_at(s * N_Y + (y ^ k))
+        for j, (k, piece) in enumerate(zip(ks, pieces)):
+            rows = rows_at(s * N_Y + partner(y, k))
             kept = piece[s].astype(F32)
-            held[rows, :] = kept
-            direction[rows, :] = kept * spread[rows, :]
-        rows = pl.ds(s * N_Y * ROWS, N_Y * ROWS)
-        stores.append(pltpu.make_async_copy(held.at[rows], out.at[rows], sems.at[s]))
-        stores[-1].start()
+            held[j, s] = kept
+            direction[rows, :] = kept * direction[rows, :]
+            stores.append(pltpu.make_async_copy(held.at[j, s], out.at[rows], sems.at[j, s]))
+            stores[-1].start()
     for store in stores:
         store.wait()
 
 
-def momentum_of(pieces, spread):
+def momentum_of(ks, pieces, spread, *partial):
     out = like((BLOCKS, QB), F32)
+    count = len(ks)
+    aliases = {count: 1}
+    if partial:
+        aliases[count + 1] = 0
     return call(
-        momentum_kernel,
+        functools.partial(momentum_kernel, ks),
         (),
-        (*pieces, spread),
-        on_chip(N_Y + 1),
+        (*pieces, spread, *partial),
+        on_chip(count + 1) + anywhere(len(partial)),
         anywhere(1) + on_chip(1),
         (out, out),
-        scratch=[pltpu.VMEM((BLOCKS, QB), F32), pltpu.SemaphoreType.DMA((N_Z,))],
-        aliases={N_Y: 1},
+        scratch=[pltpu.VMEM((count, N_Z, ROWS, QB), F32), pltpu.SemaphoreType.DMA((count, N_Z))],
+        aliases=aliases,
     )
 
 
@@ -288,9 +321,9 @@
         entries = (end - offsets[k]).astype(F32) * N_TENSOR
         squares = jnp.sum(jnp.where(lane == k, total, 0.0), axis=1, keepdims=True)
         inverse.append(1.0 / jnp.maximum(1.0, jnp.sqrt(squares / entries + 1e-06) / CLIP_RMS))
-    copies = []
-    for part in range(BLOCKS // ROWS):
-        first = part * ROWS
+    stores = []
+    for block in range(N_DP):
+        first = block * ROWS
         rows = pl.ds(first, ROWS)
         mixed = has_boundary(offsets, first, ROWS)
 
@@ -308,10 +341,10 @@
                 factor = jnp.where(mask, inverse[k + 1], factor)
             held[rows, :] = direction[rows, :] * factor + DECAY * dense[rows, :].astype(F32)
 
-        copies.append(pltpu.make_async_copy(held.at[rows], out.at[rows], sems.at[part]))
-        copies[-1].start()
-    for copy in copies:
-        copy.wait()
+        stores.append(pltpu.make_async_copy(held.at[rows], out.at[rows], sems.at[block]))
+        stores[-1].start()
+    for store in stores:
+        store.wait()
 
 
 def step_of(offsets, totals, direction, dense):
@@ -322,13 +355,22 @@
         on_chip(3),
         anywhere(1),
         [like((BLOCKS, QB), F32)],
-        scratch=[pltpu.VMEM((BLOCKS, QB), F32), pltpu.SemaphoreType.DMA((BLOCKS // ROWS,))],
+        scratch=[pltpu.VMEM((BLOCKS, QB), F32), pltpu.SemaphoreType.DMA((N_DP,))],
     )
     return out
 
 
 def exchange(value, axis, mask):
     return lax.ppermute(value, axis, [(i, i ^ mask) for i in range(lax.axis_size(axis))])
+
+
+def exchange_y(value, k):
+    pairs = []
+    for y in range(N_Y):
+        for t in range(N_TENSOR):
+            to = y ^ k ^ (2 * (t % N_CORE) if k % 2 else 0)
+            pairs.append((y * N_TENSOR + t, to * N_TENSOR + t))
+    return lax.ppermute(value, ("y", "chip", "core"), pairs)
 
 
 def exchange_z(value, even, odd):
@@ -337,7 +379,7 @@
         for z in range(N_Z)
         for t in range(N_TENSOR)
     ]
-    return lax.ppermute(value, ("z", "tensor"), pairs)
+    return lax.ppermute(value, ("z", "chip", "core"), pairs)
 
 
 def body(grad, worker_err, momentum, variance, params, server_err, offsets, step_count):
@@ -349,31 +391,33 @@
     spread, column_spread = spread_of(bias, variance)
     dense = dense_of(params)
     low_y, high_y = prepare(0, grad, worker_err), prepare(1, grad, worker_err)
-    low = [low_y[0]] + [exchange(low_y[k], "y", k) for k in ORDER]
-    high = [high_y[0]] + [exchange(high_y[k], "y", k) for k in ORDER]
+    low = [low_y[0]] + [exchange_y(low_y[k], k) for k in ORDER]
+    high = [high_y[0]] + [exchange_y(high_y[k], k) for k in ORDER]
     low = reduce_y(0, low, server_err)
     high = reduce_y(1, high, server_err, dense)
-    low = add(low, exchange_z(low, 1, 3))
-    high = add(high, exchange_z(high, 3, 1))
-    halves = (low, high, exchange_z(low, 3, 1), exchange_z(high, 1, 3))
+    low = add(low, exchange_z(low, 3, 1))
+    high = add(high, exchange_z(high, 1, 3))
+    halves = (low, high, exchange_z(low, 1, 3), exchange_z(high, 3, 1))
     column, squares = server(offsets, halves, momentum, column_spread)
-    columns = [column] + [exchange(column, "y", k) for k in LAST_ORDER]
-    totals = lax.all_to_all(squares, ("y", "tensor"), split_axis=0, concat_axis=0, tiled=True)
-    momentum_new, direction = momentum_of(columns, spread)
+    received = {k: exchange_y(column, k) for k in GATHER}
+    squares = pair(squares, exchange(squares, "core", 1))
+    totals = lax.all_to_all(squares, ("y", "chip"), split_axis=0, concat_axis=0, tiled=True)
+    partial, direction = momentum_of(EARLY, [column] + [received[k] for k in EARLY[1:]], spread)
+    momentum_new, direction = momentum_of(LATE, [received[k] for k in LATE], direction, partial)
     param_step = step_of(offsets, totals, direction, dense)
     return (momentum_new.reshape(1, BUCKET), param_step.reshape(1, BUCKET))
 
 
 def solution(mesh):
-    split = Mesh(mesh.devices.reshape(N_Z, N_Y, N_TENSOR), ("z", "y", "tensor"))
-    dp = ("z", "y")
+    split = Mesh(mesh.devices.reshape(N_Z, N_Y, N_CHIP, N_CORE), ("z", "y", "chip", "core"))
+    dp, tensor = ("z", "y"), ("chip", "core")
     placed = (
-        P(dp, "tensor", None),
-        P(dp, "tensor", None),
-        P("tensor", None),
-        P("tensor", None),
-        P("tensor", None),
-        P("tensor", dp),
+        P(dp, tensor, None),
+        P(dp, tensor, None),
+        P(tensor, None),
+        P(tensor, None),
+        P(tensor, None),
+        P(tensor, dp),
         P(),
         P(),
     )
@@ -381,6 +425,6 @@
         body,
         mesh=split,
         in_specs=placed,
-        out_specs=(P("tensor", None), P("tensor", None)),
+        out_specs=(P(tensor, None), P(tensor, None)),
         check_vma=False,
     )

time: 61.7 us -> 60 us (0.972)
  starting transfers between devices: 33.8 us -> 29.3 us
  Pallas kernels: 13.1 us -> 14.7 us
  waiting for transfers between devices: 12.8 us -> 13.8 us
    ppermute x9 -> x1, starting transfers between devices: 11.4 us -> 1.39 us  [exchange(): lax.ppermute(value, axis, [(i, i ^ mask) for i in range(lax.axis_size(axi...]
    ppermute x4 -> x13, waiting for transfers between devices: 4.86 us -> 13.6 us  [the longest x4 7.62 us: exchange_z(): return lax.ppermute(value, ('z', 'chip', 'core'), pairs)]
    ppermute x4 -> x13, starting transfers between devices: 12.9 us -> 21.1 us  [the longest x9 11.9 us: exchange_y(): return lax.ppermute(value, ('y', 'chip', 'core'), pairs)]
    all_to_all x1, waiting for transfers between devices: 4.41 us -> 0.24 us  [body(): lax.all_to_all(squares, ('y', 'chip'), split_axis=0, concat_axis=0, tiled...]
    ppermute x9 -> x1, waiting for transfers between devices: 3.52 us -> 0.01 us  [exchange(): lax.ppermute(value, axis, [(i, i ^ mask) for i in range(lax.axis_size(axi...]
    all_to_all x1, starting transfers between devices: 9.6 us -> 6.8 us  [body(): lax.all_to_all(squares, ('y', 'chip'), split_axis=0, concat_axis=0, tiled...]
    pallas_call x11 -> x13, Pallas kernels: 13.1 us -> 14.7 us  [call(): pl.pallas_call(kernel, in_specs=[pl.BlockSpec(memory_space=pltpu.SMEM)] *...]
  transfers between devices with their start and end apart: 14 -> 15, of which waited for: 7 -> 6; matrix products, arithmetic and copies ran while one was open for 0% -> 0% of each run, Pallas kernels for 11% -> 15%
where the time goes in v5:
time: 60 us; the launch traced here: 59.5 us
  starting transfers between devices  29.3 us (49%)
  Pallas kernels  14.7 us (24%)
  waiting for transfers between devices  13.8 us (23%)
  between operations  1.6 us (3%)
    pallas_call x13, Pallas kernels, call(): pl.pallas_call(kernel, in_specs=[pl.BlockSpec(memory_space=pltpu.SMEM)] *...  14.7 us
    ppermute x9, starting transfers between devices, exchange_y(): return lax.ppermute(value, ('y', 'chip', 'core'), pairs)  11.9 us
    ppermute x4, starting transfers between devices, exchange_z(): return lax.ppermute(value, ('z', 'chip', 'core'), pairs)  9.25 us
    ppermute x4, waiting for transfers between devices, exchange_z(): return lax.ppermute(value, ('z', 'chip', 'core'), pairs)  7.62 us
    all_to_all x1, starting transfers between devices, body(): lax.all_to_all(squares, ('y', 'chip'), split_axis=0, concat_axis=0, tiled...  6.8 us
    ppermute x9, waiting for transfers between devices, exchange_y(): return lax.ppermute(value, ('y', 'chip', 'core'), pairs)  5.98 us
    ppermute x1, starting transfers between devices, exchange(): lax.ppermute(value, axis, [(i, i ^ mask) for i in range(lax.axis_size(axi...  1.39 us
  transfers between devices with their start and end apart: 15, of which 6 were waited for; matrix products, arithmetic and copies ran while one was open for 0% of the time, Pallas kernels for 15%

profile of v5, /device:TPU:1, one launch (start us, length us, event | category | flops | bytes accessed | tf_op | source)
XLA Modules:
  0.0 59.5 jit_solution(11192526293168924468)
XLA Ops:
  0.6 2.4 %shard_map.95 = (bf16[2,256,128]{2,1,0:T(8,128)(2,1)}, bf16[2,256,128]{2,1,0:T(8,128)(2,1)}, bf16[2,256,128]{2,1,0:T(8,128)(2,1)}, bf16[2,256,128]{2,1,0:T(8,128)(2,1)}) custom-call(bf16[1,1,524288]{2,1,0:T(2,128)(2,1)} %grad.3, bf16[1,1,524288]{2,1,0:T(2,128)(2,1)} %err.3), custom_call_target="tpu_custom_call" | custom-call | tf_op jit(solution)/shard_map/pallas_call | solution.py:56
  3.1 3.8 %collective-permute-start = (bf16[2,256,128]{2,1,0:T(8,128)(2,1)}, bf16[2,256,128]{2,1,0:T(8,128)(2,1)S(1)}, u32[]{:S(2)}, u32[]{:S(2)}) collective-permute-start(bf16[2,256,128]{2,1,0:T(8,128)(2,1)} %get-tuple-element.19), channel_id=1, source_target_pairs={{0,32},{1,33},{2,34},{3,35},{4,36},{5,37},{6,38},{7,39},{8,40},{9,... | collective-permute-start | bytes 393224 | tf_op jit(solution)/shard_map/ppermute | solution.py:373
  6.9 0.8 %collective-permute-start.1 = (bf16[2,256,128]{2,1,0:T(8,128)(2,1)}, bf16[2,256,128]{2,1,0:T(8,128)(2,1)S(1)}, u32[]{:S(2)}, u32[]{:S(2)}) collective-permute-start(bf16[2,256,128]{2,1,0:T(8,128)(2,1)} %get-tuple-element.20), channel_id=1, source_target_pairs={{0,16},{1,49},{2,18},{3,51},{4,20},{5,53},{6,22},{7,55},{8,24},{9,... | collective-permute-start | bytes 393224 | tf_op jit(solution)/shard_map/ppermute | solution.py:373
  7.7 2.6 %shard_map.98 = (bf16[2,256,128]{2,1,0:T(8,128)(2,1)}, bf16[2,256,128]{2,1,0:T(8,128)(2,1)}, bf16[2,256,128]{2,1,0:T(8,128)(2,1)}, bf16[2,256,128]{2,1,0:T(8,128)(2,1)}) custom-call(bf16[1,1,524288]{2,1,0:T(2,128)(2,1)} %grad.3, bf16[1,1,524288]{2,1,0:T(2,128)(2,1)} %err.3), custom_call_target="tpu_custom_call" | custom-call | tf_op jit(solution)/shard_map/pallas_call | solution.py:56
  10.3 3.0 %collective-permute-start.4 = (bf16[2,256,128]{2,1,0:T(8,128)(2,1)}, bf16[2,256,128]{2,1,0:T(8,128)(2,1)S(1)}, u32[]{:S(2)}, u32[]{:S(2)}) collective-permute-start(bf16[2,256,128]{2,1,0:T(8,128)(2,1)} %get-tuple-element.23), channel_id=1, source_target_pairs={{0,32},{1,33},{2,34},{3,35},{4,36},{5,37},{6,38},{7,39},{8,40},{9,... | collective-permute-start | bytes 393224 | tf_op jit(solution)/shard_map/ppermute | solution.py:373
  13.3 0.8 %collective-permute-start.5 = (bf16[2,256,128]{2,1,0:T(8,128)(2,1)}, bf16[2,256,128]{2,1,0:T(8,128)(2,1)S(1)}, u32[]{:S(2)}, u32[]{:S(2)}) collective-permute-start(bf16[2,256,128]{2,1,0:T(8,128)(2,1)} %get-tuple-element.24), channel_id=1, source_target_pairs={{0,16},{1,49},{2,18},{3,51},{4,20},{5,53},{6,22},{7,55},{8,24},{9,... | collective-permute-start | bytes 393224 | tf_op jit(solution)/shard_map/ppermute | solution.py:373
  14.6 2.9 %collective-permute-start.3 = (bf16[2,256,128]{2,1,0:T(8,128)(2,1)S(1)}, bf16[2,256,128]{2,1,0:T(8,128)(2,1)S(1)}, u32[]{:S(2)}, u32[]{:S(2)}) collective-permute-start(bf16[2,256,128]{2,1,0:T(8,128)(2,1)S(1)} %shard_map.96.ours), channel_id=1, source_target_pairs={{0,192},{1,65},{2,194},{3,67},{4,196},{5,69},{6,198},{7,71},{8,200... | collective-permute-start | bytes 393224 | tf_op jit(solution)/shard_map/ppermute | solution.py:382
  17.5 3.0 %collective-permute-done.5.refs_2_ = bf16[2,256,128]{2,1,0:T(8,128)(2,1)S(1)} collective-permute-done((bf16[2,256,128]{2,1,0:T(8,128)(2,1)}, bf16[2,256,128]{2,1,0:T(8,128)(2,1)S(1)}, u32[]{:S(2)}, u32[]{:S(2)}) %collective-permute-start.5) | collective-permute-done | bytes 131104 | tf_op jit(solution)/shard_map/ppermute | solution.py:373
  20.7 5.3 %collective-permute-start.7 = (bf16[2,256,128]{2,1,0:T(8,128)(2,1)S(1)}, bf16[2,256,128]{2,1,0:T(8,128)(2,1)S(1)}, u32[]{:S(2)}, u32[]{:S(2)}) collective-permute-start(bf16[2,256,128]{2,1,0:T(8,128)(2,1)S(1)} %shard_map.100.ours), channel_id=1, source_target_pairs={{0,64},{1,193},{2,66},{3,195},{4,68},{5,197},{6,70},{7,199},{8,72}... | collective-permute-start | bytes 393224 | tf_op jit(solution)/shard_map/ppermute | solution.py:382
  26.1 4.0 %collective-permute-done.7.theirs = bf16[2,256,128]{2,1,0:T(8,128)(2,1)S(1)} collective-permute-done((bf16[2,256,128]{2,1,0:T(8,128)(2,1)S(1)}, bf16[2,256,128]{2,1,0:T(8,128)(2,1)S(1)}, u32[]{:S(2)}, u32[]{:S(2)}) %collective-permute-start.7) | collective-permute-done | bytes 131104 | tf_op jit(solution)/shard_map/ppermute | solution.py:382
  30.1 0.9 %collective-permute-start.9 = (bf16[2,256,128]{2,1,0:T(8,128)(2,1)S(1)}, bf16[2,256,128]{2,1,0:T(8,128)(2,1)S(1)}, u32[]{:S(2)}, u32[]{:S(2)}) collective-permute-start(bf16[2,256,128]{2,1,0:T(8,128)(2,1)S(1)} %shard_map.101.high), channel_id=1, source_target_pairs={{0,192},{1,65},{2,194},{3,67},{4,196},{5,69},{6,198},{7,71},{8,200... | collective-permute-start | bytes 393224 | tf_op jit(solution)/shard_map/ppermute | solution.py:382
  31.9 1.4 %shard_map.102 = (f32[4096,128]{1,0:T(8,128)S(1)}, f32[4,256,128]{2,1,0:T(8,128)S(1)}) custom-call(f32[2]{0:T(128)S(1)} %pad_maximum_fusion.bias, f32[1,524288]{1,0:T(1,128)S(1)} %copy-done.1), custom_call_target="tpu_custom_call" | custom-call | tf_op jit(solution)/shard_map/pallas_call | solution.py:56
  33.3 3.6 %collective-permute-done.9.other_high = bf16[2,256,128]{2,1,0:T(8,128)(2,1)S(1)} collective-permute-done((bf16[2,256,128]{2,1,0:T(8,128)(2,1)S(1)}, bf16[2,256,128]{2,1,0:T(8,128)(2,1)S(1)}, u32[]{:S(2)}, u32[]{:S(2)}) %collective-permute-start.9) | collective-permute-done | bytes 131104 | tf_op jit(solution)/shard_map/ppermute | solution.py:382
  37.0 1.0 %shard_map.103 = (bf16[4,256,128]{2,1,0:T(8,128)(2,1)S(1)}, f32[512,128]{1,0:T(8,128)S(1)}) custom-call(s32[4]{0:T(128)S(1)} %copy-done.6, bf16[2,256,128]{2,1,0:T(8,128)(2,1)S(1)} %shard_map.97.low, bf16[2,256,128]{2,1,0:T(8,128)(2,1)S(1)} %shard_map.101.high, bf16[2,256,128]{2,1,0:T(8,128)(2,1)S(1)} %collective-permute-done.8.other_low, ...), custom_call_target="tpu_custom_call" | custom-call | tf_op jit(solution)/shard_map/pallas_call | solution.py:56
  38.0 1.4 %collective-permute-start.13 = (f32[512,128]{1,0:T(8,128)S(1)}, f32[512,128]{1,0:T(8,128)S(1)}, u32[]{:S(2)}, u32[]{:S(2)}) collective-permute-start(f32[512,128]{1,0:T(8,128)S(1)} %get-tuple-element.32.ours), channel_id=1, source_target_pairs={{0,1},{1,0},{2,3},{3,2},{4,5},{5,4},{6,7},{7,6},{8,9},{9,8},{10,11... | collective-permute-start | bytes 786440 | tf_op jit(solution)/shard_map/ppermute | solution.py:364
  39.4 2.3 %collective-permute-start.12 = (bf16[4,256,128]{2,1,0:T(8,128)(2,1)S(1)}, bf16[4,256,128]{2,1,0:T(8,128)(2,1)}, u32[]{:S(2)}, u32[]{:S(2)}) collective-permute-start(bf16[4,256,128]{2,1,0:T(8,128)(2,1)S(1)} %get-tuple-element.27.refs_0_), channel_id=1, source_target_pairs={{0,32},{1,33},{2,34},{3,35},{4,36},{5,37},{6,38},{7,39},{8,40},{9,... | collective-permute-start | bytes 786440 | tf_op jit(solution)/shard_map/ppermute | solution.py:373
  41.7 1.2 %collective-permute-start.11 = (bf16[4,256,128]{2,1,0:T(8,128)(2,1)S(1)}, bf16[4,256,128]{2,1,0:T(8,128)(2,1)}, u32[]{:S(2)}, u32[]{:S(2)}) collective-permute-start(bf16[4,256,128]{2,1,0:T(8,128)(2,1)S(1)} %get-tuple-element.27.refs_0_), channel_id=1, source_target_pairs={{0,48},{1,17},{2,50},{3,19},{4,52},{5,21},{6,54},{7,23},{8,56},{9,... | collective-permute-start | bytes 786440 | tf_op jit(solution)/shard_map/ppermute | solution.py:373
  42.9 0.6 %shard_map.106 = f32[32,1,128]{2,1,0:T(1,128)} custom-call(f32[512,128]{1,0:T(8,128)S(1)} %get-tuple-element.32.ours, f32[512,128]{1,0:T(8,128)S(1)} %collective-permute-done.13.theirs), custom_call_target="tpu_custom_call" | custom-call | tf_op jit(solution)/shard_map/pallas_call | solution.py:56
  43.5 6.8 %all-to-all-start = ((f32[32,1,128]{2,1,0:T(1,128)}), f32[32,1,128]{2,1,0:T(1,128)S(1)}, u32[]{:S(2)}, u32[]{:S(2)}) async-start(f32[32,1,128]{2,1,0:T(1,128)} %shard_map.106), calls=%async_computation | async-start | bytes 32768 | tf_op jit(solution)/shard_map/all_to_all | solution.py:404
  50.4 2.0 %shard_map.104 = (f32[4096,128]{1,0:T(8,128)}, f32[4096,128]{1,0:T(8,128)S(1)}) custom-call(bf16[4,256,128]{2,1,0:T(8,128)(2,1)S(1)} %get-tuple-element.27.refs_0_, bf16[4,256,128]{2,1,0:T(8,128)(2,1)} %collective-permute-done.12.refs_1_, f32[4096,128]{1,0:T(8,128)S(1)} %get-tuple-element.28.refs_2_), custom_call_target="tpu_custom_call", output_to_operand_aliasing={{1}: (2, {})} | custom-call | tf_op jit(solution)/shard_map/pallas_call | solution.py:56
  52.3 2.7 %collective-permute-done.11.refs_1_ = bf16[4,256,128]{2,1,0:T(8,128)(2,1)} collective-permute-done((bf16[4,256,128]{2,1,0:T(8,128)(2,1)S(1)}, bf16[4,256,128]{2,1,0:T(8,128)(2,1)}, u32[]{:S(2)}, u32[]{:S(2)}) %collective-permute-start.11) | collective-permute-done | bytes 262176 | tf_op jit(solution)/shard_map/ppermute | solution.py:373
  55.1 2.1 %shard_map.105 = (f32[4096,128]{1,0:T(8,128)}, f32[4096,128]{1,0:T(8,128)S(1)}) custom-call(bf16[4,256,128]{2,1,0:T(8,128)(2,1)} %collective-permute-done.10.refs_0_, bf16[4,256,128]{2,1,0:T(8,128)(2,1)} %collective-permute-done.11.refs_1_, f32[4096,128]{1,0:T(8,128)S(1)} %get-tuple-element.29.refs_2_, ...), custom_call_target="tpu_custom_call", output_to_operand_aliasing={{1}: (2, {}), {0}: (3, {})} | custom-call | tf_op jit(solution)/shard_map/pallas_call | solution.py:56
  57.2 0.2 all-to-all-done.totals
  57.4 2.1 %shard_map.107 = f32[4096,128]{1,0:T(8,128)} custom-call(s32[4]{0:T(128)S(1)} %copy-done.6, f32[32,1,128]{2,1,0:T(1,128)S(1)} %all-to-all-done.totals, f32[4096,128]{1,0:T(8,128)S(1)} %get-tuple-element.33.direction, bf16[4096,128]{1,0:T(8,128)(2,1)S(1)} %shard_map.99.refs_5_.dense), custom_call_target="tpu_custom_call" | custom-call | tf_op jit(solution)/shard_map/pallas_call | solution.py:56
  (34 shorter events, 0.8 us)
Async XLA Ops:
  3.1 11.0 %collective-permute-start = (bf16[2,256,128]{2,1,0:T(8,128)(2,1)}, bf16[2,256,128]{2,1,0:T(8,128)(2,1)S(1)}, u32[]{:S(2)}, u32[]{:S(2)}) collective-permute-start(bf16[2,256,128]{2,1,0:T(8,128)(2,1)} %get-tuple-element.19), channel_id=1, source_target_pairs={{0,32},{1,33},{2,34},{3,35},{4,36},{5,37},{6,38},{7,39},{8,40},{9,... | collective-permute-start | bytes 393224 | tf_op jit(solution)/shard_map/ppermute | solution.py:373
  6.9 7.6 %collective-permute-start.1 = (bf16[2,256,128]{2,1,0:T(8,128)(2,1)}, bf16[2,256,128]{2,1,0:T(8,128)(2,1)S(1)}, u32[]{:S(2)}, u32[]{:S(2)}) collective-permute-start(bf16[2,256,128]{2,1,0:T(8,128)(2,1)} %get-tuple-element.20), channel_id=1, source_target_pairs={{0,16},{1,49},{2,18},{3,51},{4,20},{5,53},{6,22},{7,55},{8,24},{9,... | collective-permute-start | bytes 393224 | tf_op jit(solution)/shard_map/ppermute | solution.py:373
  7.7 6.4 %copy-start = (bf16[1,524288]{1,0:T(2,128)(2,1)S(1)}, bf16[1,524288]{1,0:T(2,128)(2,1)}, u32[]{:S(2)}) copy-start(bf16[1,524288]{1,0:T(2,128)(2,1)} %weights.1) | copy-start | bytes 3145732
  7.7 6.8 %collective-permute-start.2 = (bf16[2,256,128]{2,1,0:T(8,128)(2,1)}, bf16[2,256,128]{2,1,0:T(8,128)(2,1)S(1)}, u32[]{:S(2)}, u32[]{:S(2)}) collective-permute-start(bf16[2,256,128]{2,1,0:T(8,128)(2,1)} %get-tuple-element.21), channel_id=1, source_target_pairs={{0,48},{1,17},{2,50},{3,19},{4,52},{5,21},{6,54},{7,23},{8,56},{9,... | collective-permute-start | bytes 393224 | tf_op jit(solution)/shard_map/ppermute | solution.py:373
  10.3 4.2 %copy-start.3 = (f32[1,32768]{1,0:T(1,128)S(1)}, f32[1,32768]{1,0:T(1,128)}, u32[]{:S(2)}) copy-start(f32[1,32768]{1,0:T(1,128)} %refs_4_.3) | copy-start | bytes 393220
  10.3 4.2 %copy-start.5 = (bf16[2,256,128]{2,1,0:T(8,128)(2,1)S(1)}, bf16[2,256,128]{2,1,0:T(8,128)(2,1)}, u32[]{:S(2)}) copy-start(bf16[2,256,128]{2,1,0:T(8,128)(2,1)} %get-tuple-element.18.refs_0_) | copy-start | bytes 393220
  10.3 10.2 %copy-start.4 = (bf16[2,256,128]{2,1,0:T(8,128)(2,1)S(1)}, bf16[2,256,128]{2,1,0:T(8,128)(2,1)}, u32[]{:S(2)}) copy-start(bf16[2,256,128]{2,1,0:T(8,128)(2,1)} %get-tuple-element.22.refs_0_) | copy-start | bytes 393220
  10.3 7.2 %collective-permute-start.4 = (bf16[2,256,128]{2,1,0:T(8,128)(2,1)}, bf16[2,256,128]{2,1,0:T(8,128)(2,1)S(1)}, u32[]{:S(2)}, u32[]{:S(2)}) collective-permute-start(bf16[2,256,128]{2,1,0:T(8,128)(2,1)} %get-tuple-element.23), channel_id=1, source_target_pairs={{0,32},{1,33},{2,34},{3,35},{4,36},{5,37},{6,38},{7,39},{8,40},{9,... | collective-permute-start | bytes 393224 | tf_op jit(solution)/shard_map/ppermute | solution.py:373
  13.3 7.2 %collective-permute-start.5 = (bf16[2,256,128]{2,1,0:T(8,128)(2,1)}, bf16[2,256,128]{2,1,0:T(8,128)(2,1)S(1)}, u32[]{:S(2)}, u32[]{:S(2)}) collective-permute-start(bf16[2,256,128]{2,1,0:T(8,128)(2,1)} %get-tuple-element.24), channel_id=1, source_target_pairs={{0,16},{1,49},{2,18},{3,51},{4,20},{5,53},{6,22},{7,55},{8,24},{9,... | collective-permute-start | bytes 393224 | tf_op jit(solution)/shard_map/ppermute | solution.py:373
  14.1 6.4 %collective-permute-start.6 = (bf16[2,256,128]{2,1,0:T(8,128)(2,1)}, bf16[2,256,128]{2,1,0:T(8,128)(2,1)S(1)}, u32[]{:S(2)}, u32[]{:S(2)}) collective-permute-start(bf16[2,256,128]{2,1,0:T(8,128)(2,1)} %get-tuple-element.25), channel_id=1, source_target_pairs={{0,48},{1,17},{2,50},{3,19},{4,52},{5,21},{6,54},{7,23},{8,56},{9,... | collective-permute-start | bytes 393224 | tf_op jit(solution)/shard_map/ppermute | solution.py:373
  14.3 17.7 %copy-start.1 = (f32[1,524288]{1,0:T(1,128)S(1)}, f32[1,524288]{1,0:T(1,128)}, u32[]{:S(2)}) copy-start(f32[1,524288]{1,0:T(1,128)} %variance.1) | copy-start | bytes 6291460
  14.6 11.4 %collective-permute-start.3 = (bf16[2,256,128]{2,1,0:T(8,128)(2,1)S(1)}, bf16[2,256,128]{2,1,0:T(8,128)(2,1)S(1)}, u32[]{:S(2)}, u32[]{:S(2)}) collective-permute-start(bf16[2,256,128]{2,1,0:T(8,128)(2,1)S(1)} %shard_map.96.ours), channel_id=1, source_target_pairs={{0,192},{1,65},{2,194},{3,67},{4,196},{5,69},{6,198},{7,71},{8,200... | collective-permute-start | bytes 393224 | tf_op jit(solution)/shard_map/ppermute | solution.py:382
  20.5 16.4 %copy-start.2 = (f32[1,524288]{1,0:T(1,128)S(1)}, f32[1,524288]{1,0:T(1,128)}, u32[]{:S(2)}) copy-start(f32[1,524288]{1,0:T(1,128)} %momentum.1) | copy-start | bytes 6291460
  20.5 16.4 %copy-start.6 = (s32[4]{0:T(128)S(1)}, s32[4]{0:T(128)}, u32[]{:S(2)}) copy-start(s32[4]{0:T(128)} %offsets.3) | copy-start | bytes 52
  20.7 9.4 %collective-permute-start.7 = (bf16[2,256,128]{2,1,0:T(8,128)(2,1)S(1)}, bf16[2,256,128]{2,1,0:T(8,128)(2,1)S(1)}, u32[]{:S(2)}, u32[]{:S(2)}) collective-permute-start(bf16[2,256,128]{2,1,0:T(8,128)(2,1)S(1)} %shard_map.100.ours), channel_id=1, source_target_pairs={{0,64},{1,193},{2,66},{3,195},{4,68},{5,197},{6,70},{7,199},{8,72}... | collective-permute-start | bytes 393224 | tf_op jit(solution)/shard_map/ppermute | solution.py:382
  26.0 7.3 %collective-permute-start.8 = (bf16[2,256,128]{2,1,0:T(8,128)(2,1)S(1)}, bf16[2,256,128]{2,1,0:T(8,128)(2,1)S(1)}, u32[]{:S(2)}, u32[]{:S(2)}) collective-permute-start(bf16[2,256,128]{2,1,0:T(8,128)(2,1)S(1)} %shard_map.97.low), channel_id=1, source_target_pairs={{0,64},{1,193},{2,66},{3,195},{4,68},{5,197},{6,70},{7,199},{8,72}... | collective-permute-start | bytes 393224 | tf_op jit(solution)/shard_map/ppermute | solution.py:382
  30.1 6.8 %collective-permute-start.9 = (bf16[2,256,128]{2,1,0:T(8,128)(2,1)S(1)}, bf16[2,256,128]{2,1,0:T(8,128)(2,1)S(1)}, u32[]{:S(2)}, u32[]{:S(2)}) collective-permute-start(bf16[2,256,128]{2,1,0:T(8,128)(2,1)S(1)} %shard_map.101.high), channel_id=1, source_target_pairs={{0,192},{1,65},{2,194},{3,67},{4,196},{5,69},{6,198},{7,71},{8,200... | collective-permute-start | bytes 393224 | tf_op jit(solution)/shard_map/ppermute | solution.py:382
  38.0 4.9 %collective-permute-start.13 = (f32[512,128]{1,0:T(8,128)S(1)}, f32[512,128]{1,0:T(8,128)S(1)}, u32[]{:S(2)}, u32[]{:S(2)}) collective-permute-start(f32[512,128]{1,0:T(8,128)S(1)} %get-tuple-element.32.ours), channel_id=1, source_target_pairs={{0,1},{1,0},{2,3},{3,2},{4,5},{5,4},{6,7},{7,6},{8,9},{9,8},{10,11... | collective-permute-start | bytes 786440 | tf_op jit(solution)/shard_map/ppermute | solution.py:364
  39.4 10.9 %collective-permute-start.12 = (bf16[4,256,128]{2,1,0:T(8,128)(2,1)S(1)}, bf16[4,256,128]{2,1,0:T(8,128)(2,1)}, u32[]{:S(2)}, u32[]{:S(2)}) collective-permute-start(bf16[4,256,128]{2,1,0:T(8,128)(2,1)S(1)} %get-tuple-element.27.refs_0_), channel_id=1, source_target_pairs={{0,32},{1,33},{2,34},{3,35},{4,36},{5,37},{6,38},{7,39},{8,40},{9,... | collective-permute-start | bytes 786440 | tf_op jit(solution)/shard_map/ppermute | solution.py:373
  41.7 13.4 %collective-permute-start.11 = (bf16[4,256,128]{2,1,0:T(8,128)(2,1)S(1)}, bf16[4,256,128]{2,1,0:T(8,128)(2,1)}, u32[]{:S(2)}, u32[]{:S(2)}) collective-permute-start(bf16[4,256,128]{2,1,0:T(8,128)(2,1)S(1)} %get-tuple-element.27.refs_0_), channel_id=1, source_target_pairs={{0,48},{1,17},{2,50},{3,19},{4,52},{5,21},{6,54},{7,23},{8,56},{9,... | collective-permute-start | bytes 786440 | tf_op jit(solution)/shard_map/ppermute | solution.py:373
  42.9 12.2 %collective-permute-start.10 = (bf16[4,256,128]{2,1,0:T(8,128)(2,1)S(1)}, bf16[4,256,128]{2,1,0:T(8,128)(2,1)}, u32[]{:S(2)}, u32[]{:S(2)}) collective-permute-start(bf16[4,256,128]{2,1,0:T(8,128)(2,1)S(1)} %get-tuple-element.27.refs_0_), channel_id=1, source_target_pairs={{0,16},{1,49},{2,18},{3,51},{4,20},{5,53},{6,22},{7,55},{8,24},{9,... | collective-permute-start | bytes 786440 | tf_op jit(solution)/shard_map/ppermute | solution.py:373
  43.5 13.9 %all-to-all-start = ((f32[32,1,128]{2,1,0:T(1,128)}), f32[32,1,128]{2,1,0:T(1,128)S(1)}, u32[]{:S(2)}, u32[]{:S(2)}) async-start(f32[32,1,128]{2,1,0:T(1,128)} %shard_map.106), calls=%async_computation | async-start | bytes 32768 | tf_op jit(solution)/shard_map/all_to_all | solution.py:404

commit v6 on v5

--- a/solution.py
+++ b/solution.py
@@ -187,17 +187,17 @@
     return inside[0] | inside[1] | inside[2]
 
 
-def server_kernel(offsets, low, high, other_low, other_high, momentum, spread, column, out, sums):
+def server_kernel(half, offsets, ours, theirs, momentum, spread, *refs):
+    column, sums = refs[-2:] if half == 0 else (refs[2], refs[4])
     y = my_y()
     lane_row = lax.broadcasted_iota(jnp.int32, (8, QB), 0)
-    sums[...] = jnp.zeros((8, QB), F32)
-    for s in range(N_Z):
-        ours, theirs = (low, other_low) if s < HALF else (high, other_high)
-        total = ours[s % HALF].astype(F32) + theirs[s % HALF].astype(F32)
-        block = s * N_Y + y
+    sums[...] = jnp.zeros((8, QB), F32) if half == 0 else refs[0][...]
+    for s in range(HALF):
+        block = (half * HALF + s) * N_Y + y
+        total = ours[s].astype(F32) + theirs[s].astype(F32)
         sent = (total + BETA_ONE * share_of(momentum, block)).astype(BF16)
-        column[s] = sent
-        direction = sent.astype(F32) * spread[s]
+        column[half * HALF + s] = sent
+        direction = sent.astype(F32) * spread[half * HALF + s]
         squares = direction * direction
         first = block * ROWS
         mixed = has_boundary(offsets, first, ROWS)
@@ -217,23 +217,27 @@
                 if k < SEGS - 1:
                     picked = jnp.where(masks[k], 0.0, picked)
                 sums[k : k + 1, :] += jnp.sum(picked, axis=0, keepdims=True)
-    folded = sums[...]
-    folded = folded + pltpu.roll(folded, QB // 2, 1)
-    folded = folded + pltpu.roll(folded, QB // 4, 1)
-    lane = lax.broadcasted_iota(jnp.int32, (8, QB), 1) // (QB // SEGS)
-    mine = jnp.where(lane == lane_row, folded, 0.0)
-    out[...] = jnp.broadcast_to(jnp.sum(mine, axis=0, keepdims=True), out.shape)
-
-
-def server(offsets, halves, momentum, spread):
+
+    if half == 1:
+        out = refs[3]
+        folded = sums[...]
+        folded = folded + pltpu.roll(folded, QB // 2, 1)
+        folded = folded + pltpu.roll(folded, QB // 4, 1)
+        lane = lax.broadcasted_iota(jnp.int32, (8, QB), 1) // (QB // SEGS)
+        mine = jnp.where(lane == lane_row, folded, 0.0)
+        out[...] = jnp.broadcast_to(jnp.sum(mine, axis=0, keepdims=True), out.shape)
+
+
+def server(half, offsets, ours, theirs, momentum, spread, *before):
     return call(
-        server_kernel,
+        functools.partial(server_kernel, half),
         (offsets,),
-        (*halves, momentum, spread),
-        on_chip(6),
+        (ours, theirs, momentum, spread, *before),
+        on_chip(4 + len(before)),
         on_chip(2),
-        (like((N_Z, ROWS, QB), BF16), like((512, QB), F32)),
-        scratch=[pltpu.VMEM((8, QB), F32)],
+        (like((N_Z, ROWS, QB), BF16), like((512 if half else 8, QB), F32)),
+        scratch=[pltpu.VMEM((8, QB), F32)] * half,
+        aliases={6: 0} if half else None,
     )
 
 
@@ -397,8 +401,9 @@
     high = reduce_y(1, high, server_err, dense)
     low = add(low, exchange_z(low, 3, 1))
     high = add(high, exchange_z(high, 1, 3))
-    halves = (low, high, exchange_z(low, 1, 3), exchange_z(high, 3, 1))
-    column, squares = server(offsets, halves, momentum, column_spread)
+    column, sums = server(0, offsets, low, exchange_z(low, 1, 3), momentum, column_spread)
+    theirs = exchange_z(high, 3, 1)
+    column, squares = server(1, offsets, high, theirs, momentum, column_spread, sums, column)
     received = {k: exchange_y(column, k) for k in GATHER}
     squares = pair(squares, exchange(squares, "core", 1))
     totals = lax.all_to_all(squares, ("y", "chip"), split_axis=0, concat_axis=0, tiled=True)

time: 60 us -> 59.8 us (level)
  waiting for transfers between devices: 13.8 us -> 13 us
  Pallas kernels: 14.7 us -> 15.3 us
    ppermute x4, waiting for transfers between devices: 7.62 us -> 6.81 us  [exchange_z(): return lax.ppermute(value, ('z', 'chip', 'core'), pairs)]
    pallas_call x13 -> x14, Pallas kernels: 14.7 us -> 15.3 us  [call(): pl.pallas_call(kernel, in_specs=[pl.BlockSpec(memory_space=pltpu.SMEM)] *...]
  transfers between devices with their start and end apart: 15 -> 15, of which waited for: 6 -> 6; matrix products, arithmetic and copies ran while one was open for 0% -> 0% of each run, Pallas kernels for 15% -> 17%
where the time goes in v6:
time: 59.8 us; the launch traced here: 59.3 us
  starting transfers between devices  29.3 us (49%)
  Pallas kernels  15.3 us (26%)
  waiting for transfers between devices  13 us (22%)
  between operations  1.62 us (3%)
    pallas_call x14, Pallas kernels, call(): pl.pallas_call(kernel, in_specs=[pl.BlockSpec(memory_space=pltpu.SMEM)] *...  15.3 us
    ppermute x9, starting transfers between devices, exchange_y(): return lax.ppermute(value, ('y', 'chip', 'core'), pairs)  11.7 us
    ppermute x4, starting transfers between devices, exchange_z(): return lax.ppermute(value, ('z', 'chip', 'core'), pairs)  9.25 us
    all_to_all x1, starting transfers between devices, body(): lax.all_to_all(squares, ('y', 'chip'), split_axis=0, concat_axis=0, tiled...  6.88 us
    ppermute x4, waiting for transfers between devices, exchange_z(): return lax.ppermute(value, ('z', 'chip', 'core'), pairs)  6.81 us
    ppermute x9, waiting for transfers between devices, exchange_y(): return lax.ppermute(value, ('y', 'chip', 'core'), pairs)  5.94 us
    ppermute x1, starting transfers between devices, exchange(): lax.ppermute(value, axis, [(i, i ^ mask) for i in range(lax.axis_size(axi...  1.39 us
  transfers between devices with their start and end apart: 15, of which 6 were waited for; matrix products, arithmetic and copies ran while one was open for 0% of the time, Pallas kernels for 17%

profile of v6, /device:TPU:1, one launch (start us, length us, event | category | flops | bytes accessed | tf_op | source)
XLA Modules:
  0.0 59.3 jit_solution(17523493820719156840)
XLA Ops:
  0.6 2.4 %shard_map.100 = (bf16[2,256,128]{2,1,0:T(8,128)(2,1)}, bf16[2,256,128]{2,1,0:T(8,128)(2,1)}, bf16[2,256,128]{2,1,0:T(8,128)(2,1)}, bf16[2,256,128]{2,1,0:T(8,128)(2,1)}) custom-call(bf16[1,1,524288]{2,1,0:T(2,128)(2,1)} %grad.3, bf16[1,1,524288]{2,1,0:T(2,128)(2,1)} %err.3), custom_call_target="tpu_custom_call" | custom-call | tf_op jit(solution)/shard_map/pallas_call | solution.py:56
  3.1 3.8 %collective-permute-start.5 = (bf16[2,256,128]{2,1,0:T(8,128)(2,1)}, bf16[2,256,128]{2,1,0:T(8,128)(2,1)S(1)}, u32[]{:S(2)}, u32[]{:S(2)}) collective-permute-start(bf16[2,256,128]{2,1,0:T(8,128)(2,1)} %get-tuple-element.26), channel_id=1, source_target_pairs={{0,32},{1,33},{2,34},{3,35},{4,36},{5,37},{6,38},{7,39},{8,40},{9,... | collective-permute-start | bytes 393224 | tf_op jit(solution)/shard_map/ppermute | solution.py:377
  6.9 0.8 %collective-permute-start.6 = (bf16[2,256,128]{2,1,0:T(8,128)(2,1)}, bf16[2,256,128]{2,1,0:T(8,128)(2,1)S(1)}, u32[]{:S(2)}, u32[]{:S(2)}) collective-permute-start(bf16[2,256,128]{2,1,0:T(8,128)(2,1)} %get-tuple-element.27), channel_id=1, source_target_pairs={{0,16},{1,49},{2,18},{3,51},{4,20},{5,53},{6,22},{7,55},{8,24},{9,... | collective-permute-start | bytes 393224 | tf_op jit(solution)/shard_map/ppermute | solution.py:377
  7.7 2.6 %shard_map.95 = (bf16[2,256,128]{2,1,0:T(8,128)(2,1)}, bf16[2,256,128]{2,1,0:T(8,128)(2,1)}, bf16[2,256,128]{2,1,0:T(8,128)(2,1)}, bf16[2,256,128]{2,1,0:T(8,128)(2,1)}) custom-call(bf16[1,1,524288]{2,1,0:T(2,128)(2,1)} %grad.3, bf16[1,1,524288]{2,1,0:T(2,128)(2,1)} %err.3), custom_call_target="tpu_custom_call" | custom-call | tf_op jit(solution)/shard_map/pallas_call | solution.py:56
  10.3 3.0 %collective-permute-start = (bf16[2,256,128]{2,1,0:T(8,128)(2,1)}, bf16[2,256,128]{2,1,0:T(8,128)(2,1)S(1)}, u32[]{:S(2)}, u32[]{:S(2)}) collective-permute-start(bf16[2,256,128]{2,1,0:T(8,128)(2,1)} %get-tuple-element.21), channel_id=1, source_target_pairs={{0,32},{1,33},{2,34},{3,35},{4,36},{5,37},{6,38},{7,39},{8,40},{9,... | collective-permute-start | bytes 393224 | tf_op jit(solution)/shard_map/ppermute | solution.py:377
  13.3 0.8 %collective-permute-start.1 = (bf16[2,256,128]{2,1,0:T(8,128)(2,1)}, bf16[2,256,128]{2,1,0:T(8,128)(2,1)S(1)}, u32[]{:S(2)}, u32[]{:S(2)}) collective-permute-start(bf16[2,256,128]{2,1,0:T(8,128)(2,1)} %get-tuple-element.22), channel_id=1, source_target_pairs={{0,16},{1,49},{2,18},{3,51},{4,20},{5,53},{6,22},{7,55},{8,24},{9,... | collective-permute-start | bytes 393224 | tf_op jit(solution)/shard_map/ppermute | solution.py:377
  14.6 2.9 %collective-permute-start.8 = (bf16[2,256,128]{2,1,0:T(8,128)(2,1)S(1)}, bf16[2,256,128]{2,1,0:T(8,128)(2,1)S(1)}, u32[]{:S(2)}, u32[]{:S(2)}) collective-permute-start(bf16[2,256,128]{2,1,0:T(8,128)(2,1)S(1)} %shard_map.101.ours), channel_id=1, source_target_pairs={{0,192},{1,65},{2,194},{3,67},{4,196},{5,69},{6,198},{7,71},{8,200... | collective-permute-start | bytes 393224 | tf_op jit(solution)/shard_map/ppermute | solution.py:386
  17.5 3.0 %collective-permute-done.1.refs_2_ = bf16[2,256,128]{2,1,0:T(8,128)(2,1)S(1)} collective-permute-done((bf16[2,256,128]{2,1,0:T(8,128)(2,1)}, bf16[2,256,128]{2,1,0:T(8,128)(2,1)S(1)}, u32[]{:S(2)}, u32[]{:S(2)}) %collective-permute-start.1) | collective-permute-done | bytes 131104 | tf_op jit(solution)/shard_map/ppermute | solution.py:377
  20.7 5.3 %collective-permute-start.3 = (bf16[2,256,128]{2,1,0:T(8,128)(2,1)S(1)}, bf16[2,256,128]{2,1,0:T(8,128)(2,1)S(1)}, u32[]{:S(2)}, u32[]{:S(2)}) collective-permute-start(bf16[2,256,128]{2,1,0:T(8,128)(2,1)S(1)} %shard_map.97.ours), channel_id=1, source_target_pairs={{0,64},{1,193},{2,66},{3,195},{4,68},{5,197},{6,70},{7,199},{8,72}... | collective-permute-start | bytes 393224 | tf_op jit(solution)/shard_map/ppermute | solution.py:386
  26.1 4.0 %collective-permute-done.3.theirs = bf16[2,256,128]{2,1,0:T(8,128)(2,1)S(1)} collective-permute-done((bf16[2,256,128]{2,1,0:T(8,128)(2,1)S(1)}, bf16[2,256,128]{2,1,0:T(8,128)(2,1)S(1)}, u32[]{:S(2)}, u32[]{:S(2)}) %collective-permute-start.3) | collective-permute-done | bytes 131104 | tf_op jit(solution)/shard_map/ppermute | solution.py:386
  30.1 0.9 %collective-permute-start.4 = (bf16[2,256,128]{2,1,0:T(8,128)(2,1)S(1)}, bf16[2,256,128]{2,1,0:T(8,128)(2,1)S(1)}, u32[]{:S(2)}, u32[]{:S(2)}) collective-permute-start(bf16[2,256,128]{2,1,0:T(8,128)(2,1)S(1)} %shard_map.98.ours), channel_id=1, source_target_pairs={{0,192},{1,65},{2,194},{3,67},{4,196},{5,69},{6,198},{7,71},{8,200... | collective-permute-start | bytes 393224 | tf_op jit(solution)/shard_map/ppermute | solution.py:386
  31.9 1.4 %shard_map.99 = (f32[4096,128]{1,0:T(8,128)S(1)}, f32[4,256,128]{2,1,0:T(8,128)S(1)}) custom-call(f32[2]{0:T(128)S(1)} %pad_maximum_fusion.bias, f32[1,524288]{1,0:T(1,128)S(1)} %copy-done.2), custom_call_target="tpu_custom_call" | custom-call | tf_op jit(solution)/shard_map/pallas_call | solution.py:56
  33.4 0.8 %shard_map.103 = (bf16[4,256,128]{2,1,0:T(8,128)(2,1)S(1)}, f32[8,128]{1,0:T(8,128)S(1)}) custom-call(s32[4]{0:T(128)S(1)} %copy-done.6, bf16[2,256,128]{2,1,0:T(8,128)(2,1)S(1)} %shard_map.102.ours, bf16[2,256,128]{2,1,0:T(8,128)(2,1)S(1)} %collective-permute-done.9.theirs, f32[1,524288]{1,0:T(1,128)S(1)} %copy-done, ...), custom_call_target="tpu_custom_call" | custom-call | tf_op jit(solution)/shard_map/pallas_call | solution.py:56
  34.1 2.8 %collective-permute-done.4.theirs = bf16[2,256,128]{2,1,0:T(8,128)(2,1)S(1)} collective-permute-done((bf16[2,256,128]{2,1,0:T(8,128)(2,1)S(1)}, bf16[2,256,128]{2,1,0:T(8,128)(2,1)S(1)}, u32[]{:S(2)}, u32[]{:S(2)}) %collective-permute-start.4) | collective-permute-done | bytes 131104 | tf_op jit(solution)/shard_map/ppermute | solution.py:386
  37.0 0.9 %shard_map.104 = (bf16[4,256,128]{2,1,0:T(8,128)(2,1)S(1)}, f32[512,128]{1,0:T(8,128)S(1)}) custom-call(s32[4]{0:T(128)S(1)} %copy-done.6, bf16[2,256,128]{2,1,0:T(8,128)(2,1)S(1)} %shard_map.98.ours, bf16[2,256,128]{2,1,0:T(8,128)(2,1)S(1)} %collective-permute-done.4.theirs, f32[1,524288]{1,0:T(1,128)S(1)} %copy-done, ...), custom_call_target="tpu_custom_call", output_to_operand_aliasing={{0}: (6, {})} | custom-call | tf_op jit(solution)/shard_map/pallas_call | solution.py:56
  37.9 1.4 %collective-permute-start.13 = (f32[512,128]{1,0:T(8,128)S(1)}, f32[512,128]{1,0:T(8,128)S(1)}, u32[]{:S(2)}, u32[]{:S(2)}) collective-permute-start(f32[512,128]{1,0:T(8,128)S(1)} %get-tuple-element.36.ours), channel_id=1, source_target_pairs={{0,1},{1,0},{2,3},{3,2},{4,5},{5,4},{6,7},{7,6},{8,9},{9,8},{10,11... | collective-permute-start | bytes 786440 | tf_op jit(solution)/shard_map/ppermute | solution.py:368
  39.3 2.3 %collective-permute-start.12 = (bf16[4,256,128]{2,1,0:T(8,128)(2,1)S(1)}, bf16[4,256,128]{2,1,0:T(8,128)(2,1)}, u32[]{:S(2)}, u32[]{:S(2)}) collective-permute-start(bf16[4,256,128]{2,1,0:T(8,128)(2,1)S(1)} %get-tuple-element.31.refs_0_), channel_id=1, source_target_pairs={{0,32},{1,33},{2,34},{3,35},{4,36},{5,37},{6,38},{7,39},{8,40},{9,... | collective-permute-start | bytes 786440 | tf_op jit(solution)/shard_map/ppermute | solution.py:377
  41.6 1.0 %collective-permute-start.11 = (bf16[4,256,128]{2,1,0:T(8,128)(2,1)S(1)}, bf16[4,256,128]{2,1,0:T(8,128)(2,1)}, u32[]{:S(2)}, u32[]{:S(2)}) collective-permute-start(bf16[4,256,128]{2,1,0:T(8,128)(2,1)S(1)} %get-tuple-element.31.refs_0_), channel_id=1, source_target_pairs={{0,48},{1,17},{2,50},{3,19},{4,52},{5,21},{6,54},{7,23},{8,56},{9,... | collective-permute-start | bytes 786440 | tf_op jit(solution)/shard_map/ppermute | solution.py:377
  42.6 0.6 %shard_map.107 = f32[32,1,128]{2,1,0:T(1,128)} custom-call(f32[512,128]{1,0:T(8,128)S(1)} %get-tuple-element.36.ours, f32[512,128]{1,0:T(8,128)S(1)} %collective-permute-done.13.theirs), custom_call_target="tpu_custom_call" | custom-call | tf_op jit(solution)/shard_map/pallas_call | solution.py:56
  43.2 6.9 %all-to-all-start = ((f32[32,1,128]{2,1,0:T(1,128)}), f32[32,1,128]{2,1,0:T(1,128)S(1)}, u32[]{:S(2)}, u32[]{:S(2)}) async-start(f32[32,1,128]{2,1,0:T(1,128)} %shard_map.107), calls=%async_computation | async-start | bytes 32768 | tf_op jit(solution)/shard_map/all_to_all | solution.py:409
  50.1 2.0 %shard_map.105 = (f32[4096,128]{1,0:T(8,128)}, f32[4096,128]{1,0:T(8,128)S(1)}) custom-call(bf16[4,256,128]{2,1,0:T(8,128)(2,1)S(1)} %get-tuple-element.31.refs_0_, bf16[4,256,128]{2,1,0:T(8,128)(2,1)} %collective-permute-done.12.refs_1_, f32[4096,128]{1,0:T(8,128)S(1)} %get-tuple-element.32.refs_2_), custom_call_target="tpu_custom_call", output_to_operand_aliasing={{1}: (2, {})} | custom-call | tf_op jit(solution)/shard_map/pallas_call | solution.py:56
  52.1 2.7 %collective-permute-done.11.refs_1_ = bf16[4,256,128]{2,1,0:T(8,128)(2,1)} collective-permute-done((bf16[4,256,128]{2,1,0:T(8,128)(2,1)S(1)}, bf16[4,256,128]{2,1,0:T(8,128)(2,1)}, u32[]{:S(2)}, u32[]{:S(2)}) %collective-permute-start.11) | collective-permute-done | bytes 262176 | tf_op jit(solution)/shard_map/ppermute | solution.py:377
  54.8 2.1 %shard_map.106 = (f32[4096,128]{1,0:T(8,128)}, f32[4096,128]{1,0:T(8,128)S(1)}) custom-call(bf16[4,256,128]{2,1,0:T(8,128)(2,1)} %collective-permute-done.10.refs_0_, bf16[4,256,128]{2,1,0:T(8,128)(2,1)} %collective-permute-done.11.refs_1_, f32[4096,128]{1,0:T(8,128)S(1)} %get-tuple-element.33.refs_2_, ...), custom_call_target="tpu_custom_call", output_to_operand_aliasing={{1}: (2, {}), {0}: (3, {})} | custom-call | tf_op jit(solution)/shard_map/pallas_call | solution.py:56
  57.2 2.2 %shard_map.108 = f32[4096,128]{1,0:T(8,128)} custom-call(s32[4]{0:T(128)S(1)} %copy-done.6, f32[32,1,128]{2,1,0:T(1,128)S(1)} %all-to-all-done.totals, f32[4096,128]{1,0:T(8,128)S(1)} %get-tuple-element.37.direction, bf16[4096,128]{1,0:T(8,128)(2,1)S(1)} %shard_map.96.refs_5_.dense), custom_call_target="tpu_custom_call" | custom-call | tf_op jit(solution)/shard_map/pallas_call | solution.py:56
  (35 shorter events, 1.2 us)
Async XLA Ops:
  3.1 11.0 %collective-permute-start.5 = (bf16[2,256,128]{2,1,0:T(8,128)(2,1)}, bf16[2,256,128]{2,1,0:T(8,128)(2,1)S(1)}, u32[]{:S(2)}, u32[]{:S(2)}) collective-permute-start(bf16[2,256,128]{2,1,0:T(8,128)(2,1)} %get-tuple-element.26), channel_id=1, source_target_pairs={{0,32},{1,33},{2,34},{3,35},{4,36},{5,37},{6,38},{7,39},{8,40},{9,... | collective-permute-start | bytes 393224 | tf_op jit(solution)/shard_map/ppermute | solution.py:377
  6.9 7.6 %collective-permute-start.6 = (bf16[2,256,128]{2,1,0:T(8,128)(2,1)}, bf16[2,256,128]{2,1,0:T(8,128)(2,1)S(1)}, u32[]{:S(2)}, u32[]{:S(2)}) collective-permute-start(bf16[2,256,128]{2,1,0:T(8,128)(2,1)} %get-tuple-element.27), channel_id=1, source_target_pairs={{0,16},{1,49},{2,18},{3,51},{4,20},{5,53},{6,22},{7,55},{8,24},{9,... | collective-permute-start | bytes 393224 | tf_op jit(solution)/shard_map/ppermute | solution.py:377
  7.7 6.4 %copy-start.1 = (bf16[1,524288]{1,0:T(2,128)(2,1)S(1)}, bf16[1,524288]{1,0:T(2,128)(2,1)}, u32[]{:S(2)}) copy-start(bf16[1,524288]{1,0:T(2,128)(2,1)} %weights.1) | copy-start | bytes 3145732
  7.7 6.8 %collective-permute-start.7 = (bf16[2,256,128]{2,1,0:T(8,128)(2,1)}, bf16[2,256,128]{2,1,0:T(8,128)(2,1)S(1)}, u32[]{:S(2)}, u32[]{:S(2)}) collective-permute-start(bf16[2,256,128]{2,1,0:T(8,128)(2,1)} %get-tuple-element.28), channel_id=1, source_target_pairs={{0,48},{1,17},{2,50},{3,19},{4,52},{5,21},{6,54},{7,23},{8,56},{9,... | collective-permute-start | bytes 393224 | tf_op jit(solution)/shard_map/ppermute | solution.py:377
  10.3 4.2 %copy-start.3 = (f32[1,32768]{1,0:T(1,128)S(1)}, f32[1,32768]{1,0:T(1,128)}, u32[]{:S(2)}) copy-start(f32[1,32768]{1,0:T(1,128)} %refs_4_.3) | copy-start | bytes 393220
  10.3 4.2 %copy-start.5 = (bf16[2,256,128]{2,1,0:T(8,128)(2,1)S(1)}, bf16[2,256,128]{2,1,0:T(8,128)(2,1)}, u32[]{:S(2)}) copy-start(bf16[2,256,128]{2,1,0:T(8,128)(2,1)} %get-tuple-element.25.refs_0_) | copy-start | bytes 393220
  10.3 10.2 %copy-start.4 = (bf16[2,256,128]{2,1,0:T(8,128)(2,1)S(1)}, bf16[2,256,128]{2,1,0:T(8,128)(2,1)}, u32[]{:S(2)}) copy-start(bf16[2,256,128]{2,1,0:T(8,128)(2,1)} %get-tuple-element.20.refs_0_) | copy-start | bytes 393220
  10.3 7.2 %collective-permute-start = (bf16[2,256,128]{2,1,0:T(8,128)(2,1)}, bf16[2,256,128]{2,1,0:T(8,128)(2,1)S(1)}, u32[]{:S(2)}, u32[]{:S(2)}) collective-permute-start(bf16[2,256,128]{2,1,0:T(8,128)(2,1)} %get-tuple-element.21), channel_id=1, source_target_pairs={{0,32},{1,33},{2,34},{3,35},{4,36},{5,37},{6,38},{7,39},{8,40},{9,... | collective-permute-start | bytes 393224 | tf_op jit(solution)/shard_map/ppermute | solution.py:377
  13.3 7.2 %collective-permute-start.1 = (bf16[2,256,128]{2,1,0:T(8,128)(2,1)}, bf16[2,256,128]{2,1,0:T(8,128)(2,1)S(1)}, u32[]{:S(2)}, u32[]{:S(2)}) collective-permute-start(bf16[2,256,128]{2,1,0:T(8,128)(2,1)} %get-tuple-element.22), channel_id=1, source_target_pairs={{0,16},{1,49},{2,18},{3,51},{4,20},{5,53},{6,22},{7,55},{8,24},{9,... | collective-permute-start | bytes 393224 | tf_op jit(solution)/shard_map/ppermute | solution.py:377
  14.1 6.4 %collective-permute-start.2 = (bf16[2,256,128]{2,1,0:T(8,128)(2,1)}, bf16[2,256,128]{2,1,0:T(8,128)(2,1)S(1)}, u32[]{:S(2)}, u32[]{:S(2)}) collective-permute-start(bf16[2,256,128]{2,1,0:T(8,128)(2,1)} %get-tuple-element.23), channel_id=1, source_target_pairs={{0,48},{1,17},{2,50},{3,19},{4,52},{5,21},{6,54},{7,23},{8,56},{9,... | collective-permute-start | bytes 393224 | tf_op jit(solution)/shard_map/ppermute | solution.py:377
  14.3 17.7 %copy-start.2 = (f32[1,524288]{1,0:T(1,128)S(1)}, f32[1,524288]{1,0:T(1,128)}, u32[]{:S(2)}) copy-start(f32[1,524288]{1,0:T(1,128)} %variance.1) | copy-start | bytes 6291460
  14.6 11.4 %collective-permute-start.8 = (bf16[2,256,128]{2,1,0:T(8,128)(2,1)S(1)}, bf16[2,256,128]{2,1,0:T(8,128)(2,1)S(1)}, u32[]{:S(2)}, u32[]{:S(2)}) collective-permute-start(bf16[2,256,128]{2,1,0:T(8,128)(2,1)S(1)} %shard_map.101.ours), channel_id=1, source_target_pairs={{0,192},{1,65},{2,194},{3,67},{4,196},{5,69},{6,198},{7,71},{8,200... | collective-permute-start | bytes 393224 | tf_op jit(solution)/shard_map/ppermute | solution.py:386
  20.5 12.8 %copy-start = (f32[1,524288]{1,0:T(1,128)S(1)}, f32[1,524288]{1,0:T(1,128)}, u32[]{:S(2)}) copy-start(f32[1,524288]{1,0:T(1,128)} %momentum.3) | copy-start | bytes 6291460
  20.5 12.8 %copy-start.6 = (s32[4]{0:T(128)S(1)}, s32[4]{0:T(128)}, u32[]{:S(2)}) copy-start(s32[4]{0:T(128)} %offsets.5) | copy-start | bytes 52
  20.7 9.4 %collective-permute-start.3 = (bf16[2,256,128]{2,1,0:T(8,128)(2,1)S(1)}, bf16[2,256,128]{2,1,0:T(8,128)(2,1)S(1)}, u32[]{:S(2)}, u32[]{:S(2)}) collective-permute-start(bf16[2,256,128]{2,1,0:T(8,128)(2,1)S(1)} %shard_map.97.ours), channel_id=1, source_target_pairs={{0,64},{1,193},{2,66},{3,195},{4,68},{5,197},{6,70},{7,199},{8,72}... | collective-permute-start | bytes 393224 | tf_op jit(solution)/shard_map/ppermute | solution.py:386
  26.0 7.3 %collective-permute-start.9 = (bf16[2,256,128]{2,1,0:T(8,128)(2,1)S(1)}, bf16[2,256,128]{2,1,0:T(8,128)(2,1)S(1)}, u32[]{:S(2)}, u32[]{:S(2)}) collective-permute-start(bf16[2,256,128]{2,1,0:T(8,128)(2,1)S(1)} %shard_map.102.ours), channel_id=1, source_target_pairs={{0,64},{1,193},{2,66},{3,195},{4,68},{5,197},{6,70},{7,199},{8,72}... | collective-permute-start | bytes 393224 | tf_op jit(solution)/shard_map/ppermute | solution.py:386
  30.1 6.8 %collective-permute-start.4 = (bf16[2,256,128]{2,1,0:T(8,128)(2,1)S(1)}, bf16[2,256,128]{2,1,0:T(8,128)(2,1)S(1)}, u32[]{:S(2)}, u32[]{:S(2)}) collective-permute-start(bf16[2,256,128]{2,1,0:T(8,128)(2,1)S(1)} %shard_map.98.ours), channel_id=1, source_target_pairs={{0,192},{1,65},{2,194},{3,67},{4,196},{5,69},{6,198},{7,71},{8,200... | collective-permute-start | bytes 393224 | tf_op jit(solution)/shard_map/ppermute | solution.py:386
  37.9 4.7 %collective-permute-start.13 = (f32[512,128]{1,0:T(8,128)S(1)}, f32[512,128]{1,0:T(8,128)S(1)}, u32[]{:S(2)}, u32[]{:S(2)}) collective-permute-start(f32[512,128]{1,0:T(8,128)S(1)} %get-tuple-element.36.ours), channel_id=1, source_target_pairs={{0,1},{1,0},{2,3},{3,2},{4,5},{5,4},{6,7},{7,6},{8,9},{9,8},{10,11... | collective-permute-start | bytes 786440 | tf_op jit(solution)/shard_map/ppermute | solution.py:368
  39.3 10.8 %collective-permute-start.12 = (bf16[4,256,128]{2,1,0:T(8,128)(2,1)S(1)}, bf16[4,256,128]{2,1,0:T(8,128)(2,1)}, u32[]{:S(2)}, u32[]{:S(2)}) collective-permute-start(bf16[4,256,128]{2,1,0:T(8,128)(2,1)S(1)} %get-tuple-element.31.refs_0_), channel_id=1, source_target_pairs={{0,32},{1,33},{2,34},{3,35},{4,36},{5,37},{6,38},{7,39},{8,40},{9,... | collective-permute-start | bytes 786440 | tf_op jit(solution)/shard_map/ppermute | solution.py:377
  41.6 13.2 %collective-permute-start.11 = (bf16[4,256,128]{2,1,0:T(8,128)(2,1)S(1)}, bf16[4,256,128]{2,1,0:T(8,128)(2,1)}, u32[]{:S(2)}, u32[]{:S(2)}) collective-permute-start(bf16[4,256,128]{2,1,0:T(8,128)(2,1)S(1)} %get-tuple-element.31.refs_0_), channel_id=1, source_target_pairs={{0,48},{1,17},{2,50},{3,19},{4,52},{5,21},{6,54},{7,23},{8,56},{9,... | collective-permute-start | bytes 786440 | tf_op jit(solution)/shard_map/ppermute | solution.py:377
  42.6 12.2 %collective-permute-start.10 = (bf16[4,256,128]{2,1,0:T(8,128)(2,1)S(1)}, bf16[4,256,128]{2,1,0:T(8,128)(2,1)}, u32[]{:S(2)}, u32[]{:S(2)}) collective-permute-start(bf16[4,256,128]{2,1,0:T(8,128)(2,1)S(1)} %get-tuple-element.31.refs_0_), channel_id=1, source_target_pairs={{0,16},{1,49},{2,18},{3,51},{4,20},{5,53},{6,22},{7,55},{8,24},{9,... | collective-permute-start | bytes 786440 | tf_op jit(solution)/shard_map/ppermute | solution.py:377
  43.2 13.9 %all-to-all-start = ((f32[32,1,128]{2,1,0:T(1,128)}), f32[32,1,128]{2,1,0:T(1,128)S(1)}, u32[]{:S(2)}, u32[]{:S(2)}) async-start(f32[32,1,128]{2,1,0:T(1,128)} %shard_map.107), calls=%async_computation | async-start | bytes 32768 | tf_op jit(solution)/shard_map/all_to_all | solution.py:409
